TPU v7x, 32 devices: a whole 2x2x4 slice. The times are simulated.
32 devices in a mesh: dp: 8 (over y, x, core), mp: 4 (over z).
Axes of the slice: x: 2, y: 2, z: 4, core: 2. Of those that a mesh axis runs over, the one named last changes fastest.
Arguments:
- tokens: int32 [32, 512], P('dp'), may hold values from 0 to 15359
- text_box: int32 [32, 512, 4], P(('dp', 'mp')), may hold values from 0 to 1000, as said below
- segments: int32 [32, 512], P(('dp', 'mp')), may hold values from 0 to 3, never falling along the last dimension, each value on 1 to 256 neighbouring positions
- alive_text: int32 [32, 512], P(('dp', 'mp')), may hold values from 0 to 1, as said below
- features: bfloat16 [1568, 256], P(('dp', 'mp')), may hold values from -6 to 6
- mask_pos: int32 [2560], P(('dp', 'mp')), may hold values from 0 to 511
- mask_label: int32 [2560], P('dp'), may hold values from 0 to 15359
- mask_valid: int32 [2560], P('dp'), may hold values from 0 to 1
- projections: float32 [4, 768, 768], P(None, 'dp')
- projections_first: float32 [4, 768, 768], P(None, 'dp'), may hold values from -7.1525574e-07 to 7.1525574e-07
- projections_second: float32 [4, 768, 768], P(None, 'dp'), may hold values from 1.249904e-15 to 4.999616e-15
- box_tables: float32 [4, 1024, 128], P(None, 'dp'), may hold values from -0.3125 to 0.3125
- box_tables_first: float32 [4, 1024, 128], P(None, 'dp'), may hold values from -7.1525574e-07 to 7.1525574e-07
- box_tables_second: float32 [4, 1024, 128], P(None, 'dp'), may hold values from 1.249904e-15 to 4.999616e-15
- position_table: float32 [512, 768], P('dp'), may hold values from -0.3125 to 0.3125
- position_table_first: float32 [512, 768], P('dp'), may hold values from -7.1525574e-07 to 7.1525574e-07
- position_table_second: float32 [512, 768], P('dp'), may hold values from 1.249904e-15 to 4.999616e-15
- visual_proj: float32 [256, 768], P('dp'), may hold values from -0.375 to 0.375
- visual_proj_first: float32 [256, 768], P('dp'), may hold values from -7.1525574e-07 to 7.1525574e-07
- visual_proj_second: float32 [256, 768], P('dp'), may hold values from 1.249904e-15 to 4.999616e-15
- small_params: float32 [17, 768], P(None, 'dp')
- small_params_first: float32 [17, 768], P(None, 'dp'), may hold values from -3.8146973e-06 to 3.8146973e-06
- small_params_second: float32 [17, 768], P(None, 'dp'), may hold values from 3.12476e-14 to 1.249904e-13
- word_table: float32 [15360, 768], P(('mp', 'dp'))
- word_table_first: float32 [15360, 768], P(('mp', 'dp')), may hold values from -7.1525574e-07 to 7.1525574e-07
- word_table_second: float32 [15360, 768], P(('mp', 'dp')), may hold values from 1.249904e-15 to 4.999616e-15
- feedforward: float32 [2, 768, 3072], P(None, 'dp', 'mp'), may hold values from -0.21875 to 0.21875
- feedforward_first: float32 [2, 768, 3072], P(None, 'dp', 'mp'), may hold values from -7.1525574e-07 to 7.1525574e-07
- feedforward_second: float32 [2, 768, 3072], P(None, 'dp', 'mp'), may hold values from 1.249904e-15 to 4.999616e-15
Outputs:
- new_projections: float32 [4, 768, 768], P(None, 'dp')
- new_projections_first: float32 [4, 768, 768], P(None, 'dp')
- new_projections_second: float32 [4, 768, 768], P(None, 'dp')
- new_box_tables: float32 [4, 1024, 128], P(None, 'dp')
- new_box_tables_first: float32 [4, 1024, 128], P(None, 'dp')
- new_box_tables_second: float32 [4, 1024, 128], P(None, 'dp')
- new_position_table: float32 [512, 768], P('dp')
- new_position_table_first: float32 [512, 768], P('dp')
- new_position_table_second: float32 [512, 768], P('dp')
- new_visual_proj: float32 [256, 768], P('dp')
- new_visual_proj_first: float32 [256, 768], P('dp')
- new_visual_proj_second: float32 [256, 768], P('dp')
- new_small_params: float32 [17, 768], P(None, 'dp')
- new_small_params_first: float32 [17, 768], P(None, 'dp')
- new_small_params_second: float32 [17, 768], P(None, 'dp')
- new_word_table: float32 [15360, 768], P(('mp', 'dp'))
- new_word_table_first: float32 [15360, 768], P(('mp', 'dp'))
- new_word_table_second: float32 [15360, 768], P(('mp', 'dp'))
- new_feedforward: float32 [2, 768, 3072], P(None, 'dp', 'mp')
- new_feedforward_first: float32 [2, 768, 3072], P(None, 'dp', 'mp')
- new_feedforward_second: float32 [2, 768, 3072], P(None, 'dp', 'mp')
- loss_sum: float32 [], replicated
- loss_count: float32 [], replicated
- grad_norm: float32 [], replicated
Inputs may be any that keep to these rules, and one draw needn't show every extreme that they name: `text_box`: left < right and top < bottom in every box, each side at most 100 apart. `alive_text`: each row is 1 on a leading run of 256 or more positions and 0 after it.
All inputs are finite; a program needn't handle non-finite values.
Results may differ from a plain program's by a relative error of at most 0.02.
The roundings to bfloat16 on the way count: a program that leaves them out, or rounds other values in their place, can miss the bound.
Values may be sent and summed in bfloat16 or wider, within the bound.
A program may use at most 256 MiB of HBM per device.

v0:
```python
from functools import partial

import jax
import jax.numpy as jnp
from jax import lax
from jax.sharding import PartitionSpec as P

D = 768
H = 12
HD = 64
FF = 3072
NB = 64
GRID = 7
TEXT = 512
STEP = 10


MASKED = -1e30
CLIP = 0.005
BETA_ONE = 0.9
BETA_TWO = 0.999
EPSILON = 1e-08
DECAY = 0.01
RATES = (0.02, 0.03, 0.03, 0.04, 0.3, 0.05, 0.02)


def combined_all(part, axis, combine):
    gathered = jax.tree.map(lambda a: lax.all_gather(a, axis), part)

    def take(source):
        return jax.tree.map(lambda a: lax.dynamic_index_in_dim(a, source, 0, False), gathered)

    return lax.fori_loop(
        1, lax.axis_size(axis), lambda source, state: combine(state, take(source)), take(0)
    )


def layer_norm(value, gain, shift):
    average = jnp.mean(value, -1, keepdims=True)
    centred = value - average
    variance = jnp.mean(centred * centred, -1, keepdims=True)
    return centred * lax.rsqrt(variance + 1e-05) * gain + shift


def grid_boxes():
    cells = jnp.arange(GRID * GRID, dtype=jnp.int32)
    row_place = cells // GRID
    column_place = cells % GRID
    return jnp.stack(
        [
            column_place * 1000 // GRID,
            row_place * 1000 // GRID,
            (column_place + 1) * 1000 // GRID,
            (row_place + 1) * 1000 // GRID,
        ],
        -1,
    )


def spatial(boxes, tables):
    left_edge, top_edge = (boxes[..., 0], boxes[..., 1])
    right_edge, bottom_edge = (boxes[..., 2], boxes[..., 3])
    return jnp.concatenate(
        [
            tables[0][left_edge],
            tables[1][top_edge],
            tables[0][right_edge],
            tables[1][bottom_edge],
            tables[2][bottom_edge - top_edge],
            tables[3][right_edge - left_edge],
        ],
        -1,
    )


def layout(text_box, segments, alive_text):
    full_box = jnp.concatenate([text_box, grid_boxes()], 0)
    positions = jnp.concatenate(
        [jnp.arange(TEXT, dtype=jnp.int32), jnp.arange(GRID * GRID, dtype=jnp.int32)]
    )
    segment_all = jnp.concatenate([segments, jnp.full((GRID * GRID,), -1, jnp.int32)])
    alive = jnp.concatenate([alive_text, jnp.ones((GRID * GRID,), jnp.int32)])
    shared = (
        (segment_all[:, None] == segment_all[None, :])
        | (segment_all[:, None] < 0)
        | (segment_all[None, :] < 0)
    )
    allowed = shared & (alive[None, :] > 0)
    half = NB // 2

    def bucket(places, step):
        return jnp.clip((places[None, :] - places[:, None]) // step, -half, half - 1) + half

    buckets = jnp.stack(
        [bucket(positions, 8), bucket(full_box[:, 0], 16) + NB, bucket(full_box[:, 3], 16) + 2 * NB]
    )
    return (allowed, buckets)


def kind_onehot(buckets, kind):
    labels = jnp.arange(NB, dtype=jnp.int32) + kind * NB
    return (buckets[kind][None] == labels[:, None, None]).astype(jnp.bfloat16)


def scores_of(rel_low, queries, keys, text_box, segments, alive_text):
    allowed, buckets = layout(text_box, segments, alive_text)
    scaled = jnp.einsum("qhc,khc->hqk", queries, keys, preferred_element_type=jnp.float32) * 0.125
    bias_sum = jnp.zeros(scaled.shape, jnp.float32)
    for kind in range(3):
        bias_sum = bias_sum + jnp.einsum(
            "vti,vn->nti",
            kind_onehot(buckets, kind),
            rel_low[kind * NB : (kind + 1) * NB],
            preferred_element_type=jnp.float32,
        )
    scaled = scaled + bias_sum
    return (jnp.where(allowed[None], scaled, MASKED), buckets)


def gelu_back(pre_piece, grad_active):
    gelu_pullback = jax.vjp(partial(jax.nn.gelu, approximate=False), pre_piece)[1]
    return gelu_pullback(grad_active)[0].astype(jnp.bfloat16)


def adam_step(weight, grad, first, second, rate):
    first = BETA_ONE * first + (1.0 - BETA_ONE) * grad
    second = BETA_TWO * second + (1.0 - BETA_TWO) * grad * grad
    fixed_first = first / (1.0 - BETA_ONE**STEP)
    fixed_second = second / (1.0 - BETA_TWO**STEP)
    weight = weight - rate * (fixed_first / (jnp.sqrt(fixed_second) + EPSILON) + DECAY * weight)
    return (weight, first, second)


def on_device(
    tokens,
    text_box,
    segments,
    alive_text,
    features,
    mask_pos,
    mask_label,
    mask_valid,
    projections,
    projections_first,
    projections_second,
    box_tables,
    box_tables_first,
    box_tables_second,
    position_table,
    position_table_first,
    position_table_second,
    visual_proj,
    visual_proj_first,
    visual_proj_second,
    small_params,
    small_params_first,
    small_params_second,
    word_table,
    word_table_first,
    word_table_second,
    feedforward,
    feedforward_first,
    feedforward_second,
):
    work_proj, work_boxes, work_places, work_visual, work_small, work_table, work_ffn = (
        lax.all_gather(projections.astype(jnp.bfloat16), "dp", axis=1, tiled=True),
        lax.all_gather(box_tables.astype(jnp.bfloat16), "dp", axis=1, tiled=True),
        lax.all_gather(position_table.astype(jnp.bfloat16), "dp", axis=0, tiled=True),
        lax.all_gather(visual_proj.astype(jnp.bfloat16), "dp", axis=0, tiled=True),
        lax.all_gather(small_params.astype(jnp.bfloat16), "dp", axis=1, tiled=True),
        lax.all_gather(word_table.astype(jnp.bfloat16), "dp", axis=0, tiled=True),
        lax.all_gather(feedforward.astype(jnp.bfloat16), "dp", axis=1, tiled=True),
    )
    small_float = work_small.astype(jnp.float32)
    model_index = lax.axis_index("mp")
    vocab_shard = work_table.shape[0]
    hidden_shard = work_ffn.shape[2]
    width = D
    seq_count = text_box.shape[0]
    length = TEXT + GRID * GRID
    row_count = seq_count * length
    rel_low = work_small[10 + FF // D : 13 + FF // D].reshape(3 * NB, H)
    local_ids = tokens - model_index * vocab_shard
    inside = (local_ids >= 0) & (local_ids < vocab_shard)
    safe_index = jnp.clip(local_ids, 0, vocab_shard - 1)
    partial_word = jnp.where(
        inside[..., None], jnp.take(work_table, safe_index, axis=0), jnp.zeros((), jnp.bfloat16)
    )
    word = lax.psum_scatter(partial_word, "mp", scatter_dimension=0, tiled=True).astype(jnp.float32)
    vis_term = jnp.dot(features, work_visual, preferred_element_type=jnp.float32).reshape(
        seq_count, GRID * GRID, width
    )

    def embed_local(word_in, vis_in, places_in, boxes_in):
        text = word_in + places_in + spatial(text_box, boxes_in)
        visual = vis_in + places_in[: GRID * GRID] + spatial(grid_boxes(), boxes_in)[None]
        return jnp.concatenate([text, visual], 1)

    embedded, embed_pullback = jax.vjp(
        embed_local, word, vis_term, work_places.astype(jnp.float32), work_boxes.astype(jnp.float32)
    )
    normed_zero, norm_zero_pullback = jax.vjp(layer_norm, embedded, small_float[0], small_float[1])
    normed_low = normed_zero.reshape(row_count, width).astype(jnp.bfloat16)
    bias_rows = jnp.stack([small_float[2], jnp.zeros_like(small_float[2]), small_float[3]])
    projected = jnp.einsum(
        "nd,kde->kne", normed_low, work_proj[:3], preferred_element_type=jnp.float32
    )
    projected = (
        (projected + bias_rows[:, None, :])
        .astype(jnp.bfloat16)
        .reshape(3, seq_count, length, H, HD)
    )

    def attend_forward(inputs):
        queries, keys, values, box_in, segment_in, alive_in = inputs
        scores, buckets = scores_of(rel_low, queries, keys, box_in, segment_in, alive_in)
        highest = jnp.max(scores, -1, keepdims=True)
        powers = jnp.exp(scores - highest)
        summed = jnp.sum(powers, -1, keepdims=True)
        shares = (powers / summed).astype(jnp.bfloat16)
        mixture = jnp.einsum("hqk,khc->qhc", shares, values, preferred_element_type=jnp.float32)
        return (mixture.astype(jnp.bfloat16), highest + jnp.log(summed))

    mixture, log_total = lax.map(
        attend_forward, (projected[0], projected[1], projected[2], text_box, segments, alive_text)
    )
    mixed_flat = mixture.reshape(row_count, width)
    attn_out = (
        jnp.dot(mixed_flat, work_proj[3], preferred_element_type=jnp.float32) + small_float[4]
    )
    summed_one = normed_zero.reshape(row_count, width) + attn_out
    normed_one, norm_one_pullback = jax.vjp(layer_norm, summed_one, small_float[5], small_float[6])
    normed_one_low = normed_one.astype(jnp.bfloat16)
    ffn_bias_full = small_float[10 : 10 + FF // D].reshape(-1)
    ffn_bias = lax.dynamic_slice_in_dim(ffn_bias_full, model_index * hidden_shard, hidden_shard)
    piece = lax.all_gather(normed_one_low, "mp", axis=0, tiled=True)
    kept_rows = piece
    fresh = jnp.dot(piece, work_ffn[0], preferred_element_type=jnp.float32) + ffn_bias
    pre_active = fresh
    active_low = jax.nn.gelu(pre_active, approximate=False).astype(jnp.bfloat16)
    ffn_out = (
        lax.psum_scatter(
            jnp.dot(active_low, work_ffn[1].T, preferred_element_type=jnp.float32),
            "mp",
            scatter_dimension=0,
            tiled=True,
        )
        + small_float[7]
    )
    summed_two = normed_one + ffn_out
    normed_two, norm_two_pullback = jax.vjp(layer_norm, summed_two, small_float[8], small_float[9])
    token_rows = mask_pos // TEXT * length + mask_pos % TEXT
    picked = jnp.take(normed_two, token_rows, axis=0).astype(jnp.bfloat16)
    group_picked = lax.all_gather(picked, "mp", axis=0, tiled=True)
    logits = jnp.dot(group_picked, work_table.T, preferred_element_type=jnp.float32)
    local_high = jnp.max(logits, -1)
    local_sum = jnp.sum(jnp.exp(logits - local_high[:, None]), -1)
    label_local = mask_label - model_index * vocab_shard
    label_here = (label_local >= 0) & (label_local < vocab_shard)
    label_clamped = jnp.clip(label_local, 0, vocab_shard - 1)
    target_part = jnp.where(
        label_here, jnp.take_along_axis(logits, label_clamped[:, None], 1)[:, 0], 0.0
    )

    def combine_stats(earlier, later):
        highest = jnp.maximum(earlier[0], later[0])
        return (
            highest,
            earlier[1] * jnp.exp(earlier[0] - highest) + later[1] * jnp.exp(later[0] - highest),
            earlier[2] + later[2],
        )

    high_all, sum_all, target_all = combined_all(
        (local_high, local_sum, target_part), "mp", combine_stats
    )
    log_rows = high_all + jnp.log(sum_all)
    valid_float = mask_valid.astype(jnp.float32)
    slot_count = mask_pos.shape[0]
    own_loss = lax.dynamic_slice_in_dim(
        valid_float * (log_rows - target_all), model_index * slot_count, slot_count
    )
    own_valid = lax.dynamic_slice_in_dim(valid_float, model_index * slot_count, slot_count)
    label_hit = (jnp.arange(vocab_shard)[None, :] == label_local[:, None]).astype(jnp.float32)
    grad_logits = ((jnp.exp(logits - log_rows[:, None]) - label_hit) * valid_float[:, None]).astype(
        jnp.bfloat16
    )
    grad_table = jnp.dot(grad_logits.T, group_picked, preferred_element_type=jnp.float32)
    grad_picked = lax.psum_scatter(
        jnp.dot(grad_logits, work_table, preferred_element_type=jnp.float32),
        "mp",
        scatter_dimension=0,
        tiled=True,
    )
    grad_two = jnp.zeros((row_count, width), jnp.float32).at[token_rows].add(grad_picked)
    grad_summed_two, grad_gain_two, grad_shift_two = norm_two_pullback(grad_two)
    grad_ffn_low = grad_summed_two.astype(jnp.bfloat16)
    piece = lax.all_gather(grad_ffn_low, "mp", axis=0, tiled=True)
    grad_down = jnp.dot(piece.T, active_low, preferred_element_type=jnp.float32)
    grad_active = jnp.dot(piece, work_ffn[1], preferred_element_type=jnp.float32)
    fresh = gelu_back(pre_active, grad_active)
    grad_down, grad_pre = (grad_down, fresh)
    grad_up = jnp.dot(kept_rows.T, grad_pre, preferred_element_type=jnp.float32)
    grad_ffn_bias = jnp.sum(grad_pre.astype(jnp.float32), 0)
    grad_one = grad_summed_two + lax.psum_scatter(
        jnp.dot(grad_pre, work_ffn[0].T, preferred_element_type=jnp.float32),
        "mp",
        scatter_dimension=0,
        tiled=True,
    )
    grad_ffn = jnp.stack([grad_up, grad_down])
    bias_full = lax.dynamic_update_slice_in_dim(
        jnp.zeros((FF,), jnp.float32), grad_ffn_bias, model_index * hidden_shard, 0
    ).reshape(FF // D, width)
    grad_summed_one, grad_gain_one, grad_shift_one = norm_one_pullback(grad_one)
    grad_attn_low = grad_summed_one.astype(jnp.bfloat16)
    grad_out_weight = jnp.dot(mixed_flat.T, grad_attn_low, preferred_element_type=jnp.float32)
    grad_mixed = jnp.dot(grad_attn_low, work_proj[3].T, preferred_element_type=jnp.float32)
    grad_mixed = grad_mixed.astype(jnp.bfloat16).reshape(seq_count, length, H, HD)

    def attend_backward(inputs):
        queries, keys, values, box_in, segment_in, alive_in, log_in, grad_in = inputs
        scores, buckets = scores_of(rel_low, queries, keys, box_in, segment_in, alive_in)
        shares = jnp.exp(scores - log_in)
        grad_values = jnp.einsum(
            "hqk,qhc->khc", shares.astype(jnp.bfloat16), grad_in, preferred_element_type=jnp.float32
        )
        grad_shares = jnp.einsum(
            "qhc,khc->hqk", grad_in, values, preferred_element_type=jnp.float32
        )
        grad_scores = shares * (grad_shares - jnp.sum(shares * grad_shares, -1, keepdims=True))
        grad_scores_low = grad_scores.astype(jnp.bfloat16)
        grad_queries = (
            jnp.einsum("hqk,khc->qhc", grad_scores_low, keys, preferred_element_type=jnp.float32)
            * 0.125
        )
        grad_keys = (
            jnp.einsum("hqk,qhc->khc", grad_scores_low, queries, preferred_element_type=jnp.float32)
            * 0.125
        )
        grad_rel = jnp.concatenate(
            [
                jnp.einsum(
                    "gjl,sjl->gs",
                    kind_onehot(buckets, kind),
                    grad_scores_low,
                    preferred_element_type=jnp.float32,
                )
                for kind in range(3)
            ],
            0,
        )
        return (
            grad_queries.astype(jnp.bfloat16),
            grad_keys.astype(jnp.bfloat16),
            grad_values.astype(jnp.bfloat16),
            grad_rel,
        )

    grad_queries, grad_keys, grad_values, grad_rel = lax.map(
        attend_backward,
        (
            projected[0],
            projected[1],
            projected[2],
            text_box,
            segments,
            alive_text,
            log_total,
            grad_mixed,
        ),
    )
    grad_proj = jnp.stack([grad_queries, grad_keys, grad_values]).reshape(3, row_count, width)
    grad_in_weight = jnp.einsum(
        "nd,kne->kde", normed_low, grad_proj, preferred_element_type=jnp.float32
    )
    grad_zero = grad_summed_one + jnp.einsum(
        "kne,kde->nd", grad_proj, work_proj[:3], preferred_element_type=jnp.float32
    )
    grad_embedded, grad_gain_zero, grad_shift_zero = norm_zero_pullback(
        grad_zero.reshape(seq_count, length, width)
    )
    grad_word, grad_vis, grad_places, grad_boxes = embed_pullback(grad_embedded)
    group_word = lax.all_gather(grad_word.astype(jnp.bfloat16), "mp", axis=0, tiled=True)
    grad_table = grad_table + jnp.zeros((vocab_shard, width), jnp.float32).at[safe_index].add(
        jnp.where(inside[..., None], group_word.astype(jnp.float32), 0.0)
    )
    grad_visual = jnp.dot(
        features.T,
        grad_vis.astype(jnp.bfloat16).reshape(-1, width),
        preferred_element_type=jnp.float32,
    )
    grad_proj_float = grad_proj.astype(jnp.float32)
    grad_small = jnp.concatenate(
        [
            jnp.stack(
                [
                    grad_gain_zero,
                    grad_shift_zero,
                    jnp.sum(grad_proj_float[0], 0),
                    jnp.sum(grad_proj_float[2], 0),
                    jnp.sum(grad_attn_low.astype(jnp.float32), 0),
                    grad_gain_one,
                    grad_shift_one,
                    jnp.sum(grad_ffn_low.astype(jnp.float32), 0),
                    grad_gain_two,
                    grad_shift_two,
                ]
            ),
            bias_full,
            jnp.sum(grad_rel, 0).reshape(3, width),
        ],
        0,
    )
    grad_attn = jnp.concatenate([grad_in_weight, grad_out_weight[None]], 0)
    shared_parts = (
        lax.psum_scatter(grad_attn, "dp", scatter_dimension=1, tiled=True),
        lax.psum_scatter(grad_boxes, "dp", scatter_dimension=1, tiled=True),
        lax.psum_scatter(grad_places, "dp", scatter_dimension=0, tiled=True),
        lax.psum_scatter(grad_visual, "dp", scatter_dimension=0, tiled=True),
        lax.psum_scatter(grad_small, "dp", scatter_dimension=1, tiled=True),
    )
    reduced_proj, reduced_boxes, reduced_places, reduced_visual, reduced_small = lax.psum(
        (shared_parts[0], shared_parts[1], shared_parts[2], shared_parts[3], shared_parts[4]), "mp"
    )
    reduced_table, reduced_ffn = (
        lax.psum_scatter(grad_table, "dp", scatter_dimension=0, tiled=True),
        lax.psum_scatter(grad_ffn, "dp", scatter_dimension=1, tiled=True),
    )
    reduced = (
        reduced_proj,
        reduced_boxes,
        reduced_places,
        reduced_visual,
        reduced_small,
        reduced_table,
        reduced_ffn,
    )
    shared_squares = jnp.zeros((), jnp.float32)
    for part in reduced[:5]:
        shared_squares = shared_squares + jnp.sum(part * part)
    split_squares = jnp.sum(reduced_table * reduced_table) + jnp.sum(reduced_ffn * reduced_ffn)
    squares = split_squares + jnp.where(model_index == 0, shared_squares, 0.0)
    total_squares, loss_sum, loss_count = lax.psum(
        (squares, jnp.sum(own_loss), jnp.sum(own_valid)), ("dp", "mp")
    )
    grad_norm = jnp.sqrt(total_squares) / loss_count
    factor = jnp.minimum(1.0, CLIP / grad_norm)
    masters = (
        projections,
        box_tables,
        position_table,
        visual_proj,
        small_params,
        word_table,
        feedforward,
    )
    firsts = (
        projections_first,
        box_tables_first,
        position_table_first,
        visual_proj_first,
        small_params_first,
        word_table_first,
        feedforward_first,
    )
    seconds = (
        projections_second,
        box_tables_second,
        position_table_second,
        visual_proj_second,
        small_params_second,
        word_table_second,
        feedforward_second,
    )
    outputs = []
    for index in range(7):
        outputs.extend(
            adam_step(
                masters[index],
                reduced[index] / loss_count * factor,
                firsts[index],
                seconds[index],
                RATES[index],
            )
        )
    return tuple(outputs) + (loss_sum, loss_count, grad_norm)


def solution(mesh):
    in_specs = (
        P("dp", None),
        P(("dp", "mp"), None, None),
        P(("dp", "mp"), None),
        P(("dp", "mp"), None),
        P(("dp", "mp"), None),
        P(("dp", "mp")),
        P("dp"),
        P("dp"),
        P(None, "dp", None),
        P(None, "dp", None),
        P(None, "dp", None),
        P(None, "dp", None),
        P(None, "dp", None),
        P(None, "dp", None),
        P("dp", None),
        P("dp", None),
        P("dp", None),
        P("dp", None),
        P("dp", None),
        P("dp", None),
        P(None, "dp"),
        P(None, "dp"),
        P(None, "dp"),
        P(("mp", "dp"), None),
        P(("mp", "dp"), None),
        P(("mp", "dp"), None),
        P(None, "dp", "mp"),
        P(None, "dp", "mp"),
        P(None, "dp", "mp"),
    )
    out_specs = (
        P(None, "dp", None),
        P(None, "dp", None),
        P(None, "dp", None),
        P(None, "dp", None),
        P(None, "dp", None),
        P(None, "dp", None),
        P("dp", None),
        P("dp", None),
        P("dp", None),
        P("dp", None),
        P("dp", None),
        P("dp", None),
        P(None, "dp"),
        P(None, "dp"),
        P(None, "dp"),
        P(("mp", "dp"), None),
        P(("mp", "dp"), None),
        P(("mp", "dp"), None),
        P(None, "dp", "mp"),
        P(None, "dp", "mp"),
        P(None, "dp", "mp"),
        P(),
        P(),
        P(),
    )
    return jax.shard_map(
        on_device, mesh=mesh, in_specs=in_specs, out_specs=out_specs, check_vma=False
    )
```

profile of v0, /device:TPU:0, one launch (start us, length us, event | category | flops | bytes accessed | tf_op | source)
XLA Modules:
  0.0 1658.2 jit_solution(2389925356989884977)
XLA Ops:
  11.1 46.0 %all-gather.14.cloned.1.call-done = bf16[3840,768]{1,0:T(8,128)(2,1)} async-done(((bf16[480,768]{1,0:T(8,128)(2,1)}), bf16[3840,768]{1,0:T(8,128)(2,1)}) %all-gather.14.cloned.1.call-update) | async-done | bytes 5898256 | tf_op jit(solution)/shard_map/all_gather | solution.py:171
  57.1 11.9 gather_fusion
  73.5 9.1 all-gather.3
  82.8 9.5 all_gather.52
  95.1 16.8 %fusion.4 = f32[561,561,12]{1,2,0:T(8,128)} fusion(s32[561,561]{1,0:T(8,128)S(1)} %fusion.59, s32[64]{0:T(128)S(1)} %iota_add_fusion, bf16[64,12]{1,0:T(8,128)(2,1)S(1)} %slice.186), kind=kOutput, calls=%fused_computation.35 | convolution fusion | flops 503553600 | bytes 16367284 | tf_op jit(solution)/shard_map/while/body/eval_jaxpr/vti,vn->nti/dot_general | solution.py:110
  111.8 26.3 %copy.172 = f32[561,561,12]{0,1,2:T(8,128)} copy(f32[561,561,12]{1,2,0:T(8,128)} %fusion.4) | data formatting | bytes 30213216 | tf_op jit(solution)/shard_map/while/body/eval_jaxpr/vti,vn->nti/dot_general | solution.py:110
  139.5 19.3 %fusion.11 = f32[561,561,12]{1,2,0:T(8,128)} fusion(s32[561,561]{1,0:T(8,128)S(1)} %fusion.53, bf16[64,12]{1,0:T(8,128)(2,1)S(1)} %slice.180), kind=kOutput, calls=%fused_computation.43 | convolution fusion | flops 503553600 | bytes 16367028 | tf_op jit(solution)/shard_map/while/body/eval_jaxpr/vti,vn->nti/dot_general | solution.py:110
  158.8 26.8 %copy.169 = f32[561,561,12]{0,1,2:T(8,128)} copy(f32[561,561,12]{1,2,0:T(8,128)} %fusion.11) | data formatting | bytes 30213216 | tf_op jit(solution)/shard_map/while/body/eval_jaxpr/vti,vn->nti/dot_general | solution.py:110
  186.9 16.5 fusion.8
  203.4 26.3 %copy.170 = f32[561,561,12]{0,1,2:T(8,128)} copy(f32[561,561,12]{1,2,0:T(8,128)} %fusion.8) | data formatting | bytes 30213216 | tf_op jit(solution)/shard_map/while/body/eval_jaxpr/vti,vn->nti/dot_general | solution.py:110
  229.8 9.5 all_gather.54
  273.4 25.3 %fusion.171 = (f32[12,561]{1,0:T(8,128)S(1)}, f32[12,561,561]{1,2,0:T(8,128)}) fusion(f32[561,561,12]{0,1,2:T(8,128)} %copy.172, f32[561,561,12]{0,1,2:T(8,128)} %copy.169, f32[561,561,12]{0,1,2:T(8,128)} %copy.170, bf16[561,12,64]{0,2,1:T(8,128)(2,1)} %bitcast.233, bf16[561,12,64]{0,2,1:T(8,128)(2,1)S(1)} %bitcast.228, pred[561,561]{0,1:T(8,128)(4,1)S(1)} %copy-done.42), kind=kOutput, calls=%fused_computation.427 | convolution fusion | flops 506064576 | bytes 62491472 | tf_op jit(solution)/shard_map/while/body/eval_jaxpr/qhc,khc->hqk/dot_general | solution.py:107
  298.7 8.5 fusion.23
  307.3 9.2 fusion.47
  326.5 63.9 %all-gather.24.cloned.1.call-done = bf16[4,561,768]{2,1,0:T(8,128)(2,1)} async-done(((bf16[1,561,768]{2,1,0:T(8,128)(2,1)}), bf16[4,561,768]{2,1,0:T(8,128)(2,1)}) %all-gather.24.cloned.1.call-update) | async-done | bytes 3446800 | tf_op jit(solution)/shard_map/all_gather | solution.py:236
  395.0 25.4 %all-gather.20.cloned.1.call-done = bf16[2,768,768]{2,1,0:T(8,128)(2,1)} async-done(((bf16[2,96,768]{2,1,0:T(8,128)(2,1)}), bf16[2,768,768]{2,1,0:T(8,128)(2,1)}) %all-gather.20.cloned.1.call-update) | async-done | bytes 2359312 | tf_op jit(solution)/shard_map/all_gather | solution.py:172
  420.4 20.8 %multiply_convert_fusion.1 = (bf16[2244,768]{1,0:T(8,128)(2,1)S(1)}, f32[2244,768]{1,0:T(8,128)}, f32[2244,768]{1,0:T(8,128)}) fusion(f32[768]{0:T(1024)S(1)} %dynamic_slice.81, bf16[2244,768]{1,0:T(8,128)(2,1)} %reshape.1170, bf16[2,768,768]{2,1,0:T(8,128)(2,1)} %all-gather.20.cloned.1.call-done), kind=kOutput, calls=%fused_computation.71 | convolution fusion | flops 2760873984 | bytes 21869568 | tf_op jit(solution)/shard_map/dot_general | solution.py:238
  447.8 124.0 %fusion = f32[568,768]{1,0:T(8,128)S(1)} fusion(f32[2244,768]{1,0:T(8,128)} %fusion.87), kind=kCustom, calls=%all-reduce-scatter | all-reduce-scatter fusion | flops 1744897 | bytes 8638976
  588.7 15.8 all_gather.59
  613.3 6.8 gather_fusion.14
  623.8 19.1 %all-reduce.24 = (f32[1280]{0:T(1024)}, f32[1280]{0:T(1024)}, f32[1280]{0:T(1024)}) all-reduce(f32[1280]{0:T(1024)} %copy-done.81, f32[1280]{0:T(1024)} %dynamic-update-slice.1, f32[1280]{0:T(1024)S(1)} %select_dynamic-update-slice_fusion), channel_id=2, replica_groups=mesh['dp'=8,'mp'=4] {'mp'}, use_global_device_ids=true, to_apply=%add.15 | all-reduce | flops 3840 | bytes 30720
  655.4 7.9 fusion.154
  663.4 23.9 %reduce-scatter.19.cloned.1.call-done = f32[80,768]{1,0:T(8,128)} async-done(((f32[320,768]{1,0:T(8,128)}), f32[80,768]{1,0:T(8,128)}) %reduce-scatter.19.cloned.1.call-update) | async-done | bytes 245776 | tf_op jit(solution)/shard_map/reduce_scatter | solution.py:288
  696.1 67.9 %all-gather.26.cloned.1.call-done = bf16[4,561,768]{2,1,0:T(8,128)(2,1)} async-done(((bf16[1,561,768]{2,1,0:T(8,128)(2,1)}), bf16[4,561,768]{2,1,0:T(8,128)(2,1)}) %all-gather.26.cloned.1.call-update) | async-done | bytes 3446800 | tf_op jit(solution)/shard_map/all_gather | solution.py:297
  768.7 12.1 convert_reduce_fusion
  787.7 121.7 %fusion.1 = f32[568,768]{1,0:T(8,128)S(1)} fusion(f32[2244,768]{1,0:T(8,128)} %fusion.84), kind=kCustom, calls=%all-reduce-scatter.1 | all-reduce-scatter fusion | flops 1744897 | bytes 8638976
  913.4 7.3 concatenate.74
  928.2 9.7 fusion.48
  937.9 11.2 multiply_reduce_fusion
  949.1 12.4 multiply_convert_fusion
  984.0 12.0 copy.183
  1046.7 19.4 %copy.186 = bf16[12,561,561]{2,0,1:T(8,128)(2,1)} copy(bf16[12,561,561]{1,2,0:T(8,128)(2,1)} %copy-done.1) | data formatting | bytes 15106608 | tf_op jit(solution)/shard_map/while/body/eval_jaxpr/convert_element_type | solution.py:331
  1068.6 16.7 %fusion.77 = f32[64,12]{0,1:T(8,128)S(1)} fusion(bf16[12,561,561]{2,0,1:T(8,128)(2,1)} %copy.186, s32[561,561]{1,0:T(8,128)S(1)} %copy-done.19), kind=kOutput, calls=%fused_computation.205 | convolution fusion | flops 503553600 | bytes 8815260 | tf_op jit(solution)/shard_map/while/body/eval_jaxpr/gjl,sjl->gs/dot_general | solution.py:342
  1085.4 17.2 %fusion.81 = f32[64,12]{0,1:T(8,128)S(1)} fusion(bf16[12,561,561]{2,0,1:T(8,128)(2,1)S(1)} %bitcast.232, s32[561,561]{1,0:T(8,128)S(1)} %copy-done.17, s32[64]{0:T(128)S(1)} %copy-done.107), kind=kOutput, calls=%fused_computation.207 | convolution fusion | flops 503553600 | bytes 8815516 | tf_op jit(solution)/shard_map/while/body/eval_jaxpr/gjl,sjl->gs/dot_general | solution.py:342
  1102.6 17.5 %fusion.78 = f32[64,12]{0,1:T(8,128)S(1)} fusion(bf16[12,561,561]{2,0,1:T(8,128)(2,1)S(1)} %bitcast.232, s32[561,561]{1,0:T(8,128)S(1)} %copy-done.21, s32[64]{0:T(128)S(1)} %copy-done.105), kind=kOutput, calls=%fused_computation.206 | convolution fusion | flops 503553600 | bytes 8815516 | tf_op jit(solution)/shard_map/while/body/eval_jaxpr/gjl,sjl->gs/dot_general | solution.py:342
  1121.6 12.6 all-reduce.29.cloned.1.call-done
  1136.8 35.5 %reduce-scatter.29.cloned.1.call-done = f32[32,768]{1,0:T(8,128)} async-done(((f32[256,768]{1,0:T(8,128)}), f32[32,768]{1,0:T(8,128)}) %reduce-scatter.29.cloned.1.call-update) | async-done | bytes 98320 | tf_op jit(solution)/shard_map/reduce_scatter | solution.py:419
  1172.3 41.8 %reduce-scatter.27.cloned.1.call-done = f32[64,768]{1,0:T(8,128)} async-done(((f32[512,768]{1,0:T(8,128)}), f32[64,768]{1,0:T(8,128)}) %reduce-scatter.27.cloned.1.call-update) | async-done | bytes 196624 | tf_op jit(solution)/shard_map/reduce_scatter | solution.py:418
  1214.1 44.4 %reduce-scatter.25.cloned.1.call-done = f32[4,128,128]{2,1,0:T(8,128)} async-done(((f32[4,1024,128]{2,1,0:T(8,128)}), f32[4,128,128]{2,1,0:T(8,128)}) %reduce-scatter.25.cloned.1.call-update) | async-done | bytes 262160 | tf_op jit(solution)/shard_map/reduce_scatter | solution.py:417
  1271.5 10.7 fusion.153
  1282.1 41.5 %all-gather.22.cloned.1.call-done = bf16[4,512,768]{2,1,0:T(8,128)(2,1)} async-done(((bf16[1,512,768]{2,1,0:T(8,128)(2,1)}), bf16[4,512,768]{2,1,0:T(8,128)(2,1)}) %all-gather.22.cloned.1.call-update) | async-done | bytes 3145744 | tf_op jit(solution)/shard_map/all_gather | solution.py:383
  1328.1 23.3 %scatter_fusion = f32[3840,768]{1,0:T(8,128)} fusion(f32[3840,768]{1,0:T(8,128)} %fusion.153, s32[2048]{0:T(1024)S(1)} %bitcast.259, f32[2048,768]{1,0:T(8,128)} %bitcast.227), kind=kCustom, calls=%fused_computation.16 | custom fusion | flops 1572864 | bytes 18882560 | tf_op jit(solution)/shard_map/scatter-add | solution.py:384
  1352.8 7.2 reduce-scatter.31.cloned.1.call-done
  1360.9 19.2 %psum.61 = f32[17,96]{1,0:T(8,128)S(1)} all-reduce(f32[17,96]{1,0:T(8,128)S(1)} %copy.204), channel_id=1, replica_groups=mesh['dp'=8,'mp'=4] {'mp'}, use_global_device_ids=true, to_apply=%region_67.68 | all-reduce | flops 1632 | bytes 13056 | tf_op jit(solution)/shard_map/psum | solution.py:422
  1380.6 58.3 %all-reduce.31.cloned.1.call-done = (f32[4,96,768]{2,1,0:T(8,128)}, f32[4,128,128]{2,1,0:T(8,128)}, f32[64,768]{1,0:T(8,128)}, f32[32,768]{1,0:T(8,128)}) async-done(((f32[4,96,768]{2,1,0:T(8,128)}, f32[4,128,128]{2,1,0:T(8,128)}, f32[64,768]{1,0:T(8,128)}, f32[32,768]{1,0:T(8,128)}), (f32[4,96,768]{2,1,0:T(8,128)}, f32[4,128,128]{2,1,0:T(8,128)}, f32[64,768]{1,0:T(8,128)}, ...) | async-done | bytes 1736720 | tf_op jit(solution)/shard_map/psum | solution.py:422
  1449.3 45.9 %reduce-scatter.23.cloned.1.call-done = f32[2,96,768]{2,1,0:T(8,128)} async-done(((f32[2,768,768]{2,1,0:T(8,128)}), f32[2,96,768]{2,1,0:T(8,128)}) %reduce-scatter.23.cloned.1.call-update) | async-done | bytes 589840 | tf_op jit(solution)/shard_map/reduce_scatter | solution.py:427
  1497.0 90.2 %reduce-scatter.21.cloned.1.call-done = f32[480,768]{1,0:T(8,128)} async-done(((f32[3840,768]{1,0:T(8,128)}), f32[480,768]{1,0:T(8,128)}) %reduce-scatter.21.cloned.1.call-update) | async-done | bytes 1474576 | tf_op jit(solution)/shard_map/reduce_scatter | solution.py:426
  1590.8 39.8 %all-reduce.23 = (f32[]{:T(128)}, f32[]{:T(128)}, f32[]{:T(128)}) all-reduce(f32[]{:T(128)} %get-tuple-element.481, f32[]{:T(128)S(6)} %add.946, f32[]{:T(128)} %get-tuple-element.480), channel_id=1, replica_groups=mesh['dp'=8,'mp'=4] {'dp','mp'}, use_global_device_ids=true, to_apply=%region_25.26 | all-reduce | flops 3 | bytes 24 | tf_op jit(solution)/shard_map/psum | solution.py:443
  (561 shorter events, 272.5 us)
Async XLA Ops:
  7.2 252.7 %copy-start = (bf16[49,256]{1,0:T(8,128)(2,1)S(1)}, bf16[49,256]{1,0:T(8,128)(2,1)}, u32[]{:S(2)}) copy-start(bf16[49,256]{1,0:T(8,128)(2,1)} %param.35) | copy-start | bytes 75268
  7.2 49.9 %all-gather.14.cloned.1.call-start = ((), (), s32[]{:S(2)}) async-start(), calls=%async_computation.8 | async-start | bytes 6635520 | tf_op jit(solution)/shard_map/all_gather | solution.py:171
  9.6 233.1 %all-gather.16.cloned.1.call-start = ((), (), s32[]{:S(2)}) async-start(), calls=%async_computation.10 | async-start | bytes 1179648 | tf_op jit(solution)/shard_map/all_gather | solution.py:167
  10.4 250.7 %reduce-scatter.17.cloned.1.call-start = ((), (), s32[]{:S(2)}) async-start(), calls=%async_computation.9 | async-start | bytes 3932160 | tf_op jit(solution)/shard_map/reduce_scatter | solution.py:189
  10.5 58.5 %copy-start.86 = (pred[4,512]{1,0:T(4,128)(4,1)}, pred[4,512]{1,0:T(4,128)(4,1)S(1)}, u32[]{:S(2)}) copy-start(pred[4,512]{1,0:T(4,128)(4,1)S(1)} %get-tuple-element.458) | copy-start | bytes 6148
  71.2 192.4 %all-gather.18.cloned.1.call-start = ((), (), s32[]{:S(2)}) async-start(), calls=%async_computation.11 | async-start | bytes 5308416 | tf_op jit(solution)/shard_map/all_gather | solution.py:166
  73.3 317.1 %all-gather.24.cloned.1.call-start = ((), (), s32[]{:S(2)}) async-start(), calls=%async_computation.19 | async-start | bytes 4362240 | tf_op jit(solution)/shard_map/all_gather | solution.py:236
  73.4 21.6 %copy-start.106 = (s32[64]{0:T(128)}, s32[64]{0:T(128)S(1)}, u32[]{:S(2)}) copy-start(s32[64]{0:T(128)S(1)} %iota_add_fusion) | copy-start | bytes 772
  73.5 113.4 %copy-start.104 = (s32[64]{0:T(128)}, s32[64]{0:T(128)S(1)}, u32[]{:S(2)}) copy-start(s32[64]{0:T(128)S(1)} %iota_add_fusion.1) | copy-start | bytes 772
  94.9 17.0 %copy-start.16 = (s32[561,561]{1,0:T(8,128)}, s32[561,561]{1,0:T(8,128)S(1)}, u32[]{:S(2)}) copy-start(s32[561,561]{1,0:T(8,128)S(1)} %fusion.59) | copy-start | bytes 3776656
  139.3 19.5 %copy-start.18 = (s32[561,561]{1,0:T(8,128)}, s32[561,561]{1,0:T(8,128)S(1)}, u32[]{:S(2)}) copy-start(s32[561,561]{1,0:T(8,128)S(1)} %fusion.53) | copy-start | bytes 3776656
  203.4 26.4 %copy-start.102 = (s32[1,512]{1,0:T(1,128)S(1)}, s32[1,512]{1,0:T(1,128)}, u32[]{:S(2)}) copy-start(s32[1,512]{1,0:T(1,128)} %param.33) | copy-start | bytes 6148
  203.4 36.1 %copy-start.116 = (s32[1,512]{1,0:T(1,128)S(1)}, s32[1,512]{1,0:T(1,128)}, u32[]{:S(2)}) copy-start(s32[1,512]{1,0:T(1,128)} %param.34) | copy-start | bytes 6148
  241.0 75.5 %copy-start.77 = (f32[768]{0:T(1024)}, f32[768]{0:T(1024)S(1)}, u32[]{:S(2)}) copy-start(f32[768]{0:T(1024)S(1)} %get-tuple-element.450) | copy-start | bytes 9220
  261.0 55.5 %copy-start.27 = (f32[49,768]{1,0:T(8,128)}, f32[49,768]{1,0:T(8,128)S(1)}, u32[]{:S(2)}) copy-start(f32[49,768]{1,0:T(8,128)S(1)} %fusion.76) | copy-start | bytes 451588
  263.0 53.5 %copy-start.2 = (f32[1,512,768]{2,1,0:T(8,128)}, f32[1,512,768]{2,1,0:T(8,128)S(1)}, u32[]{:S(2)}) copy-start(f32[1,512,768]{2,1,0:T(8,128)S(1)} %fusion.43) | copy-start | bytes 4718596
  263.2 53.3 %copy-start.67 = (f32[561]{0:T(1024)}, f32[561]{0:T(1024)S(1)}, u32[]{:S(2)}) copy-start(f32[561]{0:T(1024)S(1)} %broadcast_multiply_fusion.2) | copy-start | bytes 6736
  263.6 53.0 %copy-start.79 = (f32[561]{0:T(1024)}, f32[561]{0:T(1024)S(1)}, u32[]{:S(2)}) copy-start(f32[561]{0:T(1024)S(1)} %fusion.132) | copy-start | bytes 6736
  273.4 25.3 %copy-start.8 = (bf16[1,561,768]{1,2,0:T(8,128)(2,1)}, bf16[1,561,768]{1,2,0:T(8,128)(2,1)S(1)}, u32[]{:S(2)}) copy-start(bf16[1,561,768]{1,2,0:T(8,128)(2,1)S(1)} %copy.165) | copy-start | bytes 2585092
  321.1 99.3 %all-gather.20.cloned.1.call-start = ((), (), s32[]{:S(2)}) async-start(), calls=%async_computation.12 | async-start | bytes 2654208 | tf_op jit(solution)/shard_map/all_gather | solution.py:172
  321.9 365.4 %reduce-scatter.19.cloned.1.call-start = ((), (), s32[]{:S(2)}) async-start(), calls=%async_computation.13 | async-start | bytes 1228800 | tf_op jit(solution)/shard_map/reduce_scatter | solution.py:288
  324.0 96.4 %copy-start.113 = (f32[768]{0:T(1024)}, f32[768]{0:T(1024)S(1)}, u32[]{:S(2)}) copy-start(f32[768]{0:T(1024)S(1)} %dynamic_slice.81) | copy-start | bytes 9220
  326.5 247.2 %copy-start.125 = (s32[80]{0:T(128)}, s32[80]{0:T(128)S(1)}, u32[]{:S(2)}) copy-start(s32[80]{0:T(128)S(1)} %get-tuple-element.433) | copy-start | bytes 964
  420.4 22.5 %copy-start.126 = (bf16[2,768,768]{2,1,0:T(8,128)(2,1)S(1)}, bf16[2,768,768]{2,1,0:T(8,128)(2,1)}, u32[]{:S(2)}) copy-start(bf16[2,768,768]{2,1,0:T(8,128)(2,1)} %all-gather.20.cloned.1.call-done) | copy-start | bytes 7077892
  571.7 3.3 collective-permute-start
  663.3 100.7 %all-gather.26.cloned.1.call-start = ((), (), s32[]{:S(2)}) async-start(), calls=%async_computation.20 | async-start | bytes 4362240 | tf_op jit(solution)/shard_map/all_gather | solution.py:297
  696.1 72.6 %copy-start.114 = (f32[768]{0:T(1024)S(1)}, f32[768]{0:T(1024)}, u32[]{:S(2)}) copy-start(f32[768]{0:T(1024)} %copy-done.113) | copy-start | bytes 9220
  696.1 438.1 %all-reduce.29.cloned.1.call-start = ((), (), s32[]{:S(2)}) async-start(), calls=%async_computation.23 | async-start | bytes 18874368
  909.4 3.9 collective-permute-start.1
  996.1 176.2 %reduce-scatter.29.cloned.1.call-start = ((), (), s32[]{:S(2)}) async-start(), calls=%async_computation.21 | async-start | bytes 884736 | tf_op jit(solution)/shard_map/reduce_scatter | solution.py:419
  1006.4 207.8 %reduce-scatter.27.cloned.1.call-start = ((), (), s32[]{:S(2)}) async-start(), calls=%async_computation.18 | async-start | bytes 1769472 | tf_op jit(solution)/shard_map/reduce_scatter | solution.py:418
  1007.8 250.7 %reduce-scatter.25.cloned.1.call-start = ((), (), s32[]{:S(2)}) async-start(), calls=%async_computation.17 | async-start | bytes 2359296 | tf_op jit(solution)/shard_map/reduce_scatter | solution.py:417
  1039.2 284.4 %all-gather.22.cloned.1.call-start = ((), (), s32[]{:S(2)}) async-start(), calls=%async_computation.14 | async-start | bytes 3932160 | tf_op jit(solution)/shard_map/all_gather | solution.py:383
  1042.5 317.5 %reduce-scatter.31.cloned.1.call-start = ((), (), s32[]{:S(2)}) async-start(), calls=%async_computation.22 | async-start | bytes 442368
  1046.7 19.4 %copy-start.112 = (f32[768]{0:T(1024)S(1)}, f32[768]{0:T(1024)}, u32[]{:S(2)}) copy-start(f32[768]{0:T(1024)} %get-tuple-element.359) | copy-start | bytes 9220
  1046.7 21.8 %copy-start.19 = (s32[561,561]{1,0:T(8,128)S(1)}, s32[561,561]{1,0:T(8,128)}, u32[]{:S(2)}) copy-start(s32[561,561]{1,0:T(8,128)} %copy-done.18) | copy-start | bytes 3776656
  1066.1 19.2 %slice-start = ((s8[11489280]{0:T(1024)(128)(4,1)}), s8[4194304]{0:T(1024)(128)(4,1)S(1)}, s32[]{:S(2)}) async-start(s8[11489280]{0:T(1024)(128)(4,1)} %bitcast.231), calls=%async_computation.25 | async-start | bytes 8388608
  1068.6 16.7 %slice-start.1 = ((s8[11489280]{0:T(1024)(128)(4,1)}), s8[4194304]{0:T(1024)(128)(4,1)S(1)}, s32[]{:S(2)}) async-start(s8[11489280]{0:T(1024)(128)(4,1)} %bitcast.231), calls=%async_computation.26 | async-start | bytes 8388608
  1068.6 16.7 %slice-start.2 = ((s8[11489280]{0:T(1024)(128)(4,1)}), s8[3100672]{0:T(1024)(128)(4,1)S(1)}, s32[]{:S(2)}) async-start(s8[11489280]{0:T(1024)(128)(4,1)} %bitcast.231), calls=%async_computation.27 | async-start | bytes 6201344
  1085.4 17.3 %copy-start.21 = (s32[561,561]{1,0:T(8,128)S(1)}, s32[561,561]{1,0:T(8,128)}, u32[]{:S(2)}) copy-start(s32[561,561]{1,0:T(8,128)} %copy-done.20) | copy-start | bytes 3776656
  1085.4 17.3 %copy-start.105 = (s32[64]{0:T(128)S(1)}, s32[64]{0:T(128)}, u32[]{:S(2)}) copy-start(s32[64]{0:T(128)} %copy-done.104) | copy-start | bytes 772
  1121.6 317.4 %all-reduce.31.cloned.1.call-start = ((), (), s32[]{:S(2)}) async-start(), calls=%async_computation.24 | async-start | bytes 3473408 | tf_op jit(solution)/shard_map/psum | solution.py:422
  1258.5 236.6 %reduce-scatter.23.cloned.1.call-start = ((), (), s32[]{:S(2)}) async-start(), calls=%async_computation.16 | async-start | bytes 5308416 | tf_op jit(solution)/shard_map/reduce_scatter | solution.py:427
  1270.5 53.2 %copy-start.87 = (pred[4,512]{1,0:T(4,128)(4,1)S(1)}, pred[4,512]{1,0:T(4,128)(4,1)}, u32[]{:S(2)}) copy-start(pred[4,512]{1,0:T(4,128)(4,1)} %copy-done.86) | copy-start | bytes 6148
  1270.5 316.7 %reduce-scatter.21.cloned.1.call-start = ((), (), s32[]{:S(2)}) async-start(), calls=%async_computation.15 | async-start | bytes 13271040 | tf_op jit(solution)/shard_map/reduce_scatter | solution.py:426
  1282.1 46.0 %copy-start.66 = (s32[1,4,4,128]{3,1,2,0:T(4,128)S(1)}, s32[1,4,4,128]{3,1,2,0:T(4,128)}, u32[]{:S(2)}) copy-start(s32[1,4,4,128]{3,1,2,0:T(4,128)} %copy-done.65) | copy-start | bytes 24580
  1440.6 192.1 %copy-start.25 = (f32[4,96,768]{2,1,0:T(8,128)S(1)}, f32[4,96,768]{2,1,0:T(8,128)}, u32[]{:S(2)}) copy-start(f32[4,96,768]{2,1,0:T(8,128)} %param.39) | copy-start | bytes 3538948
  1440.6 192.1 %copy-start.26 = (f32[4,96,768]{2,1,0:T(8,128)S(1)}, f32[4,96,768]{2,1,0:T(8,128)}, u32[]{:S(2)}) copy-start(f32[4,96,768]{2,1,0:T(8,128)} %get-tuple-element.394) | copy-start | bytes 3538948
  (109 other events, 501.5 us)
Sparse Core Ops, SparseCore 0:
  10.5 46.5 all-gather.13
  59.6 23.6 all-gather.15
  85.6 60.2 reduce-scatter.16
  148.2 38.9 all-gather.17
  321.2 69.1 all-gather.23
  392.7 27.5 all-gather.19
  663.4 23.8 reduce-scatter.18
  696.2 67.7 all-gather.25
  996.2 137.9 all-reduce.28
  1137.2 35.0 reduce-scatter.28
  1175.6 38.4 reduce-scatter.26
  1217.3 41.2 reduce-scatter.24
  1260.1 63.4 all-gather.21
  1327.5 32.4 reduce-scatter.30
  1363.2 75.6 all-reduce.30
  1442.2 52.8 reduce-scatter.22
  1499.0 88.1 reduce-scatter.20
where the time goes:
time: 1670 us; the launch traced here: 1660 us
  waiting for transfers between devices  606 us (36%)
  blocking collectives  368 us (22%)
  matrix products  265 us (16%)
  local copies, waits for them, and re-layouts  219 us (13%)
  other arithmetic  169 us (10%)
  between operations  26.1 us (2%)
    unnamed x3, blocking collectives  265 us
    reduce_scatter x1, waiting for transfers between devices, on_device(): lax.psum_scatter(grad_table, 'dp', scatter_dimension=0, tiled=True)  90.2 us
    dot_general x3, local copies, waits for them, and re-layouts, scores_of(): jnp.einsum('vti,vn->nti', kind_onehot(buckets, kind), rel_low[kind * NB:(...  79.5 us
    all_gather x1, waiting for transfers between devices, on_device(): piece = lax.all_gather(grad_ffn_low, 'mp', axis=0, tiled=True)  67.9 us
    all_gather x1, waiting for transfers between devices, on_device(): piece = lax.all_gather(normed_one_low, 'mp', axis=0, tiled=True)  63.9 us
    psum x1, waiting for transfers between devices, on_device(): lax.psum((shared_parts[0], shared_parts[1], shared_parts[2], shared_parts...  58.3 us
    dot_general x3, matrix products, scores_of(): jnp.einsum('vti,vn->nti', kind_onehot(buckets, kind), rel_low[kind * NB:(...  52.6 us
    dot_general x3, matrix products, attend_backward(): jnp.einsum('gjl,sjl->gs', kind_onehot(buckets, kind), grad_scores_low, pr...  51.4 us
  transfers between devices with their start and end apart: 19, of which 15 were waited for; matrix products, arithmetic and copies ran while one was open for 23% of the time, Pallas kernels for 0%

commit v1 on v0

v1 whole, which is shorter than its diff:
```python
from functools import partial

import jax
import jax.numpy as jnp
from jax import lax
from jax.sharding import PartitionSpec as P

D = 768
H = 12
HD = 64
FF = 3072
NB = 64
GRID = 7
TEXT = 512
STEP = 10


MASKED = -1e30
CLIP = 0.005
BETA_ONE = 0.9
BETA_TWO = 0.999
EPSILON = 1e-08
DECAY = 0.01
RATES = (0.02, 0.03, 0.03, 0.04, 0.3, 0.05, 0.02)


def layer_norm(value, gain, shift):
    average = jnp.mean(value, -1, keepdims=True)
    centred = value - average
    variance = jnp.mean(centred * centred, -1, keepdims=True)
    return centred * lax.rsqrt(variance + 1e-05) * gain + shift


def grid_boxes():
    cells = jnp.arange(GRID * GRID, dtype=jnp.int32)
    row_place = cells // GRID
    column_place = cells % GRID
    return jnp.stack(
        [
            column_place * 1000 // GRID,
            row_place * 1000 // GRID,
            (column_place + 1) * 1000 // GRID,
            (row_place + 1) * 1000 // GRID,
        ],
        -1,
    )


def spatial(boxes, tables):
    left_edge, top_edge = (boxes[..., 0], boxes[..., 1])
    right_edge, bottom_edge = (boxes[..., 2], boxes[..., 3])
    return jnp.concatenate(
        [
            tables[0][left_edge],
            tables[1][top_edge],
            tables[0][right_edge],
            tables[1][bottom_edge],
            tables[2][bottom_edge - top_edge],
            tables[3][right_edge - left_edge],
        ],
        -1,
    )


def coarse(values, step):
    return (values // step, values % step)


def spread(rel_low, lag):
    places = jnp.arange(NB, dtype=jnp.int32)
    half = NB // 2
    index = jnp.clip(places[None, :] - places[:, None] - lag, -half, half - 1) + half
    hot = (index[..., None] == places).astype(jnp.bfloat16)
    table = jnp.einsum(
        "cab,kbh->khca", hot, rel_low.reshape(3, NB, H), preferred_element_type=jnp.float32
    )
    return table.astype(jnp.bfloat16)


def gathered_rel(grad_tables, lag):
    places = jnp.arange(NB, dtype=jnp.int32)
    half = NB // 2
    index = jnp.clip(places[None, :] - places[:, None] - lag, -half, half - 1) + half
    hot = (index[..., None] == places).astype(jnp.float32)
    return jnp.einsum(
        "cab,khca->kbh", hot, grad_tables, precision=lax.Precision.HIGHEST
    ).reshape(3 * NB, H)


def pair_layout(text_box, segments, alive_text, slots):
    full_box = jnp.concatenate([text_box, grid_boxes()], 0)
    positions = jnp.concatenate(
        [jnp.arange(TEXT, dtype=jnp.int32), jnp.arange(GRID * GRID, dtype=jnp.int32)]
    )
    segment_all = jnp.concatenate([segments, jnp.full((GRID * GRID,), -1, jnp.int32)])
    alive = jnp.concatenate([alive_text, jnp.ones((GRID * GRID,), jnp.int32)])
    own_segment = segment_all[slots]
    allowed = (
        (own_segment[:, None] == segment_all[None, :]) | (segment_all[None, :] < 0)
    ) & (alive[None, :] > 0)
    labels = jnp.arange(NB, dtype=jnp.int32)
    hots_key, hots_slot, below = [], [], []
    for values, step in ((positions, 8), (full_box[:, 0], 16), (full_box[:, 3], 16)):
        whole, rest = coarse(values, step)
        hots_key.append((whole[None, :] == labels[:, None]).astype(jnp.bfloat16))
        hots_slot.append((whole[slots][:, None] == labels[None, :]).astype(jnp.bfloat16))
        below.append(rest[None, :] < rest[slots][:, None])
    return allowed, jnp.stack(hots_key), jnp.stack(hots_slot), jnp.stack(below)


def pair_bias(rel_low, hots_key, hots_slot, below):
    sides = []
    for lag in range(2):
        rows = jnp.einsum(
            "kic,khca->khia", hots_slot, spread(rel_low, lag), preferred_element_type=jnp.float32
        ).astype(jnp.bfloat16)
        sides.append(
            jnp.einsum("khia,kaj->khij", rows, hots_key, preferred_element_type=jnp.float32)
        )
    return jnp.sum(jnp.where(below[:, None], sides[1], sides[0]), 0)


def pair_bias_back(grad_scores, hots_key, hots_slot, below):
    total = 0.0
    for lag in range(2):
        chosen = below if lag else ~below
        masked = jnp.where(chosen[:, None], grad_scores[None], jnp.zeros((), grad_scores.dtype))
        rows = jnp.einsum("khij,kaj->khia", masked, hots_key, preferred_element_type=jnp.float32)
        tables = jnp.einsum(
            "khia,kic->khca", rows, hots_slot.astype(jnp.float32), precision=lax.Precision.HIGHEST
        )
        total = total + gathered_rel(tables, lag)
    return total


def gelu_back(pre_piece, grad_active):
    gelu_pullback = jax.vjp(partial(jax.nn.gelu, approximate=False), pre_piece)[1]
    return gelu_pullback(grad_active)[0].astype(jnp.bfloat16)


def adam_step(weight, grad, first, second, rate):
    first = BETA_ONE * first + (1.0 - BETA_ONE) * grad
    second = BETA_TWO * second + (1.0 - BETA_TWO) * grad * grad
    fixed_first = first / (1.0 - BETA_ONE**STEP)
    fixed_second = second / (1.0 - BETA_TWO**STEP)
    weight = weight - rate * (fixed_first / (jnp.sqrt(fixed_second) + EPSILON) + DECAY * weight)
    return (weight, first, second)


def on_device(
    tokens,
    text_box,
    segments,
    alive_text,
    features,
    mask_pos,
    mask_label,
    mask_valid,
    projections,
    projections_first,
    projections_second,
    box_tables,
    box_tables_first,
    box_tables_second,
    position_table,
    position_table_first,
    position_table_second,
    visual_proj,
    visual_proj_first,
    visual_proj_second,
    small_params,
    small_params_first,
    small_params_second,
    word_table,
    word_table_first,
    word_table_second,
    feedforward,
    feedforward_first,
    feedforward_second,
):
    work_proj, work_boxes, work_places, work_visual, work_small, work_table, work_ffn = (
        lax.all_gather(projections.astype(jnp.bfloat16), "dp", axis=1, tiled=True),
        lax.all_gather(box_tables.astype(jnp.bfloat16), "dp", axis=1, tiled=True),
        lax.all_gather(position_table.astype(jnp.bfloat16), "dp", axis=0, tiled=True),
        lax.all_gather(visual_proj.astype(jnp.bfloat16), "dp", axis=0, tiled=True),
        lax.all_gather(small_params.astype(jnp.bfloat16), "dp", axis=1, tiled=True),
        lax.all_gather(word_table.astype(jnp.bfloat16), "dp", axis=0, tiled=True),
        lax.all_gather(feedforward.astype(jnp.bfloat16), "dp", axis=1, tiled=True),
    )
    small_float = work_small.astype(jnp.float32)
    model_index = lax.axis_index("mp")
    vocab_shard = work_table.shape[0]
    hidden_shard = work_ffn.shape[2]
    width = D
    seq_count = text_box.shape[0]
    length = TEXT + GRID * GRID
    row_count = seq_count * length
    rel_low = work_small[10 + FF // D : 13 + FF // D].reshape(3 * NB, H)
    local_ids = tokens - model_index * vocab_shard
    inside = (local_ids >= 0) & (local_ids < vocab_shard)
    safe_index = jnp.clip(local_ids, 0, vocab_shard - 1)
    partial_word = jnp.where(
        inside[..., None], jnp.take(work_table, safe_index, axis=0), jnp.zeros((), jnp.bfloat16)
    )
    word = lax.psum_scatter(partial_word, "mp", scatter_dimension=0, tiled=True).astype(jnp.float32)
    vis_term = jnp.dot(features, work_visual, preferred_element_type=jnp.float32).reshape(
        seq_count, GRID * GRID, width
    )

    def embed_local(word_in, vis_in, places_in, boxes_in):
        text = word_in + places_in + spatial(text_box, boxes_in)
        visual = vis_in + places_in[: GRID * GRID] + spatial(grid_boxes(), boxes_in)[None]
        return jnp.concatenate([text, visual], 1)

    embedded, embed_pullback = jax.vjp(
        embed_local, word, vis_term, work_places.astype(jnp.float32), work_boxes.astype(jnp.float32)
    )
    normed_zero, norm_zero_pullback = jax.vjp(layer_norm, embedded, small_float[0], small_float[1])
    slots = mask_pos
    slot_count = slots.shape[0]
    normed_flat = normed_zero.reshape(row_count, width)
    normed_low = normed_flat.astype(jnp.bfloat16)
    slot_zero = jnp.take(normed_flat, slots, axis=0)
    slot_low = slot_zero.astype(jnp.bfloat16)
    f32 = jnp.float32

    def dot(left, right, dims):
        return lax.dot_general(left, right, (dims, ((), ())), preferred_element_type=f32)

    queries = (dot(slot_low, work_proj[0], ((1,), (0,))) + small_float[2]).astype(jnp.bfloat16)
    keys = dot(normed_low, work_proj[1], ((1,), (0,))).astype(jnp.bfloat16)
    values = (dot(normed_low, work_proj[2], ((1,), (0,))) + small_float[3]).astype(jnp.bfloat16)
    queries = queries.reshape(slot_count, H, HD)
    keys = keys.reshape(length, H, HD)
    values = values.reshape(length, H, HD)
    allowed, hots_key, hots_slot, below = pair_layout(
        text_box[0], segments[0], alive_text[0], slots
    )
    scores = jnp.einsum("qhc,khc->hqk", queries, keys, preferred_element_type=f32) * 0.125
    scores = scores + pair_bias(rel_low, hots_key, hots_slot, below)
    scores = jnp.where(allowed[None], scores, MASKED)
    highest = jnp.max(scores, -1, keepdims=True)
    powers = jnp.exp(scores - highest)
    shares = powers / jnp.sum(powers, -1, keepdims=True)
    shares_low = shares.astype(jnp.bfloat16)
    mixture = jnp.einsum("hqk,khc->qhc", shares_low, values, preferred_element_type=f32)
    mixed_flat = mixture.astype(jnp.bfloat16).reshape(slot_count, width)
    attn_out = dot(mixed_flat, work_proj[3], ((1,), (0,))) + small_float[4]
    summed_one = slot_zero + attn_out
    normed_one, norm_one_pullback = jax.vjp(layer_norm, summed_one, small_float[5], small_float[6])
    normed_one_low = normed_one.astype(jnp.bfloat16)
    ffn_bias_full = small_float[10 : 10 + FF // D].reshape(-1)
    ffn_bias = lax.dynamic_slice_in_dim(ffn_bias_full, model_index * hidden_shard, hidden_shard)
    group_one = lax.all_gather(normed_one_low, "mp", axis=0, tiled=True)
    pre_active = dot(group_one, work_ffn[0], ((1,), (0,))) + ffn_bias
    active_low = jax.nn.gelu(pre_active, approximate=False).astype(jnp.bfloat16)
    ffn_out = (
        lax.psum_scatter(
            dot(active_low, work_ffn[1], ((1,), (1,))), "mp", scatter_dimension=0, tiled=True
        )
        + small_float[7]
    )
    summed_two = normed_one + ffn_out
    normed_two, norm_two_pullback = jax.vjp(layer_norm, summed_two, small_float[8], small_float[9])
    picked = normed_two.astype(jnp.bfloat16)
    group_picked = lax.all_gather(picked, "mp", axis=0, tiled=True)
    logits = dot(group_picked, work_table, ((1,), (1,)))
    local_high = jnp.max(logits, -1)
    local_sum = jnp.sum(jnp.exp(logits - local_high[:, None]), -1)
    label_local = mask_label - model_index * vocab_shard
    label_hit = jnp.arange(vocab_shard)[None, :] == label_local[:, None]
    target_part = jnp.sum(jnp.where(label_hit, logits, 0.0), -1)
    stats = lax.all_gather(jnp.stack([local_high, local_sum, target_part]), "mp")
    high_all = jnp.max(stats[:, 0], 0)
    sum_all = jnp.sum(stats[:, 1] * jnp.exp(stats[:, 0] - high_all), 0)
    target_all = jnp.sum(stats[:, 2], 0)
    log_rows = high_all + jnp.log(sum_all)
    valid_float = mask_valid.astype(f32)
    own_loss = lax.dynamic_slice_in_dim(
        valid_float * (log_rows - target_all), model_index * slot_count, slot_count
    )
    own_valid = lax.dynamic_slice_in_dim(valid_float, model_index * slot_count, slot_count)
    grad_logits = (
        (jnp.exp(logits - log_rows[:, None]) - label_hit.astype(f32)) * valid_float[:, None]
    ).astype(jnp.bfloat16)
    grad_table = dot(grad_logits, group_picked, ((0,), (0,)))
    grad_picked = lax.psum_scatter(
        dot(grad_logits, work_table, ((1,), (0,))), "mp", scatter_dimension=0, tiled=True
    )
    grad_summed_two, grad_gain_two, grad_shift_two = norm_two_pullback(grad_picked)
    grad_ffn_low = grad_summed_two.astype(jnp.bfloat16)
    group_grad = lax.all_gather(grad_ffn_low, "mp", axis=0, tiled=True)
    grad_down = dot(group_grad, active_low, ((0,), (0,)))
    grad_active = dot(group_grad, work_ffn[1], ((1,), (0,)))
    grad_pre = gelu_back(pre_active, grad_active)
    grad_up = dot(group_one, grad_pre, ((0,), (0,)))
    grad_ffn_bias = jnp.sum(grad_pre.astype(f32), 0)
    grad_one = grad_summed_two + lax.psum_scatter(
        dot(grad_pre, work_ffn[0], ((1,), (1,))), "mp", scatter_dimension=0, tiled=True
    )
    grad_ffn = jnp.stack([grad_up, grad_down])
    bias_full = lax.dynamic_update_slice_in_dim(
        jnp.zeros((FF,), f32), grad_ffn_bias, model_index * hidden_shard, 0
    ).reshape(FF // D, width)
    grad_summed_one, grad_gain_one, grad_shift_one = norm_one_pullback(grad_one)
    grad_attn_low = grad_summed_one.astype(jnp.bfloat16)
    grad_out_weight = dot(mixed_flat, grad_attn_low, ((0,), (0,)))
    grad_mixed = dot(grad_attn_low, work_proj[3], ((1,), (1,)))
    grad_mixed = grad_mixed.astype(jnp.bfloat16).reshape(slot_count, H, HD)
    grad_values = jnp.einsum("hqk,qhc->khc", shares_low, grad_mixed, preferred_element_type=f32)
    grad_shares = jnp.einsum("qhc,khc->hqk", grad_mixed, values, preferred_element_type=f32)
    grad_scores = shares * (grad_shares - jnp.sum(shares * grad_shares, -1, keepdims=True))
    scores_low = grad_scores.astype(jnp.bfloat16)
    grad_queries = jnp.einsum("hqk,khc->qhc", scores_low, keys, preferred_element_type=f32) * 0.125
    grad_keys = jnp.einsum("hqk,qhc->khc", scores_low, queries, preferred_element_type=f32) * 0.125
    grad_rel = pair_bias_back(scores_low, hots_key, hots_slot, below)
    grad_queries = grad_queries.astype(jnp.bfloat16).reshape(slot_count, width)
    grad_keys = grad_keys.astype(jnp.bfloat16).reshape(length, width)
    grad_values = grad_values.astype(jnp.bfloat16).reshape(length, width)
    grad_in_weight = jnp.stack(
        [
            dot(slot_low, grad_queries, ((0,), (0,))),
            dot(normed_low, grad_keys, ((0,), (0,))),
            dot(normed_low, grad_values, ((0,), (0,))),
        ]
    )
    grad_slot = grad_summed_one + dot(grad_queries, work_proj[0], ((1,), (1,)))
    grad_zero = (
        dot(grad_keys, work_proj[1], ((1,), (1,))) + dot(grad_values, work_proj[2], ((1,), (1,)))
    )
    grad_zero = grad_zero.at[slots].add(grad_slot)
    grad_embedded, grad_gain_zero, grad_shift_zero = norm_zero_pullback(
        grad_zero.reshape(seq_count, length, width)
    )
    grad_word, grad_vis, grad_places, grad_boxes = embed_pullback(grad_embedded)
    group_word = lax.all_gather(grad_word.astype(jnp.bfloat16), "mp", axis=0, tiled=True)
    grad_table = grad_table + jnp.zeros((vocab_shard, width), f32).at[safe_index].add(
        jnp.where(inside[..., None], group_word.astype(f32), 0.0)
    )
    grad_visual = dot(features, grad_vis.astype(jnp.bfloat16).reshape(-1, width), ((0,), (0,)))
    grad_small = jnp.concatenate(
        [
            jnp.stack(
                [
                    grad_gain_zero,
                    grad_shift_zero,
                    jnp.sum(grad_queries.astype(f32), 0),
                    jnp.sum(grad_values.astype(f32), 0),
                    jnp.sum(grad_attn_low.astype(jnp.float32), 0),
                    grad_gain_one,
                    grad_shift_one,
                    jnp.sum(grad_ffn_low.astype(jnp.float32), 0),
                    grad_gain_two,
                    grad_shift_two,
                ]
            ),
            bias_full,
            grad_rel.reshape(3, width),
        ],
        0,
    )
    grad_attn = jnp.concatenate([grad_in_weight, grad_out_weight[None]], 0)
    def scattered(part, axis):
        low_part = part.astype(jnp.bfloat16)
        return lax.psum_scatter(low_part, "dp", scatter_dimension=axis, tiled=True).astype(f32)

    shared_parts = (
        scattered(grad_attn, 1),
        scattered(grad_boxes, 1),
        scattered(grad_places, 0),
        scattered(grad_visual, 0),
        lax.psum_scatter(grad_small, "dp", scatter_dimension=1, tiled=True),
    )
    reduced_proj, reduced_boxes, reduced_places, reduced_visual, reduced_small = lax.psum(
        shared_parts, "mp"
    )
    reduced_table, reduced_ffn = (scattered(grad_table, 0), scattered(grad_ffn, 1))
    reduced = (
        reduced_proj,
        reduced_boxes,
        reduced_places,
        reduced_visual,
        reduced_small,
        reduced_table,
        reduced_ffn,
    )
    shared_squares = jnp.zeros((), jnp.float32)
    for part in reduced[:5]:
        shared_squares = shared_squares + jnp.sum(part * part)
    split_squares = jnp.sum(reduced_table * reduced_table) + jnp.sum(reduced_ffn * reduced_ffn)
    squares = split_squares + jnp.where(model_index == 0, shared_squares, 0.0)
    total_squares, loss_sum, loss_count = lax.psum(
        (squares, jnp.sum(own_loss), jnp.sum(own_valid)), ("dp", "mp")
    )
    grad_norm = jnp.sqrt(total_squares) / loss_count
    factor = jnp.minimum(1.0, CLIP / grad_norm)
    masters = (
        projections,
        box_tables,
        position_table,
        visual_proj,
        small_params,
        word_table,
        feedforward,
    )
    firsts = (
        projections_first,
        box_tables_first,
        position_table_first,
        visual_proj_first,
        small_params_first,
        word_table_first,
        feedforward_first,
    )
    seconds = (
        projections_second,
        box_tables_second,
        position_table_second,
        visual_proj_second,
        small_params_second,
        word_table_second,
        feedforward_second,
    )
    outputs = []
    for index in range(7):
        outputs.extend(
            adam_step(
                masters[index],
                reduced[index] / loss_count * factor,
                firsts[index],
                seconds[index],
                RATES[index],
            )
        )
    return tuple(outputs) + (loss_sum, loss_count, grad_norm)


def solution(mesh):
    in_specs = (
        P("dp", None),
        P(("dp", "mp"), None, None),
        P(("dp", "mp"), None),
        P(("dp", "mp"), None),
        P(("dp", "mp"), None),
        P(("dp", "mp")),
        P("dp"),
        P("dp"),
        P(None, "dp", None),
        P(None, "dp", None),
        P(None, "dp", None),
        P(None, "dp", None),
        P(None, "dp", None),
        P(None, "dp", None),
        P("dp", None),
        P("dp", None),
        P("dp", None),
        P("dp", None),
        P("dp", None),
        P("dp", None),
        P(None, "dp"),
        P(None, "dp"),
        P(None, "dp"),
        P(("mp", "dp"), None),
        P(("mp", "dp"), None),
        P(("mp", "dp"), None),
        P(None, "dp", "mp"),
        P(None, "dp", "mp"),
        P(None, "dp", "mp"),
    )
    out_specs = (
        P(None, "dp", None),
        P(None, "dp", None),
        P(None, "dp", None),
        P(None, "dp", None),
        P(None, "dp", None),
        P(None, "dp", None),
        P("dp", None),
        P("dp", None),
        P("dp", None),
        P("dp", None),
        P("dp", None),
        P("dp", None),
        P(None, "dp"),
        P(None, "dp"),
        P(None, "dp"),
        P(("mp", "dp"), None),
        P(("mp", "dp"), None),
        P(("mp", "dp"), None),
        P(None, "dp", "mp"),
        P(None, "dp", "mp"),
        P(None, "dp", "mp"),
        P(),
        P(),
        P(),
    )
    return jax.shard_map(
        on_device, mesh=mesh, in_specs=in_specs, out_specs=out_specs, check_vma=False
    )
```

time: 1670 us -> 873 us (0.52)
  waiting for transfers between devices: 606 us -> 347 us
  blocking collectives: 368 us -> 195 us
  matrix products: 265 us -> 96.4 us
  local copies, waits for them, and re-layouts: 219 us -> 65.4 us
  other arithmetic: 169 us -> 138 us
    unnamed x3 -> x0, blocking collectives: 265 us -> none
    dot_general x28 -> x38, matrix products: 264 us -> 95.3 us  [the longest x22 51.8 us: dot(): lax.dot_general(left, right, (dims, ((), ())), preferred_element_type=f32)]
    all_gather x2 -> x0, waiting for transfers between devices: 132 us -> none  [the longest x1 67.9 us: on_device(): piece = lax.all_gather(grad_ffn_low, 'mp', axis=0, tiled=True)]
    dot_general x3 -> x0, local copies, waits for them, and re-layouts: 79.5 us -> none  [scores_of(): jnp.einsum('vti,vn->nti', kind_onehot(buckets, kind), rel_low[kind * NB:(...]
    psum x1 -> x0, waiting for transfers between devices: 58.3 us -> none  [on_device(): lax.psum((shared_parts[0], shared_parts[1], shared_parts[2], shared_parts...]
    psum x1, blocking collectives: 19.2 us -> 67.2 us  [on_device(): lax.psum(shared_parts, 'mp')]
    all_gather x0 -> x3, blocking collectives: none -> 44.6 us  [the longest x1 15.6 us: on_device(): group_grad = lax.all_gather(grad_ffn_low, 'mp', axis=0, tiled=True)]
    all_gather x1, waiting for transfers between devices: 41.5 us -> 0.01 us  [on_device(): lax.all_gather(grad_word.astype(jnp.bfloat16), 'mp', axis=0, tiled=True)]
  transfers between devices with their start and end apart: 19 -> 16, of which waited for: 15 -> 10; matrix products, arithmetic and copies ran while one was open for 23% -> 25% of each run, Pallas kernels for 0% -> 0%
where the time goes in v1:
time: 873 us; the launch traced here: 867 us
  waiting for transfers between devices  347 us (40%)
  blocking collectives  195 us (22%)
  other arithmetic  138 us (16%)
  matrix products  96.4 us (11%)
  local copies, waits for them, and re-layouts  65.4 us (7%)
  between operations  24.8 us (3%)
    reduce_scatter x6, waiting for transfers between devices, scattered(): lax.psum_scatter(low_part, 'dp', scatter_dimension=axis, tiled=True)  203 us
    psum x1, blocking collectives, on_device(): lax.psum(shared_parts, 'mp')  67.2 us
    dot_general x22, matrix products, dot(): lax.dot_general(left, right, (dims, ((), ())), preferred_element_type=f32)  51.8 us
    all_gather x1, waiting for transfers between devices, on_device(): lax.all_gather(word_table.astype(jnp.bfloat16), 'dp', axis=0, tiled=True)  46.6 us
    psum x1, blocking collectives, on_device(): lax.psum((squares, jnp.sum(own_loss), jnp.sum(own_valid)), ('dp', 'mp'))  38.5 us
    reduce_scatter x1, waiting for transfers between devices, on_device(): lax.psum_scatter(dot(grad_pre, work_ffn[0], ((1,), (1,))), 'mp', scatter_...  24.6 us
    all_gather x1, waiting for transfers between devices, on_device(): lax.all_gather(projections.astype(jnp.bfloat16), 'dp', axis=1, tiled=True)  24.5 us
    reduce_scatter x1, waiting for transfers between devices, on_device(): lax.psum_scatter(dot(grad_logits, work_table, ((1,), (0,))), 'mp', scatte...  24.5 us
  transfers between devices with their start and end apart: 16, of which 10 were waited for; matrix products, arithmetic and copies ran while one was open for 25% of the time, Pallas kernels for 0%

profile of v1, /device:TPU:0, one launch (start us, length us, event | category | flops | bytes accessed | tf_op | source)
XLA Modules:
  0.0 867.1 jit_solution(11243610466058071493)
XLA Ops:
  10.6 46.6 %all-gather.9.cloned.1.call-done = bf16[3840,768]{1,0:T(8,128)(2,1)} async-done(((bf16[480,768]{1,0:T(8,128)(2,1)}), bf16[3840,768]{1,0:T(8,128)(2,1)}) %all-gather.9.cloned.1.call-update) | async-done | bytes 5898256 | tf_op jit(solution)/shard_map/all_gather | solution.py:187
  57.1 13.6 %gather_fusion = bf16[2048,768]{1,0:T(8,128)(2,1)} fusion(bf16[3840,768]{1,0:T(8,128)(2,1)} %all-gather.9.cloned.1.call-done, s32[2048]{0:T(1024)S(1)} %broadcast_clamp_fusion), kind=kCustom, calls=%fused_computation | custom fusion | bytes 6299648 | tf_op jit(solution)/shard_map/jit(_take)/gather | solution.py:203
  70.7 3.4 select_select_fusion
  81.4 9.1 %all-gather.1 = bf16[8,96,17]{1,2,0:T(8,128)(2,1)S(1)} all-gather(bf16[1,96,17]{1,2,0:T(8,128)(2,1)S(1)} %convert_bitcast_fusion), channel_id=1, replica_groups=mesh['dp'=8,'mp'=4] {'dp'}, dimensions={0}, use_global_device_ids=true | all-gather | bytes 29376 | tf_op jit(solution)/shard_map/all_gather | solution.py:186
  91.5 9.6 %all_gather.40 = bf16[512,768]{1,0:T(8,128)(2,1)S(1)} all-gather(bf16[64,768]{1,0:T(8,128)(2,1)S(1)} %convert_element_type.253), channel_id=1, replica_groups=mesh['dp'=8,'mp'=4] {'dp'}, dimensions={0}, use_global_device_ids=true | all-gather | bytes 884736 | tf_op jit(solution)/shard_map/all_gather | solution.py:184
  104.2 10.1 %all_gather.42 = bf16[256,768]{1,0:T(8,128)(2,1)S(1)} all-gather(bf16[32,768]{1,0:T(8,128)(2,1)S(1)} %convert_element_type.257), channel_id=1, replica_groups=mesh['dp'=8,'mp'=4] {'dp'}, dimensions={0}, use_global_device_ids=true | all-gather | bytes 442368 | tf_op jit(solution)/shard_map/all_gather | solution.py:185
  123.9 5.5 fusion.48
  129.5 6.1 select_reduce_fusion
  162.5 24.5 %all-gather.13.cloned.1.call-done = bf16[4,768,768]{2,1,0:T(8,128)(2,1)} async-done(((bf16[4,96,768]{2,1,0:T(8,128)(2,1)}), bf16[4,768,768]{2,1,0:T(8,128)(2,1)}) %all-gather.13.cloned.1.call-update) | async-done | bytes 4718608 | tf_op jit(solution)/shard_map/all_gather | solution.py:182
  189.8 2.8 gather_fusion.13
  194.6 3.4 add_convert_fusion.1
  205.0 4.3 convolution_convert_fusion.11
  212.0 15.6 %all_gather.45 = bf16[320,768]{1,0:T(8,128)(2,1)S(1)} all-gather(bf16[80,768]{1,0:T(8,128)(2,1)S(1)} %fusion.116), channel_id=1, replica_groups=mesh['dp'=8,'mp'=4] {'mp'}, dimensions={0}, use_global_device_ids=true | all-gather | bytes 614400 | tf_op jit(solution)/shard_map/all_gather | solution.py:254
  227.6 5.2 multiply_convert_fusion.3
  237.1 24.1 %reduce-scatter.18.cloned.1.call-done = f32[80,768]{1,0:T(8,128)} async-done(((f32[320,768]{1,0:T(8,128)}), f32[80,768]{1,0:T(8,128)}) %reduce-scatter.18.cloned.1.call-update) | async-done | bytes 245776 | tf_op jit(solution)/shard_map/reduce_scatter | solution.py:258
  264.0 15.7 %all_gather.47 = bf16[320,768]{1,0:T(8,128)(2,1)S(1)} all-gather(bf16[80,768]{1,0:T(8,128)(2,1)S(1)} %add_convert_fusion.3), channel_id=1, replica_groups=mesh['dp'=8,'mp'=4] {'mp'}, dimensions={0}, use_global_device_ids=true | all-gather | bytes 614400 | tf_op jit(solution)/shard_map/all_gather | solution.py:266
  279.7 5.1 fusion.175
  286.2 13.3 %all-gather.2 = f32[4,3,320]{2,1,0:T(4,128)S(1)} all-gather(f32[1,3,320]{2,1,0:T(4,128)S(1)} %maximum_bitcast_fusion), channel_id=2, replica_groups=mesh['dp'=8,'mp'=4] {'mp'}, dimensions={0}, use_global_device_ids=true | all-gather | bytes 19200 | tf_op jit(solution)/shard_map/all_gather | solution.py:273
  300.8 3.9 fusion.157
  304.8 24.5 %reduce-scatter.20.cloned.1.call-done = f32[80,768]{1,0:T(8,128)} async-done(((f32[320,768]{1,0:T(8,128)}), f32[80,768]{1,0:T(8,128)}) %reduce-scatter.20.cloned.1.call-update) | async-done | bytes 245776 | tf_op jit(solution)/shard_map/reduce_scatter | solution.py:287
  333.7 15.6 %all_gather.50 = bf16[320,768]{1,0:T(8,128)(2,1)S(1)} all-gather(bf16[80,768]{1,0:T(8,128)(2,1)S(1)} %get-tuple-element.156), channel_id=1, replica_groups=mesh['dp'=8,'mp'=4] {'mp'}, dimensions={0}, use_global_device_ids=true | all-gather | bytes 614400 | tf_op jit(solution)/shard_map/all_gather | solution.py:292
  349.4 3.4 convert_reduce_fusion.1
  354.4 24.6 %reduce-scatter.22.cloned.1.call-done = f32[80,768]{1,0:T(8,128)} async-done(((f32[320,768]{1,0:T(8,128)}), f32[80,768]{1,0:T(8,128)}) %reduce-scatter.22.cloned.1.call-update) | async-done | bytes 245776 | tf_op jit(solution)/shard_map/reduce_scatter | solution.py:298
  383.7 6.0 convert_reduce_fusion
  408.5 2.8 convolution_bitcast_fusion.1
  415.4 2.8 convolution_bitcast_fusion
  435.8 3.2 scatter_custom_fusion.8
  439.0 3.2 scatter_custom_fusion.9
  442.2 3.2 scatter_custom_fusion.10
  445.3 3.2 scatter_custom_fusion.11
  448.5 3.3 scatter_custom_fusion.12
  451.8 3.2 scatter_custom_fusion.13
  455.0 3.3 add_convert_fusion
  470.9 10.6 %fusion.156 = f32[3840,768]{1,0:T(8,128)} fusion(bf16[320,768]{1,0:T(8,128)(2,1)S(1)} %copy-done.25, f32[320,3840]{1,0:T(8,128)} %copy-done.2, f32[320]{0:T(512)S(1)} %copy-done.109, f32[320]{0:T(512)S(1)} %copy-done.113, s32[320]{0:T(512)S(1)} %copy-done.107), kind=kOutput, calls=%fused_computation.431 | convolution fusion | flops 1894809600 | bytes 17207040 | tf_op jit(solution)/shard_map/dot_general | solution.py:228
  481.6 4.5 convert_select_fusion
  486.0 23.3 %scatter_fusion.1 = f32[3840,768]{1,0:T(8,128)} fusion(f32[3840,768]{1,0:T(8,128)} %fusion.156, s32[2048]{0:T(1024)S(1)} %bitcast.353, f32[2048,768]{1,0:T(8,128)} %bitcast.316), kind=kCustom, calls=%fused_computation.22 | custom fusion | flops 1572864 | bytes 18882560 | tf_op jit(solution)/shard_map/scatter-add | solution.py:337
  509.3 7.5 convert_element_type.298
  519.0 22.1 %reduce-scatter.34.cloned.1.call-done = bf16[32,768]{1,0:T(8,128)(2,1)} async-done(((bf16[256,768]{1,0:T(8,128)(2,1)}), bf16[32,768]{1,0:T(8,128)(2,1)}) %reduce-scatter.34.cloned.1.call-update) | async-done | bytes 49168 | tf_op jit(solution)/shard_map/reduce_scatter | solution.py:365
  541.1 38.9 %reduce-scatter.32.cloned.1.call-done = bf16[64,768]{1,0:T(8,128)(2,1)} async-done(((bf16[512,768]{1,0:T(8,128)(2,1)}), bf16[64,768]{1,0:T(8,128)(2,1)}) %reduce-scatter.32.cloned.1.call-update) | async-done | bytes 98320 | tf_op jit(solution)/shard_map/reduce_scatter | solution.py:365
  580.0 40.1 %reduce-scatter.30.cloned.1.call-done = bf16[4,128,128]{2,1,0:T(8,128)(2,1)} async-done(((bf16[4,1024,128]{2,1,0:T(8,128)(2,1)}), bf16[4,128,128]{2,1,0:T(8,128)(2,1)}) %reduce-scatter.30.cloned.1.call-update) | async-done | bytes 131088 | tf_op jit(solution)/shard_map/reduce_scatter | solution.py:365
  620.2 46.1 %reduce-scatter.28.cloned.1.call-done = bf16[2,96,768]{2,1,0:T(8,128)(2,1)} async-done(((bf16[2,768,768]{2,1,0:T(8,128)(2,1)}), bf16[2,96,768]{2,1,0:T(8,128)(2,1)}) %reduce-scatter.28.cloned.1.call-update) | async-done | bytes 294928 | tf_op jit(solution)/shard_map/reduce_scatter | solution.py:365
  668.0 55.4 %reduce-scatter.24.cloned.1.call-done = bf16[4,96,768]{2,1,0:T(8,128)(2,1)} async-done(((bf16[4,768,768]{2,1,0:T(8,128)(2,1)}), bf16[4,96,768]{2,1,0:T(8,128)(2,1)}) %reduce-scatter.24.cloned.1.call-update) | async-done | bytes 589840 | tf_op jit(solution)/shard_map/reduce_scatter | solution.py:365
  723.5 67.2 %all-reduce.18 = (f32[4,96,768]{2,1,0:T(8,128)S(1)}, f32[4,128,128]{2,1,0:T(8,128)S(1)}, f32[64,768]{1,0:T(8,128)S(1)}, f32[32,768]{1,0:T(8,128)S(1)}, f32[17,96]{1,0:T(8,128)S(1)}) all-reduce(bf16[4,96,768]{2,1,0:T(8,128)(2,1)} %reduce-scatter.24.cloned.1.call-done, ...), channel_id=1, replica_groups=mesh['dp'=8,'mp'=4] {'mp'}, use_global_device_ids=true, to_apply=%region_24.25 | all-reduce | flops 435808 | bytes 2618112 | tf_op jit(solution)/shard_map/psum | solution.py:374
  800.9 38.5 %all-reduce.15 = (f32[]{:T(128)}, f32[]{:T(128)}, f32[]{:T(128)}) all-reduce(f32[]{:T(128)} %get-tuple-element.208, f32[]{:T(128)S(6)} %add.852, f32[]{:T(128)} %get-tuple-element.207), channel_id=1, replica_groups=mesh['dp'=8,'mp'=4] {'dp','mp'}, use_global_device_ids=true, to_apply=%region_26.27 | all-reduce | flops 3 | bytes 24 | tf_op jit(solution)/shard_map/psum | solution.py:392
  844.2 2.7 multiply_subtract_fusion.4
  847.0 2.7 multiply_subtract_fusion.3
  849.7 3.2 multiply_subtract_fusion.1
  855.3 3.6 multiply_subtract_fusion
  (585 shorter events, 151.7 us)
Async XLA Ops:
  7.2 150.1 %copy-start = (bf16[49,256]{1,0:T(8,128)(2,1)S(1)}, bf16[49,256]{1,0:T(8,128)(2,1)}, u32[]{:S(2)}) copy-start(bf16[49,256]{1,0:T(8,128)(2,1)} %param.33) | copy-start | bytes 75268
  7.2 49.9 %all-gather.9.cloned.1.call-start = ((), (), s32[]{:S(2)}) async-start(), calls=%async_computation.11 | async-start | bytes 6635520 | tf_op jit(solution)/shard_map/all_gather | solution.py:187
  9.6 126.7 %all-gather.11.cloned.1.call-start = ((), (), s32[]{:S(2)}) async-start(), calls=%async_computation.13 | async-start | bytes 1179648 | tf_op jit(solution)/shard_map/all_gather | solution.py:183
  10.4 148.1 %reduce-scatter.16.cloned.1.call-start = ((), (), s32[]{:S(2)}) async-start(), calls=%async_computation.12 | async-start | bytes 3932160 | tf_op jit(solution)/shard_map/reduce_scatter | solution.py:205
  10.5 60.2 %copy-start.93 = (s32[1,4,4,128]{3,1,2,0:T(4,128)}, s32[1,4,4,128]{3,1,2,0:T(4,128)S(1)}, u32[]{:S(2)}) copy-start(s32[1,4,4,128]{3,1,2,0:T(4,128)S(1)} %copy.134) | copy-start | bytes 24580
  10.5 60.2 %copy-start.110 = (pred[4,512]{1,0:T(4,128)(4,1)}, pred[4,512]{1,0:T(4,128)(4,1)S(1)}, u32[]{:S(2)}) copy-start(pred[4,512]{1,0:T(4,128)(4,1)S(1)} %get-tuple-element.178) | copy-start | bytes 6148
  74.1 112.9 %all-gather.13.cloned.1.call-start = ((), (), s32[]{:S(2)}) async-start(), calls=%async_computation.14 | async-start | bytes 5308416 | tf_op jit(solution)/shard_map/all_gather | solution.py:182
  76.3 151.4 %all-gather.15.cloned.1.call-start = ((), (), s32[]{:S(2)}) async-start(), calls=%async_computation.15 | async-start | bytes 2654208 | tf_op jit(solution)/shard_map/all_gather | solution.py:188
  77.1 184.1 %reduce-scatter.18.cloned.1.call-start = ((), (), s32[]{:S(2)}) async-start(), calls=%async_computation.16 | async-start | bytes 1228800 | tf_op jit(solution)/shard_map/reduce_scatter | solution.py:258
  77.2 23.9 %copy-start.152 = (s32[49]{0:T(128)}, s32[49]{0:T(128)S(1)}, u32[]{:S(2)}) copy-start(s32[49]{0:T(128)S(1)} %fusion.145) | copy-start | bytes 592
  77.2 23.9 %copy-start.153 = (s32[49]{0:T(128)}, s32[49]{0:T(128)S(1)}, u32[]{:S(2)}) copy-start(s32[49]{0:T(128)S(1)} %fusion.146) | copy-start | bytes 592
  77.2 23.9 %copy-start.154 = (s32[49]{0:T(128)}, s32[49]{0:T(128)S(1)}, u32[]{:S(2)}) copy-start(s32[49]{0:T(128)S(1)} %fusion.147) | copy-start | bytes 592
  77.3 24.5 %copy-start.155 = (s32[49]{0:T(128)}, s32[49]{0:T(128)S(1)}, u32[]{:S(2)}) copy-start(s32[49]{0:T(128)S(1)} %fusion.148) | copy-start | bytes 592
  77.3 25.0 %copy-start.156 = (s32[49]{0:T(128)}, s32[49]{0:T(128)S(1)}, u32[]{:S(2)}) copy-start(s32[49]{0:T(128)S(1)} %fusion.149) | copy-start | bytes 592
  77.4 25.6 %copy-start.157 = (s32[49]{0:T(128)}, s32[49]{0:T(128)S(1)}, u32[]{:S(2)}) copy-start(s32[49]{0:T(128)S(1)} %fusion.150) | copy-start | bytes 592
  78.1 43.3 %copy-start.121 = (s32[1024]{0:T(1024)}, s32[1024]{0:T(1024)S(1)}, u32[]{:S(2)}) copy-start(s32[1024]{0:T(1024)S(1)} %pad_clamp_fusion) | copy-start | bytes 12292
  78.2 51.2 %copy-start.67 = (pred[1,64,561]{2,1,0:T(32,128)(4,1)}, pred[1,64,561]{2,1,0:T(32,128)(4,1)S(1)}, u32[]{:S(2)}) copy-start(pred[1,64,561]{2,1,0:T(32,128)(4,1)S(1)} %iota_compare_fusion.3) | copy-start | bytes 107716
  80.3 49.2 %copy-start.69 = (pred[1,64,561]{2,1,0:T(32,128)(4,1)}, pred[1,64,561]{2,1,0:T(32,128)(4,1)S(1)}, u32[]{:S(2)}) copy-start(pred[1,64,561]{2,1,0:T(32,128)(4,1)S(1)} %iota_compare_fusion.4) | copy-start | bytes 107716
  81.3 48.1 %copy-start.71 = (pred[1,64,561]{2,1,0:T(32,128)(4,1)}, pred[1,64,561]{2,1,0:T(32,128)(4,1)S(1)}, u32[]{:S(2)}) copy-start(pred[1,64,561]{2,1,0:T(32,128)(4,1)S(1)} %iota_compare_fusion.5) | copy-start | bytes 107716
  81.4 36.5 %copy-start.73 = (s32[64,64]{0,1:T(8,128)}, s32[64,64]{0,1:T(8,128)S(1)}, u32[]{:S(2)}) copy-start(s32[64,64]{0,1:T(8,128)S(1)} %clamp_add_fusion.1) | copy-start | bytes 49156
  81.4 38.6 %copy-start.75 = (s32[64,64]{0,1:T(8,128)}, s32[64,64]{0,1:T(8,128)S(1)}, u32[]{:S(2)}) copy-start(s32[64,64]{0,1:T(8,128)S(1)} %clamp_add_fusion) | copy-start | bytes 49156
  91.3 69.6 %copy-start.89 = (f32[768]{0:T(1024)}, f32[768]{0:T(1024)S(1)}, u32[]{:S(2)}) copy-start(f32[768]{0:T(1024)S(1)} %get-tuple-element.117) | copy-start | bytes 9220
  162.5 24.5 %copy-start.46 = (bf16[561,768]{1,0:T(8,128)(2,1)}, bf16[561,768]{1,0:T(8,128)(2,1)S(1)}, u32[]{:S(2)}) copy-start(bf16[561,768]{1,0:T(8,128)(2,1)S(1)} %get-tuple-element.168) | copy-start | bytes 2585092
  209.3 23.5 %copy-start.50 = (bf16[12,64,80]{2,1,0:T(8,128)(2,1)}, bf16[12,64,80]{2,1,0:T(8,128)(2,1)S(1)}, u32[]{:S(2)}) copy-start(bf16[12,64,80]{2,1,0:T(8,128)(2,1)S(1)} %convolution_convert_fusion.11) | copy-start | bytes 368644
  234.4 66.4 %slice-start = ((s8[5898240]{0:T(1024)(128)(4,1)}), s8[1703936]{0:T(1024)(128)(4,1)S(1)}, s32[]{:S(2)}) async-start(s8[5898240]{0:T(1024)(128)(4,1)} %bitcast.310), calls=%async_computation.27 | async-start | bytes 3407872
  234.4 94.9 %reduce-scatter.20.cloned.1.call-start = ((), (), s32[]{:S(2)}) async-start(), calls=%async_computation.17 | async-start | bytes 1228800 | tf_op jit(solution)/shard_map/reduce_scatter | solution.py:287
  304.7 74.3 %reduce-scatter.22.cloned.1.call-start = ((), (), s32[]{:S(2)}) async-start(), calls=%async_computation.18 | async-start | bytes 1228800 | tf_op jit(solution)/shard_map/reduce_scatter | solution.py:298
  352.8 26.2 %copy-start.88 = (f32[768]{0:T(1024)S(1)}, f32[768]{0:T(1024)}, u32[]{:S(2)}) copy-start(f32[768]{0:T(1024)} %get-tuple-element.112) | copy-start | bytes 9220
  352.8 26.2 %copy-start.123 = (f32[80]{0:T(128)S(1)}, f32[80]{0:T(128)}, u32[]{:S(2)}) copy-start(f32[80]{0:T(128)} %copy-done.122) | copy-start | bytes 964
  352.8 26.2 %copy-start.136 = (f32[80]{0:T(128)S(1)}, f32[80]{0:T(128)}, u32[]{:S(2)}) copy-start(f32[80]{0:T(128)} %copy-done.135) | copy-start | bytes 964
  352.8 27.9 %copy-start.150 = (f32[80]{0:T(128)S(1)}, f32[80]{0:T(128)}, u32[]{:S(2)}) copy-start(f32[80]{0:T(128)} %copy-done.149) | copy-start | bytes 964
  354.4 29.3 %copy-start.103 = (f32[12,80]{1,0:T(8,128)S(1)}, f32[12,80]{1,0:T(8,128)}, u32[]{:S(2)}) copy-start(f32[12,80]{1,0:T(8,128)} %copy-done.102) | copy-start | bytes 11524
  354.4 127.2 %all-gather.17.cloned.1.call-start = ((), (), s32[]{:S(2)}) async-start(), calls=%async_computation.20 | async-start | bytes 3932160 | tf_op jit(solution)/shard_map/all_gather | solution.py:336
  405.9 112.2 %reduce-scatter.36.cloned.1.call-start = ((), (), s32[]{:S(2)}) async-start(), calls=%async_computation.26 | async-start | bytes 442368
  424.6 116.5 %reduce-scatter.34.cloned.1.call-start = ((), (), s32[]{:S(2)}) async-start(), calls=%async_computation.25 | async-start | bytes 442368 | tf_op jit(solution)/shard_map/reduce_scatter | solution.py:365
  425.9 154.1 %reduce-scatter.32.cloned.1.call-start = ((), (), s32[]{:S(2)}) async-start(), calls=%async_computation.24 | async-start | bytes 884736 | tf_op jit(solution)/shard_map/reduce_scatter | solution.py:365
  427.0 193.2 %reduce-scatter.30.cloned.1.call-start = ((), (), s32[]{:S(2)}) async-start(), calls=%async_computation.23 | async-start | bytes 1179648 | tf_op jit(solution)/shard_map/reduce_scatter | solution.py:365
  458.3 207.9 %reduce-scatter.28.cloned.1.call-start = ((), (), s32[]{:S(2)}) async-start(), calls=%async_computation.22 | async-start | bytes 2654208 | tf_op jit(solution)/shard_map/reduce_scatter | solution.py:365
  462.8 260.6 %reduce-scatter.24.cloned.1.call-start = ((), (), s32[]{:S(2)}) async-start(), calls=%async_computation.19 | async-start | bytes 5308416 | tf_op jit(solution)/shard_map/reduce_scatter | solution.py:365
  469.9 327.5 %reduce-scatter.26.cloned.1.call-start = ((), (), s32[]{:S(2)}) async-start(), calls=%async_computation.21 | async-start | bytes 6635520 | tf_op jit(solution)/shard_map/reduce_scatter | solution.py:365
  668.0 173.4 %copy-start.98 = (f32[17,96]{1,0:T(8,128)S(1)}, f32[17,96]{1,0:T(8,128)}, u32[]{:S(2)}) copy-start(f32[17,96]{1,0:T(8,128)} %param.49) | copy-start | bytes 19588
  668.0 173.4 %copy-start.124 = (f32[17,96]{1,0:T(8,128)S(1)}, f32[17,96]{1,0:T(8,128)}, u32[]{:S(2)}) copy-start(f32[17,96]{1,0:T(8,128)} %param.50) | copy-start | bytes 19588
  668.0 173.4 %copy-start.125 = (f32[17,96]{1,0:T(8,128)S(1)}, f32[17,96]{1,0:T(8,128)}, u32[]{:S(2)}) copy-start(f32[17,96]{1,0:T(8,128)} %param.51) | copy-start | bytes 19588
  668.0 174.7 %copy-start.66 = (f32[32,768]{1,0:T(8,128)S(1)}, f32[32,768]{1,0:T(8,128)}, u32[]{:S(2)}) copy-start(f32[32,768]{1,0:T(8,128)} %param.46) | copy-start | bytes 294916
  668.0 174.7 %copy-start.91 = (f32[32,768]{1,0:T(8,128)S(1)}, f32[32,768]{1,0:T(8,128)}, u32[]{:S(2)}) copy-start(f32[32,768]{1,0:T(8,128)} %param.47) | copy-start | bytes 294916
  668.0 174.7 %copy-start.92 = (f32[32,768]{1,0:T(8,128)S(1)}, f32[32,768]{1,0:T(8,128)}, u32[]{:S(2)}) copy-start(f32[32,768]{1,0:T(8,128)} %param.48) | copy-start | bytes 294916
  790.7 53.5 %copy-start.49 = (f32[64,768]{1,0:T(8,128)S(1)}, f32[64,768]{1,0:T(8,128)}, u32[]{:S(2)}) copy-start(f32[64,768]{1,0:T(8,128)} %param.43) | copy-start | bytes 589828
  792.2 54.7 %copy-start.36 = (f32[4,128,128]{2,1,0:T(8,128)S(1)}, f32[4,128,128]{2,1,0:T(8,128)}, u32[]{:S(2)}) copy-start(f32[4,128,128]{2,1,0:T(8,128)} %param.40) | copy-start | bytes 786436
  (131 other events, 647.9 us)
Sparse Core Ops, SparseCore 0:
  10.5 46.5 all-gather.8
  59.6 23.4 all-gather.10
  85.4 60.2 reduce-scatter.15
  148.1 38.9 all-gather.12
  189.4 29.0 all-gather.14
  234.5 26.6 reduce-scatter.17
  304.9 24.3 reduce-scatter.19
  354.5 24.4 reduce-scatter.21
  406.0 62.0 all-gather.16
  471.4 32.4 reduce-scatter.35
  507.3 33.8 reduce-scatter.33
  545.0 34.9 reduce-scatter.31
  584.1 36.0 reduce-scatter.29
  623.7 42.4 reduce-scatter.27
  669.5 53.8 reduce-scatter.23
  727.2 59.6 reduce-scatter.25

commit v2 on v1

--- a/solution.py
+++ b/solution.py
@@ -3,6 +3,8 @@
 import jax
 import jax.numpy as jnp
 from jax import lax
+from jax.experimental import pallas as pl
+from jax.experimental.pallas import tpu as pltpu
 from jax.sharding import PartitionSpec as P
 
 D = 768
@@ -13,6 +15,9 @@
 GRID = 7
 TEXT = 512
 STEP = 10
+VCH = 256
+NBOX = 1024
+VROWS = 17
 
 
 MASKED = -1e30
@@ -145,6 +150,400 @@
     fixed_second = second / (1.0 - BETA_TWO**STEP)
     weight = weight - rate * (fixed_first / (jnp.sqrt(fixed_second) + EPSILON) + DECAY * weight)
     return (weight, first, second)
+
+
+MESH = pl.DeviceIdType.MESH
+LOW = jnp.bfloat16
+WIDE = jnp.float32
+LANES = 128
+HALF = D // 2
+
+
+def pad_up(count, unit):
+    return (count + unit - 1) // unit * unit
+
+
+def bits_of(count):
+    return count.bit_length() - 1
+
+
+def flip(index, bit, ring):
+    if ring and bit == 1:
+        return 3 - index
+    return index + (1 - 2 * ((index // 2**bit) % 2)) * 2**bit
+
+
+class Plan:
+    def __init__(self, dp, mp):
+        self.dp, self.mp = dp, mp
+        self.proj = pad_up(D // dp, 16)
+        self.places = pad_up(TEXT // dp, 16)
+        self.visual = pad_up(VCH // dp, 16)
+        self.box = NBOX // dp
+        self.box_parts = 4 * (self.box // 32)
+        self.places_at = 4 * self.proj
+        self.visual_at = self.places_at + self.places
+        self.box_at = self.visual_at + self.visual
+        self.box_rows = 32 * ((self.box_parts + 6) // 6)
+        self.shared = pad_up(self.box_at + self.box_rows, 32)
+
+    def box_slot(self, part):
+        return self.box_at + 32 * (part // 6), LANES * (part % 6)
+
+
+def lanes_of(stream):
+    return pl.ds(stream * HALF, HALF)
+
+
+def ffn_slot(part, table_rows, ffn_rows, wide):
+    return table_rows + part * wide // D * ffn_rows, part * wide % D
+
+
+def row_tile(rows):
+    return next(t for t in (48, 32, 16) if rows % t == 0)
+
+
+def reduce_kernel(plan, table_rows, ffn_rows, refs):
+    (
+        table_in, proj_in, ffn_in, places_in, visual_in, boxes_in, small_in, tile_in,
+        shared_out, split_out, tile_out,
+        shared_acc, split_acc, shared_got, split_got, ring_got, ring_own, tile_mp, tile_dp,
+        load_sem, send_sem, recv_sem, ring_send, ring_recv, tile_send, tile_recv,
+    ) = refs
+    dp, mp = plan.dp, plan.mp
+    me, here = lax.axis_index("dp"), lax.axis_index("mp")
+    depth, ring_depth = bits_of(dp), bits_of(mp)
+    ring = mp == 4
+    loads = []
+
+    def load(source, target):
+        loads.append(pltpu.make_async_copy(source, target, load_sem.at[len(loads)]))
+
+    for part in range(4):
+        load(proj_in.at[part], shared_acc.at[:, pl.ds(part * plan.proj, plan.proj)])
+    load(places_in, shared_acc.at[:, pl.ds(plan.places_at, plan.places)])
+    load(visual_in, shared_acc.at[:, pl.ds(plan.visual_at, plan.visual)])
+    pieces_box = plan.box // 32
+    for part in range(plan.box_parts):
+        row, lane = plan.box_slot(part)
+        load(
+            boxes_in.at[part // pieces_box, :, pl.ds(32 * (part % pieces_box), 32)],
+            shared_acc.at[:, pl.ds(row, 32), pl.ds(lane, LANES)],
+        )
+    row, lane = plan.box_slot(plan.box_parts)
+    load(small_in, shared_acc.at[:, pl.ds(row, 32), pl.ds(lane, LANES)])
+    load(table_in, split_acc.at[:, pl.ds(0, table_rows)])
+    for part in range(2):
+        wide = ffn_in.shape[3]
+        row, lane = ffn_slot(part, table_rows, ffn_rows, wide)
+        load(ffn_in.at[part], split_acc.at[:, pl.ds(row, ffn_rows), pl.ds(lane, wide)])
+    for copy in loads:
+        copy.start()
+
+    barrier = pltpu.get_barrier_semaphore()
+    for other in range(1, dp):
+        pl.semaphore_signal(
+            barrier, 1, device_id={"dp": lax.rem(me + other, dp)}, device_id_type=MESH
+        )
+    for other in range(1, mp):
+        pl.semaphore_signal(
+            barrier, 1, device_id={"mp": lax.rem(here + other, mp)}, device_id_type=MESH
+        )
+    pl.semaphore_wait(barrier, dp + mp - 2)
+    for copy in loads:
+        copy.wait()
+
+    for part in range(plan.box_parts + 1, 6 * (plan.shared - plan.box_at) // 32):
+        row, lane = plan.box_slot(part)
+        shared_acc[:, pl.ds(row, 32), pl.ds(lane, LANES)] = jnp.zeros((dp, 32, LANES), LOW)
+
+    orders = ([0] + list(range(depth - 1, 0, -1)), list(range(depth)))
+    pieces = []
+    for acc, got, rows in (
+        (shared_acc, shared_got, plan.shared),
+        (split_acc, split_got, split_acc.shape[1]),
+    ):
+        for part in range(2):
+            pieces.append((acc, got, part * (rows // 2), rows // 2))
+
+    def chunk(order, step, free, away):
+        index = 0
+        for place, bit in enumerate(order):
+            mine = (me // 2**bit) % 2
+            if place < step or (place == step and not away):
+                index = index + mine * 2**bit
+            elif place == step:
+                index = index + (1 - mine) * 2**bit
+            else:
+                index = index + ((free >> (place - step - 1)) & 1) * 2**bit
+        return index
+
+    def slot_base(step):
+        return sum(2 ** (depth - 1 - s) for s in range(step))
+
+    def region(piece, stream, step):
+        acc, got, first, rows = pieces[piece]
+        count = 2 ** (depth - 1 - step)
+        return got.at[pl.ds(slot_base(step), count), pl.ds(first, rows), lanes_of(stream)]
+
+    def send(piece, stream, step):
+        acc, got, first, rows = pieces[piece]
+        order = orders[stream]
+        for free in range(2 ** (depth - 1 - step)):
+            pltpu.make_async_remote_copy(
+                src_ref=acc.at[chunk(order, step, free, True), pl.ds(first, rows), lanes_of(stream)],
+                dst_ref=got.at[slot_base(step) + free, pl.ds(first, rows), lanes_of(stream)],
+                send_sem=send_sem.at[piece, stream, step],
+                recv_sem=recv_sem.at[piece, stream, step],
+                device_id={"dp": flip(me, order[step], False)},
+                device_id_type=MESH,
+            ).start()
+
+    def wait_bytes(piece, stream, step, sem):
+        where = region(piece, stream, step)
+        pltpu.make_async_copy(where, where, sem.at[piece, stream, step]).wait()
+
+    def finish(piece, stream, step):
+        acc, got, first, rows = pieces[piece]
+        order = orders[stream]
+        wait_bytes(piece, stream, step, recv_sem)
+        tile = row_tile(rows)
+        last = step == depth - 1
+        out, low_out = (shared_out, True) if acc is shared_acc else (split_out, False)
+        for free in range(2 ** (depth - 1 - step)):
+            kept = chunk(order, step, free, False)
+
+            def body(index, carry):
+                at = pl.multiple_of(first + index * tile, 16)
+                where = pl.ds(at, tile)
+                total = acc[kept, where, lanes_of(stream)].astype(WIDE) + got[
+                    slot_base(step) + free, where, lanes_of(stream)
+                ].astype(WIDE)
+                if last and not low_out:
+                    out[where, lanes_of(stream)] = total
+                elif last:
+                    ring_own[0, where, lanes_of(stream)] = total.astype(LOW)
+                else:
+                    acc[kept, where, lanes_of(stream)] = total.astype(LOW)
+                return carry
+
+            lax.fori_loop(0, rows // tile, body, 0)
+
+    ring_orders = (list(range(ring_depth)), list(range(ring_depth - 1, -1, -1)))
+
+    def ring_copy(stream, step):
+        return pltpu.make_async_remote_copy(
+            src_ref=ring_own.at[step, :, lanes_of(stream)],
+            dst_ref=ring_got.at[step, :, lanes_of(stream)],
+            send_sem=ring_send.at[stream, step],
+            recv_sem=ring_recv.at[stream, step],
+            device_id={"mp": flip(here, ring_orders[stream][step], ring)},
+            device_id_type=MESH,
+        )
+
+    def ring_finish(stream, step):
+        ring_copy(stream, step).wait_recv()
+        rows = plan.shared
+        tile = row_tile(rows)
+
+        def body(index, carry):
+            where = pl.ds(pl.multiple_of(index * tile, 16), tile)
+            total = ring_own[step, where, lanes_of(stream)].astype(WIDE) + ring_got[
+                step, where, lanes_of(stream)
+            ].astype(WIDE)
+            if step == ring_depth - 1:
+                shared_out[where, lanes_of(stream)] = total
+            else:
+                ring_own[step + 1, where, lanes_of(stream)] = total.astype(LOW)
+            return carry
+
+        lax.fori_loop(0, rows // tile, body, 0)
+
+    everything = [(piece, stream) for piece in range(len(pieces)) for stream in range(2)]
+    for piece, stream in everything:
+        send(piece, stream, 0)
+    for step in range(depth):
+        for piece, stream in everything:
+            finish(piece, stream, step)
+            if step < depth - 1:
+                send(piece, stream, step + 1)
+            elif piece == 1:
+                ring_copy(stream, 0).start()
+    for step in range(ring_depth):
+        for stream in range(2):
+            ring_finish(stream, step)
+            if step < ring_depth - 1:
+                ring_copy(stream, step + 1).start()
+
+    def squares(ref, rows):
+        tile = row_tile(rows)
+
+        def body(index, total):
+            values = ref[pl.ds(pl.multiple_of(index * tile, 16), tile), :]
+            return total + jnp.sum((values * values).reshape(tile // 8, 8, D), 0)
+
+        total = lax.fori_loop(0, rows // tile, body, jnp.zeros((8, D), WIDE))
+        folded = total[:, 0:LANES]
+        for part in range(1, D // LANES):
+            folded = folded + total[:, part * LANES : (part + 1) * LANES]
+        return folded
+
+    folded = squares(shared_out, plan.shared) * (1.0 / mp) + squares(split_out, split_out.shape[0])
+    tile_mp[here, 0] = folded
+    tile_mp[here, 1] = tile_in[...]
+
+    def exchange(buffer, axis, index, count, base):
+        copies = []
+        for other in range(1, count):
+            copies.append(
+                pltpu.make_async_remote_copy(
+                    src_ref=buffer.at[index],
+                    dst_ref=buffer.at[index],
+                    send_sem=tile_send.at[base + other],
+                    recv_sem=tile_recv.at[base + other],
+                    device_id={axis: lax.rem(index + other, count)},
+                    device_id_type=MESH,
+                )
+            )
+        for copy in copies:
+            copy.start()
+        for other in range(1, count):
+            source = lax.rem(index + count - other, count)
+            pltpu.make_async_copy(
+                buffer.at[source], buffer.at[source], tile_recv.at[base + other]
+            ).wait()
+        return copies
+
+    pending = exchange(tile_mp, "mp", here, mp, 0)
+    total = tile_mp[0]
+    for index in range(1, mp):
+        total = total + tile_mp[index]
+    tile_dp[me] = total
+    pending = pending + exchange(tile_dp, "dp", me, dp, mp)
+    total = tile_dp[0]
+    for index in range(1, dp):
+        total = total + tile_dp[index]
+    tile_out[...] = total
+    for copy in pending:
+        copy.wait_send()
+    for piece, stream in everything:
+        for step in range(depth):
+            wait_bytes(piece, stream, step, send_sem)
+    for stream in range(2):
+        for step in range(ring_depth):
+            ring_copy(stream, step).wait_send()
+
+
+def reduce_gradients(plan, table, proj, ffn, places, visual, boxes, small, tile):
+    dp, mp = plan.dp, plan.mp
+    table_rows, ffn_rows = table.shape[1], ffn.shape[2]
+    split = table_rows + 2 * ffn_rows * ffn.shape[3] // D
+    depth, ring_depth = bits_of(dp), bits_of(mp)
+    loads = 4 + 2 + plan.box_parts + 1 + 1 + 2
+    anywhere = pl.BlockSpec(memory_space=pl.ANY)
+    vmem = pl.BlockSpec(memory_space=pltpu.VMEM)
+    dma = pltpu.SemaphoreType.DMA
+
+    def body(*refs):
+        reduce_kernel(plan, table_rows, ffn_rows, refs)
+
+    return pl.pallas_call(
+        body,
+        out_shape=(
+            jax.ShapeDtypeStruct((plan.shared, D), WIDE),
+            jax.ShapeDtypeStruct((split, D), WIDE),
+            jax.ShapeDtypeStruct((2, 8, LANES), WIDE),
+        ),
+        in_specs=[anywhere] * 7 + [vmem],
+        out_specs=(vmem, vmem, vmem),
+        scratch_shapes=[
+            pltpu.VMEM((dp, plan.shared, D), LOW),
+            pltpu.VMEM((dp, split, D), LOW),
+            pltpu.VMEM((dp - 1, plan.shared, D), LOW),
+            pltpu.VMEM((dp - 1, split, D), LOW),
+            pltpu.VMEM((ring_depth, plan.shared, D), LOW),
+            pltpu.VMEM((ring_depth, plan.shared, D), LOW),
+            pltpu.VMEM((mp, 2, 8, LANES), WIDE),
+            pltpu.VMEM((dp, 2, 8, LANES), WIDE),
+            dma((loads,)),
+            dma((4, 2, depth)),
+            dma((4, 2, depth)),
+            dma((2, ring_depth)),
+            dma((2, ring_depth)),
+            dma((mp + dp,)),
+            dma((mp + dp,)),
+        ],
+        compiler_params=pltpu.CompilerParams(
+            collective_id=5, has_side_effects=True, vmem_limit_bytes=56 * 2**20
+        ),
+        name="reduce_gradients",
+    )(table, proj, ffn, places, visual, boxes, small, tile)
+
+
+def adam_kernel(plan, table_rows, ffn_rows, sizes, refs):
+    shared_ref, split_ref, tile_ref = refs[:3]
+    states, outs = refs[3:24], refs[24:45]
+    totals = tile_ref[...]
+    norm = jnp.sqrt(jnp.sum(totals[0], keepdims=True)) / totals[1, 1:2, 0:1]
+    scale = jnp.minimum(1.0, CLIP / norm) / totals[1, 1:2, 0:1]
+
+    def update(index, where, rows, grad_of):
+        rate = RATES[index]
+        weight, first, second = (ref[where] for ref in states[3 * index : 3 * index + 3])
+        grad = grad_of * scale
+        results = adam_step(weight, grad, first, second, rate)
+        for ref, value in zip(outs[3 * index : 3 * index + 3], results):
+            ref[where] = value
+
+    def blocks(index, lead, source, at, rows, lane=0, wide=D):
+        tile = next(t for t in (32, 24, 16, 8) if rows % t == 0)
+
+        def body(step, carry):
+            here = pl.multiple_of(step * tile, 8)
+            where = (pl.ds(here, tile), slice(None))
+            grad = source[pl.ds(pl.multiple_of(at + here, 8), tile), pl.ds(lane, wide)]
+            update(index, where if lead is None else (lead,) + where, tile, grad)
+            return carry
+
+        lax.fori_loop(0, rows // tile, body, 0)
+
+    for part in range(4):
+        blocks(0, part, shared_ref, part * plan.proj, sizes[0])
+    pieces_box = plan.box // 32
+    for part in range(plan.box_parts):
+        row, lane = plan.box_slot(part)
+        grad = shared_ref[pl.ds(row, 32), pl.ds(lane, LANES)]
+        update(1, (part // pieces_box, pl.ds(32 * (part % pieces_box), 32)), 32, grad)
+    blocks(2, None, shared_ref, plan.places_at, sizes[2])
+    blocks(3, None, shared_ref, plan.visual_at, sizes[3])
+    row, lane = plan.box_slot(plan.box_parts)
+    grad = shared_ref[pl.ds(row, 32), pl.ds(lane, LANES)]
+    update(4, (slice(None), slice(None)), VROWS, grad[:VROWS, : sizes[4]])
+    blocks(5, None, split_ref, 0, sizes[5])
+    for part in range(2):
+        wide = states[18].shape[2]
+        row, lane = ffn_slot(part, table_rows, ffn_rows, wide)
+        blocks(6, part, split_ref, row, sizes[6], lane, wide)
+
+
+def adam_update(plan, table_rows, ffn_rows, shared, split, tile, states):
+    sizes = (
+        states[0].shape[1], 0, states[6].shape[0], states[9].shape[0], states[12].shape[1],
+        states[15].shape[0], states[18].shape[1],
+    )
+    vmem = pl.BlockSpec(memory_space=pltpu.VMEM)
+
+    def body(*refs):
+        adam_kernel(plan, table_rows, ffn_rows, sizes, refs)
+
+    return pl.pallas_call(
+        body,
+        out_shape=tuple(jax.ShapeDtypeStruct(part.shape, WIDE) for part in states),
+        in_specs=[vmem] * 24,
+        out_specs=(vmem,) * 21,
+        compiler_params=pltpu.CompilerParams(vmem_limit_bytes=48 * 2**20),
+        name="adam_update",
+    )(shared, split, tile, *states)
 
 
 def on_device(
@@ -360,78 +759,46 @@
         0,
     )
     grad_attn = jnp.concatenate([grad_in_weight, grad_out_weight[None]], 0)
-    def scattered(part, axis):
-        low_part = part.astype(jnp.bfloat16)
-        return lax.psum_scatter(low_part, "dp", scatter_dimension=axis, tiled=True).astype(f32)
-
-    shared_parts = (
-        scattered(grad_attn, 1),
-        scattered(grad_boxes, 1),
-        scattered(grad_places, 0),
-        scattered(grad_visual, 0),
-        lax.psum_scatter(grad_small, "dp", scatter_dimension=1, tiled=True),
-    )
-    reduced_proj, reduced_boxes, reduced_places, reduced_visual, reduced_small = lax.psum(
-        shared_parts, "mp"
-    )
-    reduced_table, reduced_ffn = (scattered(grad_table, 0), scattered(grad_ffn, 1))
-    reduced = (
-        reduced_proj,
-        reduced_boxes,
-        reduced_places,
-        reduced_visual,
-        reduced_small,
-        reduced_table,
-        reduced_ffn,
-    )
-    shared_squares = jnp.zeros((), jnp.float32)
-    for part in reduced[:5]:
-        shared_squares = shared_squares + jnp.sum(part * part)
-    split_squares = jnp.sum(reduced_table * reduced_table) + jnp.sum(reduced_ffn * reduced_ffn)
-    squares = split_squares + jnp.where(model_index == 0, shared_squares, 0.0)
-    total_squares, loss_sum, loss_count = lax.psum(
-        (squares, jnp.sum(own_loss), jnp.sum(own_valid)), ("dp", "mp")
-    )
-    grad_norm = jnp.sqrt(total_squares) / loss_count
-    factor = jnp.minimum(1.0, CLIP / grad_norm)
-    masters = (
-        projections,
-        box_tables,
-        position_table,
-        visual_proj,
-        small_params,
-        word_table,
-        feedforward,
-    )
-    firsts = (
-        projections_first,
-        box_tables_first,
-        position_table_first,
-        visual_proj_first,
-        small_params_first,
-        word_table_first,
-        feedforward_first,
-    )
-    seconds = (
-        projections_second,
-        box_tables_second,
-        position_table_second,
-        visual_proj_second,
-        small_params_second,
-        word_table_second,
-        feedforward_second,
-    )
-    outputs = []
-    for index in range(7):
-        outputs.extend(
-            adam_step(
-                masters[index],
-                reduced[index] / loss_count * factor,
-                firsts[index],
-                seconds[index],
-                RATES[index],
-            )
-        )
+    dp, mp = lax.axis_size("dp"), lax.axis_size("mp")
+    plan = Plan(dp, mp)
+
+    def split_rows(part):
+        rows = part.shape[-2] // dp
+        part = part.astype(LOW).reshape(part.shape[:-2] + (dp, rows, part.shape[-1]))
+        extra = [(0, 0)] * (part.ndim - 2) + [(0, pad_up(rows, 16) - rows), (0, 0)]
+        return jnp.pad(part, extra) if extra[-2][1] else part
+
+    cut = small_params.shape[1]
+    small_split = jnp.transpose(grad_small.reshape(VROWS, dp, cut), (1, 0, 2)).astype(LOW)
+    small_split = jnp.pad(small_split, ((0, 0), (0, 32 - VROWS), (0, LANES - cut)))
+    own_sums = jnp.stack([jnp.sum(own_loss), jnp.sum(own_valid)])
+    own_tile = jnp.pad(own_sums[:, None], ((0, 6), (0, LANES - 1)))
+    table_split, ffn_split = split_rows(grad_table), split_rows(grad_ffn)
+    shared_sum, split_sum, totals = reduce_gradients(
+        plan,
+        table_split,
+        split_rows(grad_attn),
+        ffn_split,
+        split_rows(grad_places),
+        split_rows(grad_visual),
+        grad_boxes.astype(LOW).reshape(4, dp, NBOX // dp, LANES),
+        small_split,
+        own_tile,
+    )
+    loss_sum, loss_count = (totals[1, 0, 0], totals[1, 1, 0])
+    grad_norm = jnp.sqrt(jnp.sum(totals[0])) / loss_count
+    states = (
+        projections, projections_first, projections_second,
+        box_tables, box_tables_first, box_tables_second,
+        position_table, position_table_first, position_table_second,
+        visual_proj, visual_proj_first, visual_proj_second,
+        small_params, small_params_first, small_params_second,
+        word_table, word_table_first, word_table_second,
+        feedforward, feedforward_first, feedforward_second,
+    )
+    outputs = adam_update(
+        plan, table_split.shape[1], ffn_split.shape[2], shared_sum, split_sum, totals, states
+    )
     return tuple(outputs) + (loss_sum, loss_count, grad_norm)
 
 

time: 873 us -> 687 us (0.79)
  waiting for transfers between devices: 347 us -> 106 us
  Pallas kernels: 0 us -> 126 us
  blocking collectives: 195 us -> 89.1 us
  local copies, waits for them, and re-layouts: 65.4 us -> 108 us
  other arithmetic: 138 us -> 121 us
  matrix products: 96.4 us -> 109 us
    reduce_scatter x6 -> x0, waiting for transfers between devices: 203 us -> none  [scattered(): lax.psum_scatter(low_part, 'dp', scatter_dimension=axis, tiled=True)]
    pallas_call x0 -> x2, Pallas kernels: none -> 126 us  [the longest x1 114 us: reduce_gradients(): pl.pallas_call(body, out_shape=(jax.ShapeDtypeStruct((plan.shared, D), WI...]
    psum x2 -> x0, blocking collectives: 106 us -> none  [the longest x1 67.2 us: on_device(): lax.psum(shared_parts, 'mp')]
    all_gather x1, waiting for transfers between devices: 24.5 us -> 3.3 us  [on_device(): lax.all_gather(projections.astype(jnp.bfloat16), 'dp', axis=1, tiled=True)]
    reduce_scatter x1, waiting for transfers between devices: 24.6 us -> 4.82 us  [on_device(): lax.psum_scatter(dot(grad_pre, work_ffn[0], ((1,), (1,))), 'mp', scatter_...]
    sub x7 -> x0, other arithmetic: 17.3 us -> none  [adam_step(): weight - rate * (fixed_first / (jnp.sqrt(fixed_second) + EPSILON) + DECAY...]
    unnamed x341 -> x348, local copies, waits for them, and re-layouts: 16.7 us -> 30.5 us
    concatenate x1 -> x13, local copies, waits for them, and re-layouts: 0.19 us -> 9.88 us  [on_device(): jnp.concatenate([jnp.stack([grad_gain_zero, grad_shift_zero, jnp.sum(grad...]
  transfers between devices with their start and end apart: 16 -> 9, of which waited for: 10 -> 5; matrix products, arithmetic and copies ran while one was open for 25% -> 33% of each run, Pallas kernels for 0% -> 0%
where the time goes in v2:
time: 687 us; the launch traced here: 679 us
  Pallas kernels  126 us (18%)
  other arithmetic  121 us (18%)
  matrix products  109 us (16%)
  local copies, waits for them, and re-layouts  108 us (16%)
  waiting for transfers between devices  106 us (15%)
  blocking collectives  89.1 us (13%)
  between operations  18.7 us (3%)
    pallas_call x1, Pallas kernels, reduce_gradients(): pl.pallas_call(body, out_shape=(jax.ShapeDtypeStruct((plan.shared, D), WI...  114 us
    dot_general x22, matrix products, dot(): lax.dot_general(left, right, (dims, ((), ())), preferred_element_type=f32)  60 us
    all_gather x1, waiting for transfers between devices, on_device(): lax.all_gather(word_table.astype(jnp.bfloat16), 'dp', axis=0, tiled=True)  46.6 us
    unnamed x348, local copies, waits for them, and re-layouts  30.5 us
    reduce_scatter x1, waiting for transfers between devices, on_device(): lax.psum_scatter(dot(active_low, work_ffn[1], ((1,), (1,))), 'mp', scatte...  26.7 us
    reduce_scatter x1, waiting for transfers between devices, on_device(): lax.psum_scatter(dot(grad_logits, work_table, ((1,), (0,))), 'mp', scatte...  24.6 us
    scatter-add x1, other arithmetic, on_device(): jnp.zeros((vocab_shard, width), f32).at[safe_index]  23.1 us
    all_gather x1, blocking collectives, on_device(): group_grad = lax.all_gather(grad_ffn_low, 'mp', axis=0, tiled=True)  15.7 us
  transfers between devices with their start and end apart: 9, of which 5 were waited for; matrix products, arithmetic and copies ran while one was open for 33% of the time, Pallas kernels for 0%

profile of v2, /device:TPU:0, one launch (start us, length us, event | category | flops | bytes accessed | tf_op | source)
XLA Modules:
  0.0 678.9 jit_solution(9016658363208288306)
XLA Ops:
  10.6 46.6 %all-gather.9.cloned.1.call-done = bf16[3840,768]{1,0:T(8,128)(2,1)} async-done(((bf16[480,768]{1,0:T(8,128)(2,1)}), bf16[3840,768]{1,0:T(8,128)(2,1)}) %all-gather.9.cloned.1.call-update) | async-done | bytes 5898256 | tf_op jit(solution)/shard_map/all_gather | solution.py:586
  57.1 13.5 %gather_fusion = bf16[2048,768]{1,0:T(8,128)(2,1)} fusion(bf16[3840,768]{1,0:T(8,128)(2,1)} %all-gather.9.cloned.1.call-done, s32[2048]{0:T(1024)S(1)} %broadcast_clamp_fusion), kind=kCustom, calls=%fused_computation | custom fusion | bytes 6299648 | tf_op jit(solution)/shard_map/jit(_take)/gather | solution.py:602
  70.7 3.4 select_select_fusion
  81.4 9.1 %all-gather.1 = bf16[8,96,17]{1,2,0:T(8,128)(2,1)S(1)} all-gather(bf16[1,96,17]{1,2,0:T(8,128)(2,1)S(1)} %convert_bitcast_fusion), channel_id=1, replica_groups=mesh['dp'=8,'mp'=4] {'dp'}, dimensions={0}, use_global_device_ids=true | all-gather | bytes 29376 | tf_op jit(solution)/shard_map/all_gather | solution.py:585
  95.9 9.7 %all_gather.42 = bf16[256,768]{1,0:T(8,128)(2,1)} all-gather(bf16[32,768]{1,0:T(8,128)(2,1)S(1)} %convert_element_type.253), channel_id=1, replica_groups=mesh['dp'=8,'mp'=4] {'dp'}, dimensions={0}, use_global_device_ids=true | all-gather | bytes 442368 | tf_op jit(solution)/shard_map/all_gather | solution.py:584
  105.6 10.5 %all_gather.40 = bf16[512,768]{1,0:T(8,128)(2,1)S(1)} all-gather(bf16[64,768]{1,0:T(8,128)(2,1)S(1)} %convert_element_type.249), channel_id=1, replica_groups=mesh['dp'=8,'mp'=4] {'dp'}, dimensions={0}, use_global_device_ids=true | all-gather | bytes 884736 | tf_op jit(solution)/shard_map/all_gather | solution.py:583
  126.8 5.6 fusion.43
  132.5 6.1 select_reduce_fusion
  147.8 2.7 gather_fusion.5
  181.3 2.4 gather_fusion.13
  183.7 3.3 all-gather.13.cloned.1.call-done
  189.5 3.6 convolution_convert_fusion.7
  194.6 4.0 add_convert_fusion.1
  198.7 2.7 copy.97
  206.5 5.4 convolution_convert_fusion.11
  214.2 15.3 %all_gather.45 = bf16[320,768]{1,0:T(8,128)(2,1)S(1)} all-gather(bf16[80,768]{1,0:T(8,128)(2,1)S(1)} %fusion.108), channel_id=1, replica_groups=mesh['dp'=8,'mp'=4] {'mp'}, dimensions={0}, use_global_device_ids=true | all-gather | bytes 614400 | tf_op jit(solution)/shard_map/all_gather | solution.py:653
  229.6 5.2 multiply_convert_fusion.3
  237.2 26.7 %reduce-scatter.7.cloned.1.call-done = f32[80,768]{1,0:T(8,128)} async-done(((f32[320,768]{1,0:T(8,128)}), f32[80,768]{1,0:T(8,128)}) %reduce-scatter.7.cloned.1.call-update) | async-done | bytes 245776 | tf_op jit(solution)/shard_map/reduce_scatter | solution.py:657
  265.4 15.6 %all_gather.47 = bf16[320,768]{1,0:T(8,128)(2,1)S(1)} all-gather(bf16[80,768]{1,0:T(8,128)(2,1)S(1)} %add_convert_fusion.3), channel_id=1, replica_groups=mesh['dp'=8,'mp'=4] {'mp'}, dimensions={0}, use_global_device_ids=true | all-gather | bytes 614400 | tf_op jit(solution)/shard_map/all_gather | solution.py:665
  281.0 5.1 fusion.165
  287.5 13.1 %all-gather.2 = f32[4,3,320]{2,1,0:T(4,128)S(1)} all-gather(f32[1,3,320]{2,1,0:T(4,128)S(1)} %maximum_bitcast_fusion), channel_id=2, replica_groups=mesh['dp'=8,'mp'=4] {'mp'}, dimensions={0}, use_global_device_ids=true | all-gather | bytes 19200 | tf_op jit(solution)/shard_map/all_gather | solution.py:672
  301.3 6.4 fusion.151
  307.8 24.6 %reduce-scatter.9.cloned.1.call-done = f32[80,768]{1,0:T(8,128)} async-done(((f32[320,768]{1,0:T(8,128)}), f32[80,768]{1,0:T(8,128)}) %reduce-scatter.9.cloned.1.call-update) | async-done | bytes 245776 | tf_op jit(solution)/shard_map/reduce_scatter | solution.py:686
  335.1 15.7 %all_gather.50 = bf16[320,768]{1,0:T(8,128)(2,1)S(1)} all-gather(bf16[80,768]{1,0:T(8,128)(2,1)S(1)} %get-tuple-element.103), channel_id=1, replica_groups=mesh['dp'=8,'mp'=4] {'mp'}, dimensions={0}, use_global_device_ids=true | all-gather | bytes 614400 | tf_op jit(solution)/shard_map/all_gather | solution.py:691
  350.8 2.9 convert_reduce_fusion
  365.1 10.7 %fusion.152 = f32[3840,768]{1,0:T(8,128)} fusion(bf16[320,768]{1,0:T(8,128)(2,1)} %copy-done.53, f32[320,3840]{1,0:T(8,128)} %copy-done.23, f32[320]{0:T(512)S(1)} %copy-done.109, f32[320]{0:T(512)S(1)} %get-tuple-element.99, s32[320]{0:T(512)S(1)} %copy-done.105), kind=kOutput, calls=%fused_computation.391 | convolution fusion | flops 1894809600 | bytes 17207040 | tf_op jit(solution)/shard_map/dot_general | solution.py:627
  375.8 4.8 reduce-scatter.11.cloned.1.call-done
  385.3 5.9 bitcast_reduce_fusion
  391.2 2.8 multiply_reduce_fusion
  402.3 4.3 scatter_fusion
  406.7 3.2 fusion.153
  423.4 3.4 scatter_custom_fusion.13
  426.8 3.4 scatter_custom_fusion.12
  430.3 3.4 scatter_custom_fusion.11
  433.7 3.8 scatter_custom_fusion.10
  437.5 3.5 scatter_custom_fusion.9
  441.0 3.4 scatter_custom_fusion.8
  462.8 2.9 fusion.1
  465.7 2.8 convolution_bitcast_fusion
  468.5 3.1 copy.114
  471.6 2.9 fusion.3
  478.2 3.0 fusion.49
  493.8 2.4 pad_maximum_fusion.refs_1_
  496.2 4.4 convert_select_fusion
  500.6 23.1 %scatter_fusion.1 = f32[3840,768]{1,0:T(8,128)} fusion(f32[3840,768]{1,0:T(8,128)} %fusion.152, s32[2048]{0:T(1024)S(1)} %bitcast.385, f32[2048,768]{1,0:T(8,128)} %bitcast.339), kind=kCustom, calls=%fused_computation.22 | custom fusion | flops 1572864 | bytes 18882560 | tf_op jit(solution)/shard_map/scatter-add | solution.py:736
  523.7 7.5 %convert_element_type.293 = bf16[3840,768]{1,0:T(8,128)(2,1)} convert(f32[3840,768]{1,0:T(8,128)} %scatter_fusion.1) | non-fusion elementwise | flops 2949120 | bytes 17694720 | tf_op jit(solution)/shard_map/convert_element_type | solution.py:767
  531.3 114.3 %reduce_gradients.1 = (f32[576,768]{1,0:T(8,128)}, f32[672,768]{1,0:T(8,128)}, f32[2,8,128]{2,1,0:T(8,128)}) custom-call(bf16[8,480,768]{2,1,0:T(8,128)(2,1)} %bitcast.340, bf16[4,8,96,768]{3,2,1,0:T(8,128)(2,1)} %pad_maximum_fusion.refs_1_, bf16[2,8,96,768]{3,2,1,0:T(8,128)(2,1)} %pad_maximum_fusion.1.refs_2_, bf16[8,64,768]{2,1,0:T(8,128)(2,1)} %bitcast.347, ...), custom_call_target="tpu_custom_call" | custom-call | tf_op jit(solution)/shard_map/reduce_gradients/pallas_call | solution.py:450
  659.3 11.7 %adam_update.1 = (f32[4,96,768]{2,1,0:T(8,128)}, f32[4,96,768]{2,1,0:T(8,128)}, f32[4,96,768]{2,1,0:T(8,128)}, f32[4,128,128]{2,1,0:T(8,128)}, f32[4,128,128]{2,...) custom-call(f32[576,768]{1,0:T(8,128)} %get-tuple-element.48.refs_0_, ...), custom_call_target="tpu_custom_call" | custom-call | tf_op jit(solution)/shard_map/adam_update/pallas_call | solution.py:539
  (562 shorter events, 170.1 us)
Async XLA Ops:
  7.2 167.9 %copy-start = (bf16[49,256]{1,0:T(8,128)(2,1)S(1)}, bf16[49,256]{1,0:T(8,128)(2,1)}, u32[]{:S(2)}) copy-start(bf16[49,256]{1,0:T(8,128)(2,1)} %param.33) | copy-start | bytes 75268
  7.2 49.9 %all-gather.9.cloned.1.call-start = ((), (), s32[]{:S(2)}) async-start(), calls=%async_computation.4 | async-start | bytes 6635520 | tf_op jit(solution)/shard_map/all_gather | solution.py:586
  9.6 128.9 %all-gather.11.cloned.1.call-start = ((), (), s32[]{:S(2)}) async-start(), calls=%async_computation.6 | async-start | bytes 1179648 | tf_op jit(solution)/shard_map/all_gather | solution.py:582
  10.4 165.9 %reduce-scatter.5.cloned.1.call-start = ((), (), s32[]{:S(2)}) async-start(), calls=%async_computation.5 | async-start | bytes 3932160 | tf_op jit(solution)/shard_map/reduce_scatter | solution.py:604
  10.5 60.2 %copy-start.91 = (s32[1,4,4,128]{3,1,2,0:T(4,128)}, s32[1,4,4,128]{3,1,2,0:T(4,128)S(1)}, u32[]{:S(2)}) copy-start(s32[1,4,4,128]{3,1,2,0:T(4,128)S(1)} %copy.148) | copy-start | bytes 24580
  10.5 60.1 %copy-start.106 = (pred[4,512]{1,0:T(4,128)(4,1)}, pred[4,512]{1,0:T(4,128)(4,1)S(1)}, u32[]{:S(2)}) copy-start(pred[4,512]{1,0:T(4,128)(4,1)S(1)} %get-tuple-element.127) | copy-start | bytes 6148
  74.1 112.9 %all-gather.13.cloned.1.call-start = ((), (), s32[]{:S(2)}) async-start(), calls=%async_computation.7 | async-start | bytes 5308416 | tf_op jit(solution)/shard_map/all_gather | solution.py:581
  76.3 153.3 %all-gather.15.cloned.1.call-start = ((), (), s32[]{:S(2)}) async-start(), calls=%async_computation.8 | async-start | bytes 2654208 | tf_op jit(solution)/shard_map/all_gather | solution.py:587
  77.1 186.8 %reduce-scatter.7.cloned.1.call-start = ((), (), s32[]{:S(2)}) async-start(), calls=%async_computation.9 | async-start | bytes 1228800 | tf_op jit(solution)/shard_map/reduce_scatter | solution.py:657
  77.7 44.5 %copy-start.157 = (s32[49]{0:T(128)}, s32[49]{0:T(128)S(1)}, u32[]{:S(2)}) copy-start(s32[49]{0:T(128)S(1)} %fusion.142) | copy-start | bytes 592
  77.8 44.5 %copy-start.158 = (s32[49]{0:T(128)}, s32[49]{0:T(128)S(1)}, u32[]{:S(2)}) copy-start(s32[49]{0:T(128)S(1)} %fusion.141) | copy-start | bytes 592
  77.8 43.8 %copy-start.159 = (s32[49]{0:T(128)}, s32[49]{0:T(128)S(1)}, u32[]{:S(2)}) copy-start(s32[49]{0:T(128)S(1)} %fusion.140) | copy-start | bytes 592
  77.8 43.8 %copy-start.160 = (s32[49]{0:T(128)}, s32[49]{0:T(128)S(1)}, u32[]{:S(2)}) copy-start(s32[49]{0:T(128)S(1)} %fusion.139) | copy-start | bytes 592
  77.9 43.1 %copy-start.161 = (s32[49]{0:T(128)}, s32[49]{0:T(128)S(1)}, u32[]{:S(2)}) copy-start(s32[49]{0:T(128)S(1)} %fusion.138) | copy-start | bytes 592
  77.9 43.1 %copy-start.162 = (s32[49]{0:T(128)}, s32[49]{0:T(128)S(1)}, u32[]{:S(2)}) copy-start(s32[49]{0:T(128)S(1)} %fusion.137) | copy-start | bytes 592
  78.0 39.5 %copy-start.78 = (s32[64,64]{0,1:T(8,128)}, s32[64,64]{0,1:T(8,128)S(1)}, u32[]{:S(2)}) copy-start(s32[64,64]{0,1:T(8,128)S(1)} %clamp_add_fusion.1) | copy-start | bytes 49156
  78.1 38.0 %copy-start.80 = (s32[64,64]{0,1:T(8,128)}, s32[64,64]{0,1:T(8,128)S(1)}, u32[]{:S(2)}) copy-start(s32[64,64]{0,1:T(8,128)S(1)} %clamp_add_fusion) | copy-start | bytes 49156
  78.1 44.7 %copy-start.136 = (s32[1,512,1]{1,2,0:T(1,128)}, s32[1,512,1]{1,2,0:T(1,128)S(1)}, u32[]{:S(2)}) copy-start(s32[1,512,1]{1,2,0:T(1,128)S(1)} %get-tuple-element.131) | copy-start | bytes 6148
  78.2 44.7 %copy-start.137 = (s32[1,512,1]{1,2,0:T(1,128)}, s32[1,512,1]{1,2,0:T(1,128)S(1)}, u32[]{:S(2)}) copy-start(s32[1,512,1]{1,2,0:T(1,128)S(1)} %get-tuple-element.130) | copy-start | bytes 6148
  78.2 45.3 %copy-start.134 = (s32[1,512,1]{1,2,0:T(1,128)}, s32[1,512,1]{1,2,0:T(1,128)S(1)}, u32[]{:S(2)}) copy-start(s32[1,512,1]{1,2,0:T(1,128)S(1)} %get-tuple-element.129) | copy-start | bytes 6148
  78.2 45.2 %copy-start.135 = (s32[1,512,1]{1,2,0:T(1,128)}, s32[1,512,1]{1,2,0:T(1,128)S(1)}, u32[]{:S(2)}) copy-start(s32[1,512,1]{1,2,0:T(1,128)S(1)} %get-tuple-element.134) | copy-start | bytes 6148
  78.2 45.8 %copy-start.138 = (s32[1,512,1]{1,2,0:T(1,128)}, s32[1,512,1]{1,2,0:T(1,128)S(1)}, u32[]{:S(2)}) copy-start(s32[1,512,1]{1,2,0:T(1,128)S(1)} %get-tuple-element.132) | copy-start | bytes 6148
  78.2 45.8 %copy-start.139 = (s32[1,512,1]{1,2,0:T(1,128)}, s32[1,512,1]{1,2,0:T(1,128)S(1)}, u32[]{:S(2)}) copy-start(s32[1,512,1]{1,2,0:T(1,128)S(1)} %get-tuple-element.133) | copy-start | bytes 6148
  78.3 54.1 %copy-start.74 = (pred[1,64,561]{2,1,0:T(32,128)(4,1)}, pred[1,64,561]{2,1,0:T(32,128)(4,1)S(1)}, u32[]{:S(2)}) copy-start(pred[1,64,561]{2,1,0:T(32,128)(4,1)S(1)} %iota_compare_fusion.4) | copy-start | bytes 107716
  80.3 52.1 %copy-start.76 = (pred[1,64,561]{2,1,0:T(32,128)(4,1)}, pred[1,64,561]{2,1,0:T(32,128)(4,1)S(1)}, u32[]{:S(2)}) copy-start(pred[1,64,561]{2,1,0:T(32,128)(4,1)S(1)} %iota_compare_fusion.3) | copy-start | bytes 107716
  81.4 51.0 %copy-start.77 = (pred[1,64,561]{2,1,0:T(32,128)(4,1)}, pred[1,64,561]{2,1,0:T(32,128)(4,1)S(1)}, u32[]{:S(2)}) copy-start(pred[1,64,561]{2,1,0:T(32,128)(4,1)S(1)} %iota_compare_fusion.5) | copy-start | bytes 107716
  95.4 37.1 %copy-start.83 = (pred[1,80,64]{1,2,0:T(32,128)(4,1)}, pred[1,80,64]{1,2,0:T(32,128)(4,1)S(1)}, u32[]{:S(2)}) copy-start(pred[1,80,64]{1,2,0:T(32,128)(4,1)S(1)} %iota_compare_fusion.7) | copy-start | bytes 15364
  95.4 37.1 %copy-start.86 = (pred[1,80,64]{1,2,0:T(32,128)(4,1)}, pred[1,80,64]{1,2,0:T(32,128)(4,1)S(1)}, u32[]{:S(2)}) copy-start(pred[1,80,64]{1,2,0:T(32,128)(4,1)S(1)} %iota_compare_fusion.6) | copy-start | bytes 15364
  183.7 28.2 %copy-start.36 = (f32[80,768]{1,0:T(8,128)}, f32[80,768]{1,0:T(8,128)S(1)}, u32[]{:S(2)}) copy-start(f32[80,768]{1,0:T(8,128)S(1)} %gather_fusion.13) | copy-start | bytes 737284
  211.9 17.6 %copy-start.145 = (f32[768]{0:T(1024)S(1)}, f32[768]{0:T(1024)}, u32[]{:S(2)}) copy-start(f32[768]{0:T(1024)} %dynamic_slice.9) | copy-start | bytes 9220
  213.8 50.1 %copy-start.123 = (f32[80]{0:T(128)}, f32[80]{0:T(128)S(1)}, u32[]{:S(2)}) copy-start(f32[80]{0:T(128)S(1)} %broadcast_multiply_fusion.2) | copy-start | bytes 964
  214.0 20.7 %copy-start.155 = (f32[80]{0:T(128)}, f32[80]{0:T(128)S(1)}, u32[]{:S(2)}) copy-start(f32[80]{0:T(128)S(1)} %multiply_reduce_fusion.9) | copy-start | bytes 964
  214.0 49.9 %copy-start.141 = (f32[80]{0:T(128)}, f32[80]{0:T(128)S(1)}, u32[]{:S(2)}) copy-start(f32[80]{0:T(128)S(1)} %fusion.143) | copy-start | bytes 964
  235.5 28.4 %copy-start.111 = (f32[768]{0:T(1024)S(1)}, f32[768]{0:T(1024)}, u32[]{:S(2)}) copy-start(f32[768]{0:T(1024)} %get-tuple-element.86) | copy-start | bytes 9220
  235.5 29.8 %copy-start.93 = (f32[768]{0:T(1024)S(1)}, f32[768]{0:T(1024)}, u32[]{:S(2)}) copy-start(f32[768]{0:T(1024)} %get-tuple-element.84) | copy-start | bytes 9220
  235.5 29.8 %copy-start.110 = (f32[768]{0:T(1024)S(1)}, f32[768]{0:T(1024)}, u32[]{:S(2)}) copy-start(f32[768]{0:T(1024)} %get-tuple-element.85) | copy-start | bytes 9220
  237.1 95.3 %reduce-scatter.9.cloned.1.call-start = ((), (), s32[]{:S(2)}) async-start(), calls=%async_computation.10 | async-start | bytes 1228800 | tf_op jit(solution)/shard_map/reduce_scatter | solution.py:686
  237.2 64.1 %copy-start.108 = (f32[320]{0:T(512)}, f32[320]{0:T(512)S(1)}, u32[]{:S(2)}) copy-start(f32[320]{0:T(512)S(1)} %convert_element_type.278) | copy-start | bytes 3844
  237.2 64.1 %copy-start.104 = (s32[320]{0:T(512)}, s32[320]{0:T(512)S(1)}, u32[]{:S(2)}) copy-start(s32[320]{0:T(512)S(1)} %broadcast_subtract_fusion) | copy-start | bytes 3844
  307.8 72.8 %reduce-scatter.11.cloned.1.call-start = ((), (), s32[]{:S(2)}) async-start(), calls=%async_computation.11 | async-start | bytes 1228800 | tf_op jit(solution)/shard_map/reduce_scatter | solution.py:697
  332.4 18.4 %copy-start.164 = (f32[320,768]{1,0:T(8,128)S(1)}, f32[320,768]{1,0:T(8,128)}, u32[]{:S(2)}) copy-start(f32[320,768]{1,0:T(8,128)} %get-tuple-element.116) | copy-start | bytes 2949124
  332.4 18.4 %copy-start.165 = (f32[320,768]{1,0:T(8,128)S(1)}, f32[320,768]{1,0:T(8,128)}, u32[]{:S(2)}) copy-start(f32[320,768]{1,0:T(8,128)} %get-tuple-element.145) | copy-start | bytes 2949124
  334.9 18.8 %copy-start.39 = (f32[80,768]{1,0:T(8,128)}, f32[80,768]{1,0:T(8,128)S(1)}, u32[]{:S(2)}) copy-start(f32[80,768]{1,0:T(8,128)S(1)} %get-tuple-element.112) | copy-start | bytes 737284
  335.0 18.7 %copy-start.148 = (f32[80]{0:T(128)}, f32[80]{0:T(128)S(1)}, u32[]{:S(2)}) copy-start(f32[80]{0:T(128)S(1)} %negate_multiply_fusion.3) | copy-start | bytes 964
  356.1 140.1 %all-gather.17.cloned.1.call-start = ((), (), s32[]{:S(2)}) async-start(), calls=%async_computation.12 | async-start | bytes 3932160 | tf_op jit(solution)/shard_map/all_gather | solution.py:735
  445.3 17.4 %copy-start.75 = (pred[1,64,561]{2,1,0:T(32,128)(4,1)S(1)}, pred[1,64,561]{2,1,0:T(32,128)(4,1)}, u32[]{:S(2)}) copy-start(pred[1,64,561]{2,1,0:T(32,128)(4,1)} %copy-done.74) | copy-start | bytes 107716
  531.3 118.2 %copy-start.3 = (f32[4,96,768]{2,1,0:T(8,128)S(1)}, f32[4,96,768]{2,1,0:T(8,128)}, u32[]{:S(2)}) copy-start(f32[4,96,768]{2,1,0:T(8,128)} %refs_4_.1) | copy-start | bytes 3538948
  531.3 118.2 %copy-start.5 = (f32[4,128,128]{2,1,0:T(8,128)S(1)}, f32[4,128,128]{2,1,0:T(8,128)}, u32[]{:S(2)}) copy-start(f32[4,128,128]{2,1,0:T(8,128)} %refs_6_.1) | copy-start | bytes 786436
  (129 other events, 581.8 us)
Sparse Core Ops, SparseCore 0:
  10.5 46.5 all-gather.8
  59.6 23.4 all-gather.10
  85.4 60.2 reduce-scatter.4
  148.1 38.9 all-gather.12
  189.4 29.0 all-gather.14
  237.2 26.6 reduce-scatter.6
  307.9 24.4 reduce-scatter.8
  356.2 24.3 reduce-scatter.10
  414.1 62.1 all-gather.16

commit v3 on v2

v3 whole, which is shorter than its diff:
```python
import jax
import jax.numpy as jnp
from jax import lax
from jax.experimental import pallas as pl
from jax.experimental.pallas import tpu as pltpu
from jax.sharding import PartitionSpec as P

D = 768
H = 12
HD = 64
FF = 3072
NB = 64
GRID = 7
TEXT = 512
STEP = 10
VCH = 256
NBOX = 1024
VROWS = 17


MASKED = -1e30
CLIP = 0.005
BETA_ONE = 0.9
BETA_TWO = 0.999
EPSILON = 1e-08
DECAY = 0.01
RATES = (0.02, 0.03, 0.03, 0.04, 0.3, 0.05, 0.02)


def grid_boxes():
    cells = jnp.arange(GRID * GRID, dtype=jnp.int32)
    row_place = cells // GRID
    column_place = cells % GRID
    return jnp.stack(
        [
            column_place * 1000 // GRID,
            row_place * 1000 // GRID,
            (column_place + 1) * 1000 // GRID,
            (row_place + 1) * 1000 // GRID,
        ],
        -1,
    )


def adam_step(weight, grad, first, second, rate):
    first = BETA_ONE * first + (1.0 - BETA_ONE) * grad
    second = BETA_TWO * second + (1.0 - BETA_TWO) * grad * grad
    fixed_first = first / (1.0 - BETA_ONE**STEP)
    fixed_second = second / (1.0 - BETA_TWO**STEP)
    weight = weight - rate * (fixed_first / (jnp.sqrt(fixed_second) + EPSILON) + DECAY * weight)
    return (weight, first, second)


MESH = pl.DeviceIdType.MESH
LOW = jnp.bfloat16
WIDE = jnp.float32
LANES = 128
HALF = D // 2


def pad_up(count, unit):
    return (count + unit - 1) // unit * unit


def bits_of(count):
    return count.bit_length() - 1


def flip(index, bit, ring):
    if ring and bit == 1:
        return 3 - index
    return index + (1 - 2 * ((index // 2**bit) % 2)) * 2**bit


class Plan:
    def __init__(self, dp, mp):
        self.dp, self.mp = dp, mp
        self.proj = pad_up(D // dp, 16)
        self.places = pad_up(TEXT // dp, 16)
        self.visual = pad_up(VCH // dp, 16)
        self.box = NBOX // dp
        self.box_parts = 4 * (self.box // 32)
        self.places_at = 4 * self.proj
        self.visual_at = self.places_at + self.places
        self.box_at = self.visual_at + self.visual
        self.box_rows = 32 * ((self.box_parts + 6) // 6)
        self.shared = pad_up(self.box_at + self.box_rows, 32 * mp)

    def box_slot(self, part):
        return self.box_at + 32 * (part // 6), LANES * (part % 6)


def group_of(axis, index):
    return {axis: index}


def lanes_of(stream):
    return pl.ds(stream * HALF, HALF)


def ffn_slot(part, table_rows, ffn_rows, wide):
    return table_rows + part * wide // D * ffn_rows, part * wide % D


def row_tile(rows):
    return next(t for t in (48, 32, 16) if rows % t == 0)


def reduce_kernel(plan, table_rows, ffn_rows, refs):
    (
        table_in, proj_in, out_in, ffn_in, places_in, visual_in, boxes_in, small_in, tile_in,
        shared_out, split_out, tile_out,
        shared_acc, split_acc, shared_got, split_got, ring_got, ring_own, tile_mp, tile_dp,
        load_sem, send_sem, recv_sem, ring_send, ring_recv, tile_send, tile_recv,
    ) = refs
    dp, mp = plan.dp, plan.mp
    me, here = lax.axis_index("dp"), lax.axis_index("mp")
    depth, ring_depth = bits_of(dp), bits_of(mp)
    ring = mp == 4
    loads = []

    def load(source, target):
        loads.append(pltpu.make_async_copy(source, target, load_sem.at[len(loads)]))

    for part in range(4):
        source = proj_in.at[part] if part < 3 else out_in
        load(source, shared_acc.at[:, pl.ds(part * plan.proj, plan.proj)])
    load(places_in, shared_acc.at[:, pl.ds(plan.places_at, plan.places)])
    load(visual_in, shared_acc.at[:, pl.ds(plan.visual_at, plan.visual)])
    pieces_box = plan.box // 32
    for part in range(plan.box_parts):
        row, lane = plan.box_slot(part)
        load(
            boxes_in.at[part // pieces_box, :, pl.ds(32 * (part % pieces_box), 32)],
            shared_acc.at[:, pl.ds(row, 32), pl.ds(lane, LANES)],
        )
    row, lane = plan.box_slot(plan.box_parts)
    load(small_in, shared_acc.at[:, pl.ds(row, 32), pl.ds(lane, LANES)])
    load(table_in, split_acc.at[:, pl.ds(0, table_rows)])
    for part in range(2):
        wide = ffn_in.shape[3]
        row, lane = ffn_slot(part, table_rows, ffn_rows, wide)
        load(ffn_in.at[part], split_acc.at[:, pl.ds(row, ffn_rows), pl.ds(lane, wide)])
    for copy in loads:
        copy.start()

    barrier = pltpu.get_barrier_semaphore()
    for other in range(1, dp):
        pl.semaphore_signal(
            barrier, 1, device_id={"dp": lax.rem(me + other, dp)}, device_id_type=MESH
        )
    for other in range(1, mp):
        pl.semaphore_signal(
            barrier, 1, device_id={"mp": lax.rem(here + other, mp)}, device_id_type=MESH
        )
    pl.semaphore_wait(barrier, dp + mp - 2)
    for copy in loads:
        copy.wait()

    for part in range(plan.box_parts + 1, 6 * (plan.shared - plan.box_at) // 32):
        row, lane = plan.box_slot(part)
        shared_acc[:, pl.ds(row, 32), pl.ds(lane, LANES)] = jnp.zeros((dp, 32, LANES), LOW)

    orders = ([0] + list(range(depth - 1, 0, -1)), list(range(depth)))
    pieces = []
    for acc, got, rows in (
        (shared_acc, shared_got, plan.shared),
        (split_acc, split_got, split_acc.shape[1]),
    ):
        for part in range(2):
            pieces.append((acc, got, part * (rows // 2), rows // 2))

    def chunk(order, step, free, away):
        index = 0
        for place, bit in enumerate(order):
            mine = (me // 2**bit) % 2
            if place < step or (place == step and not away):
                index = index + mine * 2**bit
            elif place == step:
                index = index + (1 - mine) * 2**bit
            else:
                index = index + ((free >> (place - step - 1)) & 1) * 2**bit
        return index

    def slot_base(step):
        return sum(2 ** (depth - 1 - s) for s in range(step))

    def region(piece, stream, step):
        acc, got, first, rows = pieces[piece]
        count = 2 ** (depth - 1 - step)
        return got.at[pl.ds(slot_base(step), count), pl.ds(first, rows), lanes_of(stream)]

    def send(piece, stream, step):
        acc, got, first, rows = pieces[piece]
        order = orders[stream]
        for free in range(2 ** (depth - 1 - step)):
            pltpu.make_async_remote_copy(
                src_ref=acc.at[chunk(order, step, free, True), pl.ds(first, rows), lanes_of(stream)],
                dst_ref=got.at[slot_base(step) + free, pl.ds(first, rows), lanes_of(stream)],
                send_sem=send_sem.at[piece, stream, step],
                recv_sem=recv_sem.at[piece, stream, step],
                device_id={"dp": flip(me, order[step], False)},
                device_id_type=MESH,
            ).start()

    def wait_bytes(piece, stream, step, sem):
        where = region(piece, stream, step)
        pltpu.make_async_copy(where, where, sem.at[piece, stream, step]).wait()

    def finish(piece, stream, step):
        acc, got, first, rows = pieces[piece]
        order = orders[stream]
        wait_bytes(piece, stream, step, recv_sem)
        tile = row_tile(rows)
        last = step == depth - 1
        out, low_out = (shared_out, True) if acc is shared_acc else (split_out, False)
        for free in range(2 ** (depth - 1 - step)):
            kept = chunk(order, step, free, False)

            def body(index, carry):
                at = pl.multiple_of(first + index * tile, 16)
                where = pl.ds(at, tile)
                total = acc[kept, where, lanes_of(stream)].astype(WIDE) + got[
                    slot_base(step) + free, where, lanes_of(stream)
                ].astype(WIDE)
                if last and not low_out:
                    out[where, lanes_of(stream)] = total
                elif last:
                    ring_own[0, where, lanes_of(stream)] = total.astype(LOW)
                else:
                    acc[kept, where, lanes_of(stream)] = total.astype(LOW)
                return carry

            lax.fori_loop(0, rows // tile, body, 0)

    ring_orders = (list(range(ring_depth)), list(range(ring_depth - 1, -1, -1)))

    def ring_copy(stream, step):
        return pltpu.make_async_remote_copy(
            src_ref=ring_own.at[step, :, lanes_of(stream)],
            dst_ref=ring_got.at[step, :, lanes_of(stream)],
            send_sem=ring_send.at[stream, step],
            recv_sem=ring_recv.at[stream, step],
            device_id={"mp": flip(here, ring_orders[stream][step], ring)},
            device_id_type=MESH,
        )

    def ring_finish(stream, step):
        ring_copy(stream, step).wait_recv()
        rows = plan.shared
        tile = row_tile(rows)

        def body(index, carry):
            where = pl.ds(pl.multiple_of(index * tile, 16), tile)
            total = ring_own[step, where, lanes_of(stream)].astype(WIDE) + ring_got[
                step, where, lanes_of(stream)
            ].astype(WIDE)
            if step == ring_depth - 1:
                shared_out[where, lanes_of(stream)] = total
            else:
                ring_own[step + 1, where, lanes_of(stream)] = total.astype(LOW)
            return carry

        lax.fori_loop(0, rows // tile, body, 0)

    everything = [(piece, stream) for piece in range(len(pieces)) for stream in range(2)]
    for piece, stream in everything:
        send(piece, stream, 0)
    for step in range(depth):
        for piece, stream in everything:
            finish(piece, stream, step)
            if step < depth - 1:
                send(piece, stream, step + 1)
            elif piece == 1:
                ring_copy(stream, 0).start()
    for step in range(ring_depth):
        for stream in range(2):
            ring_finish(stream, step)
            if step < ring_depth - 1:
                ring_copy(stream, step + 1).start()

    def squares(ref, rows):
        tile = row_tile(rows)

        def body(index, total):
            values = ref[pl.ds(pl.multiple_of(index * tile, 16), tile), :]
            return total + jnp.sum((values * values).reshape(tile // 8, 8, D), 0)

        total = lax.fori_loop(0, rows // tile, body, jnp.zeros((8, D), WIDE))
        folded = total[:, 0:LANES]
        for part in range(1, D // LANES):
            folded = folded + total[:, part * LANES : (part + 1) * LANES]
        return folded

    folded = squares(shared_out, plan.shared) * (1.0 / mp) + squares(split_out, split_out.shape[0])
    own = lax.broadcasted_iota(jnp.int32, (8, LANES), 0)
    tile_mp[here, 0] = folded
    tile_mp[here, 1] = tile_in[...]

    def exchange(buffer, axis, index, count, base):
        copies = []
        for other in range(1, count):
            copies.append(
                pltpu.make_async_remote_copy(
                    src_ref=buffer.at[index],
                    dst_ref=buffer.at[index],
                    send_sem=tile_send.at[base + other],
                    recv_sem=tile_recv.at[base + other],
                    device_id={axis: lax.rem(index + other, count)},
                    device_id_type=MESH,
                )
            )
        for copy in copies:
            copy.start()
        for other in range(1, count):
            source = lax.rem(index + count - other, count)
            pltpu.make_async_copy(
                buffer.at[source], buffer.at[source], tile_recv.at[base + other]
            ).wait()
        return copies

    pending = exchange(tile_mp, "mp", here, mp, 0)
    total = tile_mp[0]
    for index in range(1, mp):
        total = total + tile_mp[index]
    tile_dp[me] = total
    pending = pending + exchange(tile_dp, "dp", me, dp, mp)
    total = tile_dp[0]
    for index in range(1, dp):
        total = total + tile_dp[index]
    tile_out[...] = total
    for copy in pending:
        copy.wait_send()
    for piece, stream in everything:
        for step in range(depth):
            wait_bytes(piece, stream, step, send_sem)
    for stream in range(2):
        for step in range(ring_depth):
            ring_copy(stream, step).wait_send()


def reduce_gradients(plan, table, proj, out, ffn, places, visual, boxes, small, tile):
    dp, mp = plan.dp, plan.mp
    table_rows, ffn_rows = table.shape[1], ffn.shape[2]
    split = table_rows + 2 * ffn_rows * ffn.shape[3] // D
    depth, ring_depth = bits_of(dp), bits_of(mp)
    loads = 4 + 2 + plan.box_parts + 1 + 1 + 2
    anywhere = pl.BlockSpec(memory_space=pl.ANY)
    vmem = pl.BlockSpec(memory_space=pltpu.VMEM)
    dma = pltpu.SemaphoreType.DMA

    def body(*refs):
        reduce_kernel(plan, table_rows, ffn_rows, refs)

    return pl.pallas_call(
        body,
        out_shape=(
            jax.ShapeDtypeStruct((plan.shared, D), WIDE),
            jax.ShapeDtypeStruct((split, D), WIDE),
            jax.ShapeDtypeStruct((2, 8, LANES), WIDE),
        ),
        in_specs=[anywhere] * 8 + [vmem],
        out_specs=(vmem, vmem, vmem),
        scratch_shapes=[
            pltpu.VMEM((dp, plan.shared, D), LOW),
            pltpu.VMEM((dp, split, D), LOW),
            pltpu.VMEM((dp - 1, plan.shared, D), LOW),
            pltpu.VMEM((dp - 1, split, D), LOW),
            pltpu.VMEM((ring_depth, plan.shared, D), LOW),
            pltpu.VMEM((ring_depth, plan.shared, D), LOW),
            pltpu.VMEM((mp, 2, 8, LANES), WIDE),
            pltpu.VMEM((dp, 2, 8, LANES), WIDE),
            dma((loads,)),
            dma((4, 2, depth)),
            dma((4, 2, depth)),
            dma((2, ring_depth)),
            dma((2, ring_depth)),
            dma((mp + dp,)),
            dma((mp + dp,)),
        ],
        compiler_params=pltpu.CompilerParams(
            collective_id=5, has_side_effects=True, vmem_limit_bytes=56 * 2**20
        ),
        name="reduce_gradients",
    )(table, proj, out, ffn, places, visual, boxes, small, tile)


def adam_kernel(plan, table_rows, ffn_rows, sizes, refs):
    shared_ref, split_ref, tile_ref = refs[:3]
    states, outs = refs[3:24], refs[24:45]
    totals = tile_ref[...]
    norm = jnp.sqrt(jnp.sum(totals[0], keepdims=True)) / totals[1, 1:2, 0:1]
    scale = jnp.minimum(1.0, CLIP / norm) / totals[1, 1:2, 0:1]

    def update(index, where, rows, grad_of):
        rate = RATES[index]
        weight, first, second = (ref[where] for ref in states[3 * index : 3 * index + 3])
        grad = grad_of * scale
        results = adam_step(weight, grad, first, second, rate)
        for ref, value in zip(outs[3 * index : 3 * index + 3], results):
            ref[where] = value

    def blocks(index, lead, source, at, rows, lane=0, wide=D):
        tile = next(t for t in (32, 24, 16, 8) if rows % t == 0)

        def body(step, carry):
            here = pl.multiple_of(step * tile, 8)
            where = (pl.ds(here, tile), slice(None))
            grad = source[pl.ds(pl.multiple_of(at + here, 8), tile), pl.ds(lane, wide)]
            update(index, where if lead is None else (lead,) + where, tile, grad)
            return carry

        lax.fori_loop(0, rows // tile, body, 0)

    for part in range(4):
        blocks(0, part, shared_ref, part * plan.proj, sizes[0])
    pieces_box = plan.box // 32
    for part in range(plan.box_parts):
        row, lane = plan.box_slot(part)
        grad = shared_ref[pl.ds(row, 32), pl.ds(lane, LANES)]
        update(1, (part // pieces_box, pl.ds(32 * (part % pieces_box), 32)), 32, grad)
    blocks(2, None, shared_ref, plan.places_at, sizes[2])
    blocks(3, None, shared_ref, plan.visual_at, sizes[3])
    row, lane = plan.box_slot(plan.box_parts)
    grad = shared_ref[pl.ds(row, 32), pl.ds(lane, LANES)]
    update(4, (slice(None), slice(None)), VROWS, grad[:VROWS, : sizes[4]])
    blocks(5, None, split_ref, 0, sizes[5])
    for part in range(2):
        wide = states[18].shape[2]
        row, lane = ffn_slot(part, table_rows, ffn_rows, wide)
        blocks(6, part, split_ref, row, sizes[6], lane, wide)


def adam_update(plan, table_rows, ffn_rows, shared, split, tile, states):
    sizes = (
        states[0].shape[1], 0, states[6].shape[0], states[9].shape[0], states[12].shape[1],
        states[15].shape[0], states[18].shape[1],
    )
    vmem = pl.BlockSpec(memory_space=pltpu.VMEM)

    def body(*refs):
        adam_kernel(plan, table_rows, ffn_rows, sizes, refs)

    return pl.pallas_call(
        body,
        out_shape=tuple(jax.ShapeDtypeStruct(part.shape, WIDE) for part in states),
        in_specs=[vmem] * 24,
        out_specs=(vmem,) * 21,
        compiler_params=pltpu.CompilerParams(vmem_limit_bytes=48 * 2**20),
        name="adam_update",
    )(shared, split, tile, *states)


def combos(index, bits, ring):
    found = [index]
    for bit in bits:
        found = found + [flip(one, bit, ring) for one in found]
    return found


class Ring:
    def __init__(self, mp, sems):
        self.mp, self.here, self.ring = mp, lax.axis_index("mp"), mp == 4
        self.send, self.recv = sems
        depth = bits_of(mp)
        self.depth = depth
        self.orders = (list(range(depth)), list(range(depth - 1, -1, -1)))
        self.started = []

    def barrier(self):
        barrier = pltpu.get_barrier_semaphore()
        for other in range(1, self.mp):
            pl.semaphore_signal(
                barrier, 1, device_id={"mp": lax.rem(self.here + other, self.mp)},
                device_id_type=MESH,
            )
        pl.semaphore_wait(barrier, self.mp - 1)

    def copy(self, source, target, number, stream, index, peer):
        made = pltpu.make_async_remote_copy(
            src_ref=source, dst_ref=target,
            send_sem=self.send.at[number, stream, index],
            recv_sem=self.recv.at[number, stream, index],
            device_id={"mp": peer}, device_id_type=MESH,
        )
        return made

    def gather_start(self, buffer, number, stream, step):
        order = self.orders[stream]
        peer = flip(self.here, order[step], self.ring)
        for place, slot in enumerate(combos(self.here, order[:step], self.ring)):
            part = buffer.at[slot, :, lanes_of(stream)]
            made = self.copy(part, part, number, stream, 2**step - 1 + place, peer)
            made.start()
            self.started.append(made)

    def gather_wait(self, buffer, number, stream, step):
        order = self.orders[stream]
        peer = flip(self.here, order[step], self.ring)
        for place, slot in enumerate(combos(peer, order[:step], self.ring)):
            part = buffer.at[slot, :, lanes_of(stream)]
            self.copy(part, part, number, stream, 2**step - 1 + place, peer).wait_recv()

    def gather(self, buffer, number):
        for stream in range(2):
            self.gather_start(buffer, number, stream, 0)
        for step in range(self.depth):
            for stream in range(2):
                self.gather_wait(buffer, number, stream, step)
                if step < self.depth - 1:
                    self.gather_start(buffer, number, stream, step + 1)

    def base(self, step):
        return sum(2 ** (self.depth - 1 - s) for s in range(step))

    def reduce_start(self, buffer, got, number, stream, step):
        order = self.orders[stream]
        peer = flip(self.here, order[step], self.ring)
        for place, slot in enumerate(combos(peer, order[step + 1 :], self.ring)):
            index = self.base(step) + place
            made = self.copy(
                buffer.at[slot, :, lanes_of(stream)],
                got.at[index, :, lanes_of(stream)],
                number, stream, index, peer,
            )
            made.start()
            self.started.append(made)

    def reduce_wait(self, buffer, got, number, stream, step):
        order = self.orders[stream]
        peer = flip(self.here, order[step], self.ring)
        for place, slot in enumerate(combos(self.here, order[step + 1 :], self.ring)):
            index = self.base(step) + place
            part = got.at[index, :, lanes_of(stream)]
            self.copy(part, part, number, stream, index, peer).wait_recv()
            where = (slot, slice(None), lanes_of(stream))
            total = buffer[where].astype(WIDE) + got[index, :, lanes_of(stream)].astype(WIDE)
            buffer[where] = total.astype(buffer.dtype)

    def reduce_begin(self, buffer, got, number):
        for stream in range(2):
            self.reduce_start(buffer, got, number, stream, 0)

    def reduce_rest(self, buffer, got, number, between=()):
        between = list(between)
        for step in range(self.depth):
            if between:
                between.pop(0)()
            for stream in range(2):
                self.reduce_wait(buffer, got, number, stream, step)
                if step < self.depth - 1:
                    self.reduce_start(buffer, got, number, stream, step + 1)
        for rest in between:
            rest()

    def finish(self):
        for made in self.started:
            made.wait_send()


def mm(left, right, dims):
    return lax.dot_general(left, right, (dims, ((), ())), preferred_element_type=WIDE)


NN, NT, TN = ((1,), (0,)), ((1,), (1,)), ((0,), (0,))


def norm_rows(value):
    centred = value - jnp.mean(value, -1, keepdims=True)
    scale = lax.rsqrt(jnp.mean(centred * centred, -1, keepdims=True) + 1e-05)
    return centred * scale, scale


def norm_back(grad, plain, scale, gain):
    inner = grad * gain
    return scale * (
        inner
        - jnp.mean(inner, -1, keepdims=True)
        - plain * jnp.mean(inner * plain, -1, keepdims=True)
    )


def column_sum(value):
    return jnp.sum(value, 0, keepdims=True)


def head_kernel(mp, refs):
    (
        mixed_ref, zero_ref, out_weight, small_ref, bias_ref, ffn_ref, table_ref, label_ref,
        valid_ref,
        grad_zero_ref, grad_mixed_ref, grad_out_ref, grad_ffn_ref, grad_table_ref, rows_ref,
        bias_out, sums_ref,
        ffn, table, one, picked, down, sums_two, grad_picked, grad_one, got_two, got_picked,
        got_one, logits, low_logits, stats, load_sem, send_sem, recv_sem, stat_send, stat_recv,
    ) = refs
    ring = Ring(mp, (send_sem, recv_sem))
    here = ring.here
    slots = mixed_ref.shape[0]
    group = slots * mp
    load_ffn = pltpu.make_async_copy(ffn_ref, ffn, load_sem.at[0])
    load_table = pltpu.make_async_copy(table_ref, table, load_sem.at[1])
    load_ffn.start()
    load_table.start()
    ring.barrier()
    row = lambda index: small_ref[index : index + 1, :]

    out = mm(mixed_ref[...], out_weight[...], NN) + row(4)
    plain_one, scale_one = norm_rows(zero_ref[...] + out)
    normed_one = plain_one * row(5) + row(6)
    one[here] = normed_one.astype(LOW)
    ring.gather(one, 0)
    load_ffn.wait()
    hidden = ffn.shape[2]
    group_one = one[...].reshape(group, D)
    before = mm(group_one, ffn[0], NN) + bias_ref[...]
    erf_part = 0.5 * (1.0 + lax.erf(before * (0.5**0.5)))
    active = (before * erf_part).astype(LOW)
    slope = erf_part + before * jnp.exp(-0.5 * before * before) * 0.3989422804014327
    sums_two[...] = mm(active, ffn[1], NT).astype(sums_two.dtype).reshape(mp, slots, D)
    ring.reduce_begin(sums_two, got_two, 1)
    load_table.wait()
    ring.reduce_rest(sums_two, got_two, 1)
    plain_two, scale_two = norm_rows(normed_one + (sums_two[here].astype(WIDE) + row(7)))
    picked[here] = (plain_two * row(8) + row(9)).astype(LOW)
    ring.gather(picked, 2)

    group_picked = picked[...].reshape(group, D)
    vocab = table.shape[0]
    tile = next(t for t in (480, 512, 256, 128) if vocab % t == 0)
    tiles = vocab // tile
    label = label_ref[...] - here * vocab
    valid = valid_ref[...].astype(WIDE)

    def forward(index, carry):
        highest, total, target = carry
        where = pl.ds(pl.multiple_of(index * tile, 16), tile)
        values = mm(table[where, :], group_picked, NT)
        logits[where, :] = values
        higher = jnp.maximum(highest, jnp.max(values, 0, keepdims=True))
        total = total * jnp.exp(highest - higher) + column_sum(jnp.exp(values - higher))
        word = lax.broadcasted_iota(jnp.int32, (tile, group), 0) + index * tile
        target = target + column_sum(jnp.where(word == label, values, 0.0))
        return higher, total, target

    blank = jnp.zeros((1, group), WIDE)
    highest, total, target = lax.fori_loop(0, tiles, forward, (blank - 1e30, blank, blank))
    stats[here, 0:1, 0:group] = highest
    stats[here, 1:2, 0:group] = total
    stats[here, 2:3, 0:group] = target
    stat_copies = []
    for other in range(1, mp):
        made = pltpu.make_async_remote_copy(
            src_ref=stats.at[here], dst_ref=stats.at[here],
            send_sem=stat_send.at[other], recv_sem=stat_recv.at[other],
            device_id={"mp": lax.rem(here + other, mp)}, device_id_type=MESH,
        )
        made.start()
        stat_copies.append(made)
    for other in range(1, mp):
        source = lax.rem(here + mp - other, mp)
        pltpu.make_async_copy(stats.at[source], stats.at[source], stat_recv.at[other]).wait()
    highest = stats[0, 0:1, 0:group]
    for index in range(1, mp):
        highest = jnp.maximum(highest, stats[index, 0:1, 0:group])
    total, target = blank, blank
    for index in range(mp):
        total = total + stats[index, 1:2, 0:group] * jnp.exp(stats[index, 0:1, 0:group] - highest)
        target = target + stats[index, 2:3, 0:group]
    log_rows = highest + jnp.log(total)
    place = lax.broadcasted_iota(jnp.int32, (1, group), 1)
    own = (place >= here * slots) & (place < (here + 1) * slots)
    loss = jnp.sum(jnp.where(own, valid * (log_rows - target), 0.0), -1, keepdims=True)
    count = jnp.sum(jnp.where(own, valid, 0.0), -1, keepdims=True)
    first_lane = lax.broadcasted_iota(jnp.int32, (8, LANES), 1) == 0
    first_row = lax.broadcasted_iota(jnp.int32, (8, LANES), 0)
    sums_ref[...] = jnp.where(
        first_lane & (first_row == 0), loss, jnp.where(first_lane & (first_row == 1), count, 0.0)
    )

    def backward(index, grad):
        where = pl.ds(pl.multiple_of(index * tile, 16), tile)
        word = lax.broadcasted_iota(jnp.int32, (tile, group), 0) + index * tile
        hit = jnp.where(word == label, 1.0, 0.0)
        values = ((jnp.exp(logits[where, :] - log_rows) - hit) * valid).astype(LOW)
        low_logits[where, :] = values
        return grad + mm(values, table[where, :], TN)

    grad = lax.fori_loop(0, tiles, backward, jnp.zeros((group, D), WIDE))
    grad_picked[...] = grad.astype(grad_picked.dtype).reshape(mp, slots, D)

    def table_part(first, last):
        def run():
            def body(index, carry):
                where = pl.ds(pl.multiple_of(index * tile, 16), tile)
                grad_table_ref[where, :] = mm(low_logits[where, :], group_picked, NN).astype(LOW)
                return carry

            lax.fori_loop(first, last, body, 0)

        return run

    ring.reduce_begin(grad_picked, got_picked, 3)
    middle = tiles // 2
    ring.reduce_rest(
        grad_picked, got_picked, 3, [table_part(0, middle), table_part(middle, tiles)]
    )
    grad_two = grad_picked[here].astype(WIDE)
    rows_ref[8:9, :] = column_sum(grad_two * plain_two)
    rows_ref[9:10, :] = column_sum(grad_two)
    grad_sum_two = norm_back(grad_two, plain_two, scale_two, row(8))
    low_two = grad_sum_two.astype(LOW)
    rows_ref[7:8, :] = column_sum(low_two.astype(WIDE))
    down[here] = low_two
    ring.gather(down, 4)
    group_down = down[...].reshape(group, D)
    grad_active = mm(group_down, ffn[1], NN)
    grad_before = (grad_active * slope).astype(LOW)
    grad_one[...] = mm(grad_before, ffn[0], NT).astype(grad_one.dtype).reshape(mp, slots, D)

    def up_part():
        grad_ffn_ref[0] = mm(group_one, grad_before, TN).astype(LOW)
        bias_out[...] = column_sum(grad_before.astype(WIDE))

    def down_part():
        grad_ffn_ref[1] = mm(group_down, active, TN).astype(LOW)

    ring.reduce_begin(grad_one, got_one, 5)
    ring.reduce_rest(grad_one, got_one, 5, [up_part, down_part])
    grad = grad_sum_two + grad_one[here].astype(WIDE)
    rows_ref[5:6, :] = column_sum(grad * plain_one)
    rows_ref[6:7, :] = column_sum(grad)
    grad = norm_back(grad, plain_one, scale_one, row(5))
    low = grad.astype(LOW)
    rows_ref[4:5, :] = column_sum(low.astype(WIDE))
    grad_zero_ref[...] = grad
    grad_mixed_ref[...] = mm(low, out_weight[...], NT).astype(LOW)
    grad_out_ref[...] = mm(mixed_ref[...], low, TN).astype(LOW)
    for index in list(range(4)) + list(range(10, 16)):
        rows_ref[index : index + 1, :] = jnp.zeros((1, D), WIDE)
    ring.finish()
    for made in stat_copies:
        made.wait_send()


def head_step(mp, mixed, zero, out_weight, small, bias, ffn, table, label, valid):
    slots, hidden, vocab = mixed.shape[0], ffn.shape[2], table.shape[0]
    group = slots * mp
    wide_group = pad_up(group, LANES)
    vmem = pl.BlockSpec(memory_space=pltpu.VMEM)
    anywhere = pl.BlockSpec(memory_space=pl.ANY)
    dma = pltpu.SemaphoreType.DMA
    exchanged = [pltpu.VMEM((mp, slots, D), LOW)] * 6
    got = [pltpu.VMEM((mp - 1, slots, D), LOW)] * 3

    def body(*refs):
        head_kernel(mp, refs)

    return pl.pallas_call(
        body,
        out_shape=(
            jax.ShapeDtypeStruct((slots, D), WIDE),
            jax.ShapeDtypeStruct((slots, D), LOW),
            jax.ShapeDtypeStruct((D, D), LOW),
            jax.ShapeDtypeStruct((2, D, hidden), LOW),
            jax.ShapeDtypeStruct((vocab, D), LOW),
            jax.ShapeDtypeStruct((16, D), WIDE),
            jax.ShapeDtypeStruct((1, hidden), WIDE),
            jax.ShapeDtypeStruct((8, LANES), WIDE),
        ),
        in_specs=[vmem] * 5 + [anywhere] * 2 + [vmem] * 2,
        out_specs=(vmem,) * 8,
        scratch_shapes=[
            pltpu.VMEM((2, D, hidden), LOW),
            pltpu.VMEM((vocab, D), LOW),
            *exchanged,
            *got,
            pltpu.VMEM((vocab, group), WIDE),
            pltpu.VMEM((vocab, group), LOW),
            pltpu.VMEM((mp, 8, wide_group), WIDE),
            dma((2,)),
            dma((6, 2, mp - 1)),
            dma((6, 2, mp - 1)),
            dma((mp,)),
            dma((mp,)),
        ],
        compiler_params=pltpu.CompilerParams(
            collective_id=3, has_side_effects=True, vmem_limit_bytes=56 * 2**20
        ),
        name="head_step",
    )(mixed, zero, out_weight, small, bias, ffn, table, label, valid)


ROWS = 576
KINDS = ((6, 3), (0, 4), (3, 4))


def token_info(text_box, segments, alive_text):
    boxes = jnp.concatenate([text_box, grid_boxes()], 0)
    visual = GRID * GRID
    places = jnp.concatenate([jnp.arange(TEXT), jnp.arange(visual)]).astype(jnp.int32)
    owner = jnp.concatenate([segments, jnp.full((visual,), -1, jnp.int32)])
    alive = jnp.concatenate([alive_text, jnp.ones((visual,), jnp.int32)])
    columns = [
        boxes[:, 0], boxes[:, 1], boxes[:, 2], boxes[:, 3], boxes[:, 3] - boxes[:, 1],
        boxes[:, 2] - boxes[:, 0], places, owner, alive,
    ]
    rows = jnp.stack(columns + [jnp.zeros_like(places)] * 7)
    return jnp.pad(rows, ((0, 0), (0, ROWS - TEXT - visual)))


def edge_rows(rel_low):
    table = jnp.transpose(rel_low.reshape(3, NB, H), (0, 2, 1)).astype(WIDE)
    rows = jnp.pad(table, ((0, 0), (0, 0), (NB // 2, NB // 2)), mode="edge")
    return jnp.pad(rows.reshape(3 * H, 2 * NB), ((0, 4), (0, 0)))


def edge_rows_back(grad):
    grad = grad[: 3 * H].reshape(3, H, 2 * NB)
    half = NB // 2
    low = jnp.sum(grad[..., : half + 1], -1, keepdims=True)
    high = jnp.sum(grad[..., 3 * half - 1 :], -1, keepdims=True)
    table = jnp.concatenate([low, grad[..., half + 1 : 3 * half - 1], high], -1)
    return jnp.transpose(table, (0, 2, 1)).reshape(3 * NB * H)


def key_hot(rows_ref, kind):
    column, shift = KINDS[kind]
    coarse_row = jnp.right_shift(rows_ref[column : column + 1, :], shift)
    place = lax.broadcasted_iota(jnp.int32, (2 * NB, ROWS), 0)
    first = jnp.where(place == coarse_row, 1.0, 0.0).astype(LOW)
    second = jnp.where(place == coarse_row + NB, 1.0, 0.0).astype(LOW)
    return first, second


def below_of(rows_ref, slot_ref, kind):
    column, shift = KINDS[kind]
    mask = 2**shift - 1
    rest_key = jnp.bitwise_and(rows_ref[column : column + 1, :], mask)
    rest_slot = jnp.bitwise_and(slot_ref[:, column : column + 1], mask)
    return rest_key < rest_slot


def take_slots(slots, pos_ref, pairs):
    def body(index, carry):
        at = pos_ref[index]
        for source, target in pairs:
            target[pl.ds(index, 1), :] = source[pl.ds(at, 1), :]
        return carry

    lax.fori_loop(0, slots, body, 0)


def half_mask(rows):
    slots = rows // 2
    row = lax.broadcasted_iota(jnp.int32, (rows, LANES), 0)
    lane = lax.broadcasted_iota(jnp.int32, (rows, LANES), 1)
    return (row < slots) == (lane < HD)


def pair_rows(value):
    both = jnp.concatenate([value, value], 0)
    return jnp.where(half_mask(both.shape[0]), both, jnp.zeros((), both.dtype))


def pair_lanes(value):
    slots = value.shape[0] // 2
    lane = lax.broadcasted_iota(jnp.int32, (slots, LANES), 1)
    return jnp.where(lane < HD, value[:slots], value[slots:])


def front_kernel(
    pos_ref, word_ref, features_ref, places_ref, boxes_ref, visual_ref, small_ref, edges_ref,
    columns_ref, rows_ref, weights_ref,
    mixed_ref, zero_ref, zero_low_ref, low_ref, plain_ref, scale_ref, query_ref, key_ref,
    value_ref, shares_ref,
    normed_ref, slot_ref, bias_ref, spread_ref, stacked_ref,
):
    slots = mixed_ref.shape[0]
    row = lambda index: small_ref[index : index + 1, :]
    tile = 96
    lookups = (0, 1, 0, 1, 2, 3)

    normed_ref[0:TEXT, :] = word_ref[...].astype(WIDE) + places_ref[...].astype(WIDE)
    normed_ref[TEXT:ROWS, :] = mm(features_ref[...], visual_ref[...], NN) + places_ref[
        0 : ROWS - TEXT, :
    ].astype(WIDE)

    def embed(index, carry):
        where = pl.ds(pl.multiple_of(index * tile, 16), tile)
        place = lax.broadcasted_iota(jnp.int32, (tile, NBOX), 1)
        found = []
        for column, table in enumerate(lookups):
            hot = jnp.where(place == columns_ref[where, column : column + 1], 1.0, 0.0).astype(LOW)
            found.append(mm(hot, boxes_ref[table], NN))
        embedded = normed_ref[where, :] + jnp.concatenate(found, -1)
        plain, scale = norm_rows(embedded)
        normed = plain * row(0) + row(1)
        plain_ref[where, :] = plain
        scale_ref[where, :] = scale
        normed_ref[where, :] = normed
        low_ref[where, :] = normed.astype(LOW)
        return carry

    lax.fori_loop(0, ROWS // tile, embed, 0)
    take_slots(slots, pos_ref, ((normed_ref, zero_ref), (columns_ref, slot_ref)))
    low = low_ref[...]
    zero_low = zero_ref[...].astype(LOW)
    zero_low_ref[...] = zero_low
    query_ref[...] = (mm(zero_low, weights_ref[0], NN) + row(2)).astype(LOW)
    key_ref[...] = mm(low, weights_ref[1], NN).astype(LOW)
    value_ref[...] = (mm(low, weights_ref[2], NN) + row(3)).astype(LOW)

    lane = lax.broadcasted_iota(jnp.int32, (NB, LANES), 1)
    for kind in range(3):
        column, shift = KINDS[kind]
        for head in range(H):
            edge = jnp.broadcast_to(edges_ref[kind * H + head : kind * H + head + 1, :], (NB, LANES))
            near = pltpu.roll(edge, NB, 1, stride=1, stride_axis=0)
            far = pltpu.roll(edge, 1, 1, stride=1, stride_axis=0)
            spread_ref[:, head * LANES : (head + 1) * LANES] = jnp.where(
                lane < NB, near, far
            ).astype(LOW)
        coarse_slot = jnp.right_shift(slot_ref[:, column : column + 1], shift)
        place = lax.broadcasted_iota(jnp.int32, (slots, NB), 1)
        hot = jnp.where(place == coarse_slot, 1.0, 0.0).astype(LOW)
        wide = mm(hot, spread_ref[...], NN).astype(LOW)
        for head in range(H):
            stacked_ref[head * slots : (head + 1) * slots, :] = wide[
                :, head * LANES : (head + 1) * LANES
            ]
        first, second = key_hot(rows_ref, kind)
        below = below_of(rows_ref, slot_ref, kind)

        def add(head, carry):
            where = pl.ds(pl.multiple_of(head * 2 * slots, 16), 2 * slots)
            rows = stacked_ref[where, :]
            both = jnp.concatenate([below, below], 0)
            found = jnp.where(both, mm(rows, second, NN), mm(rows, first, NN))
            bias_ref[where, :] = found if kind == 0 else bias_ref[where, :] + found
            return carry

        lax.fori_loop(0, H // 2, add, 0)

    owner = rows_ref[7:8, :]
    allowed = ((slot_ref[:, 7:8] == owner) | (owner < 0)) & (rows_ref[8:9, :] > 0)
    allowed = jnp.concatenate([allowed, allowed], 0)
    for pair in range(H // 2):
        lanes = slice(pair * LANES, (pair + 1) * LANES)
        rows = slice(pair * 2 * slots, (pair + 1) * 2 * slots)
        scores = mm(pair_rows(query_ref[:, lanes]), key_ref[:, lanes], NT) * 0.125
        scores = jnp.where(allowed, scores + bias_ref[rows, :], MASKED)
        powers = jnp.exp(scores - jnp.max(scores, -1, keepdims=True))
        shares = powers / jnp.sum(powers, -1, keepdims=True)
        shares_ref[rows, :] = shares
        mixed_ref[:, lanes] = pair_lanes(mm(shares.astype(LOW), value_ref[:, lanes], NN)).astype(LOW)


def front_step(pos, word, features, places, boxes, visual, small, edges, columns, rows, weights):
    slots = pos.shape[0]
    vmem = pl.BlockSpec(memory_space=pltpu.VMEM)
    shape = jax.ShapeDtypeStruct
    return pl.pallas_call(
        front_kernel,
        out_shape=(
            shape((slots, D), LOW), shape((slots, D), WIDE), shape((slots, D), LOW),
            shape((ROWS, D), LOW), shape((ROWS, D), WIDE), shape((ROWS, 1), WIDE),
            shape((slots, D), LOW), shape((ROWS, D), LOW), shape((ROWS, D), LOW),
            shape((H * slots, ROWS), WIDE),
        ),
        in_specs=[pl.BlockSpec(memory_space=pltpu.SMEM)] + [vmem] * 10,
        out_specs=(vmem,) * 10,
        scratch_shapes=[
            pltpu.VMEM((ROWS, D), WIDE),
            pltpu.VMEM((slots, 16), jnp.int32),
            pltpu.VMEM((H * slots, ROWS), WIDE),
            pltpu.VMEM((NB, H * LANES), LOW),
            pltpu.VMEM((H * slots, LANES), LOW),
        ],
        compiler_params=pltpu.CompilerParams(vmem_limit_bytes=56 * 2**20),
        name="front_step",
    )(pos, word, features, places, boxes, visual, small, edges, columns, rows, weights)


def back_kernel(
    pos_ref, grad_zero_ref, grad_mixed_ref, shares_ref, query_ref, key_ref, value_ref,
    zero_low_ref, low_ref, plain_ref, scale_ref, features_ref, small_ref, columns_ref, rows_ref,
    weights_ref,
    word_out, places_out, boxes_out, visual_out, weights_out, edges_out, sums_out,
    slot_ref, score_ref, grad_query, grad_key, grad_value, grad_rows, turned_ref, grad_slot,
):
    slots = grad_zero_ref.shape[0]
    take_slots(slots, pos_ref, ((columns_ref, slot_ref),))
    for pair in range(H // 2):
        lanes = slice(pair * LANES, (pair + 1) * LANES)
        rows = slice(pair * 2 * slots, (pair + 1) * 2 * slots)
        grad_mixed = pair_rows(grad_mixed_ref[:, lanes])
        shares = shares_ref[rows, :]
        grad_value[:, lanes] = mm(shares.astype(LOW), grad_mixed, TN).astype(LOW)
        grad_shares = mm(grad_mixed, value_ref[:, lanes], NT)
        scores = shares * (grad_shares - jnp.sum(shares * grad_shares, -1, keepdims=True))
        scores = scores.astype(LOW)
        score_ref[rows, :] = scores
        grad_query[:, lanes] = pair_lanes(mm(scores, key_ref[:, lanes], NN) * 0.125).astype(LOW)
        grad_key[:, lanes] = (mm(scores, pair_rows(query_ref[:, lanes]), TN) * 0.125).astype(LOW)

    lane = lax.broadcasted_iota(jnp.int32, (NB, LANES), 1)
    for kind in range(3):
        column, shift = KINDS[kind]
        first, second = key_hot(rows_ref, kind)
        below = below_of(rows_ref, slot_ref, kind)
        coarse_slot = jnp.right_shift(slot_ref[:, column : column + 1], shift)
        place = lax.broadcasted_iota(jnp.int32, (slots, NB), 1)
        hot = jnp.where(place == NB - 1 - coarse_slot, 1.0, 0.0).astype(LOW)

        def collect(pair, carry):
            where = pl.ds(pl.multiple_of(pair * 2 * slots, 16), 2 * slots)
            both = jnp.concatenate([below, below], 0)
            scores = score_ref[where, :]
            none = jnp.zeros((), LOW)
            found = mm(jnp.where(both, none, scores), first, NT) + mm(
                jnp.where(both, scores, none), second, NT
            )
            turned_ref[where, :] = found.astype(LOW)
            return carry

        lax.fori_loop(0, H // 2, collect, 0)
        for head in range(H):
            part = mm(hot, turned_ref[head * slots : (head + 1) * slots, :], TN)
            near = pltpu.roll(jnp.where(lane < NB, part, 0.0), 1, 1, stride=1, stride_axis=0)
            far = pltpu.roll(jnp.where(lane < NB, 0.0, part), NB, 1, stride=1, stride_axis=0)
            edges_out[kind * H + head : kind * H + head + 1, :] = column_sum(near + far)
    edges_out[3 * H :, :] = jnp.zeros((4, LANES), WIDE)

    low = low_ref[...]
    weights_out[0] = mm(zero_low_ref[...], grad_query[...], TN).astype(LOW)
    weights_out[1] = mm(low, grad_key[...], TN).astype(LOW)
    weights_out[2] = mm(low, grad_value[...], TN).astype(LOW)
    sums_out[2:3, :] = column_sum(grad_query[...].astype(WIDE))
    sums_out[3:4, :] = column_sum(grad_value[...].astype(WIDE))
    sums_out[4:8, :] = jnp.zeros((4, D), WIDE)
    grad_rows[...] = mm(grad_key[...], weights_ref[1], NT) + mm(grad_value[...], weights_ref[2], NT)
    grad_slot[...] = grad_zero_ref[...] + mm(grad_query[...], weights_ref[0], NT)

    def put(index, carry):
        at = pl.ds(pos_ref[index], 1)
        grad_rows[at, :] = grad_rows[at, :] + grad_slot[pl.ds(index, 1), :]
        return carry

    lax.fori_loop(0, slots, put, 0)
    gain = small_ref[0:1, :]
    tile = 96

    def normed_back(index, carry):
        where = pl.ds(pl.multiple_of(index * tile, 16), tile)
        grad, plain = grad_rows[where, :], plain_ref[where, :]
        grad_rows[where, :] = norm_back(grad, plain, scale_ref[where, :], gain)
        return carry[0] + column_sum(grad * plain), carry[1] + column_sum(grad)

    blank = jnp.zeros((1, D), WIDE)
    gains, shifts = lax.fori_loop(0, ROWS // tile, normed_back, (blank, blank))
    sums_out[0:1, :] = gains
    sums_out[1:2, :] = shifts
    grad_low = grad_rows[...].astype(LOW)
    word_out[...] = grad_low[0:TEXT, :]
    extra = ROWS - TEXT
    places_out[...] = grad_rows[0:TEXT, :].astype(LOW)
    places_out[0:extra, :] = (grad_rows[0:extra, :] + grad_rows[TEXT:ROWS, :]).astype(LOW)
    visual_out[...] = mm(features_ref[...], grad_low[TEXT:ROWS, :], TN).astype(LOW)
    block = 256

    def table(index, carry):
        where = pl.ds(pl.multiple_of(index * block, 16), block)
        place = lax.broadcasted_iota(jnp.int32, (block, ROWS), 0) + index * block
        found = []
        for column in range(6):
            hot = jnp.where(place == rows_ref[column : column + 1, :], 1.0, 0.0).astype(LOW)
            found.append(mm(hot, grad_low[:, column * LANES : (column + 1) * LANES], NN))
        boxes_out[0, where, :] = (found[0] + found[2]).astype(LOW)
        boxes_out[1, where, :] = (found[1] + found[3]).astype(LOW)
        boxes_out[2, where, :] = found[4].astype(LOW)
        boxes_out[3, where, :] = found[5].astype(LOW)
        return carry

    lax.fori_loop(0, NBOX // block, table, 0)


def back_step(
    pos, grad_zero, grad_mixed, shares, query, key, value, zero_low, low, plain, scale, features,
    small, columns, rows, weights,
):
    slots = pos.shape[0]
    vmem = pl.BlockSpec(memory_space=pltpu.VMEM)
    shape = jax.ShapeDtypeStruct
    return pl.pallas_call(
        back_kernel,
        out_shape=(
            shape((TEXT, D), LOW), shape((TEXT, D), LOW), shape((4, NBOX, LANES), LOW),
            shape((VCH, D), LOW), shape((3, D, D), LOW), shape((3 * H + 4, LANES), WIDE),
            shape((8, D), WIDE),
        ),
        in_specs=[pl.BlockSpec(memory_space=pltpu.SMEM)] + [vmem] * 15,
        out_specs=(vmem,) * 7,
        scratch_shapes=[
            pltpu.VMEM((slots, 16), jnp.int32),
            pltpu.VMEM((H * slots, ROWS), LOW),
            pltpu.VMEM((slots, D), LOW),
            pltpu.VMEM((ROWS, D), LOW),
            pltpu.VMEM((ROWS, D), LOW),
            pltpu.VMEM((ROWS, D), WIDE),
            pltpu.VMEM((H * slots, LANES), LOW),
            pltpu.VMEM((slots, D), WIDE),
        ],
        compiler_params=pltpu.CompilerParams(vmem_limit_bytes=56 * 2**20),
        name="back_step",
    )(
        pos, grad_zero, grad_mixed, shares, query, key, value, zero_low, low, plain, scale,
        features, small, columns, rows, weights,
    )


def on_device(
    tokens, text_box, segments, alive_text, features, mask_pos, mask_label, mask_valid, *states
):
    (projections, box_tables, position_table, visual_proj, small_params, word_table, feedforward) = (
        states[::3]
    )
    dp, mp = lax.axis_size("dp"), lax.axis_size("mp")
    plan = Plan(dp, mp)

    def gathered(part, axis):
        return lax.all_gather(part.astype(LOW), "dp", axis=axis, tiled=True)

    work_table = gathered(word_table, 0)
    work_small = gathered(small_params, 1)
    work_boxes = gathered(box_tables, 1)
    work_places = gathered(position_table, 0)
    work_visual = gathered(visual_proj, 0)
    work_proj = gathered(projections, 1)
    work_ffn = gathered(feedforward, 1)
    model_index = lax.axis_index("mp")
    vocab_shard, hidden_shard = work_table.shape[0], work_ffn.shape[2]
    small_float = work_small.astype(WIDE)

    local_ids = tokens - model_index * vocab_shard
    inside = (local_ids >= 0) & (local_ids < vocab_shard)
    safe_index = jnp.clip(local_ids, 0, vocab_shard - 1)
    partial_word = jnp.where(
        inside[..., None], jnp.take(work_table, safe_index, axis=0), jnp.zeros((), LOW)
    )
    word = lax.psum_scatter(partial_word, "mp", scatter_dimension=0, tiled=True)[0]

    info = token_info(text_box[0], segments[0], alive_text[0])
    columns = info.T
    visual_rows = jnp.pad(features, ((0, ROWS - TEXT - features.shape[0]), (0, 0)))
    edges = edge_rows(work_small[10 + FF // D : 13 + FF // D].reshape(3 * NB, H))
    (
        mixed, slot_zero, slot_low, normed_low, plain, scale, queries, keys, values, shares,
    ) = front_step(
        mask_pos, word, visual_rows, work_places, work_boxes, work_visual, small_float, edges,
        columns, info, work_proj[:3],
    )
    ffn_bias_full = small_float[10 : 10 + FF // D].reshape(1, -1)
    ffn_bias = lax.dynamic_slice_in_dim(ffn_bias_full, model_index * hidden_shard, hidden_shard, 1)
    (
        grad_slot, grad_mixed, grad_out_weight, grad_ffn, grad_table, head_rows, grad_ffn_bias,
        own_tile,
    ) = head_step(
        mp, mixed, slot_zero, work_proj[3], small_float, ffn_bias, work_ffn, work_table,
        mask_label[None, :], mask_valid[None, :],
    )
    grad_word, grad_places, grad_boxes, grad_visual, grad_in_weight, grad_edges, front_rows = (
        back_step(
            mask_pos, grad_slot, grad_mixed, shares, queries, keys, values, slot_low, normed_low,
            plain, scale, visual_rows, small_float, columns, info, work_proj[:3],
        )
    )
    bias_full = lax.dynamic_update_slice_in_dim(
        jnp.zeros((FF,), WIDE), grad_ffn_bias[0], model_index * hidden_shard, 0
    ).reshape(FF // D, D)
    grad_small = jnp.concatenate(
        [front_rows[:4], head_rows[4:10], bias_full, edge_rows_back(grad_edges).reshape(3, D)], 0
    )
    group_word = lax.all_gather(grad_word[None], "mp", axis=0, tiled=True)
    grad_table = grad_table.astype(WIDE) + jnp.zeros((vocab_shard, D), WIDE).at[safe_index].add(
        jnp.where(inside[..., None], group_word.astype(WIDE), 0.0)
    )

    def split_rows(part):
        rows = part.shape[-2] // dp
        part = part.astype(LOW).reshape(part.shape[:-2] + (dp, rows, part.shape[-1]))
        extra = [(0, 0)] * (part.ndim - 2) + [(0, pad_up(rows, 16) - rows), (0, 0)]
        return jnp.pad(part, extra) if extra[-2][1] else part

    cut = small_params.shape[1]
    small_split = jnp.transpose(grad_small.reshape(VROWS, dp, cut), (1, 0, 2)).astype(LOW)
    small_split = jnp.pad(small_split, ((0, 0), (0, 32 - VROWS), (0, LANES - cut)))
    table_split, ffn_split = split_rows(grad_table), split_rows(grad_ffn)
    shared_sum, split_sum, totals = reduce_gradients(
        plan,
        table_split,
        split_rows(grad_in_weight),
        split_rows(grad_out_weight),
        ffn_split,
        split_rows(grad_places),
        split_rows(grad_visual),
        grad_boxes.reshape(4, dp, NBOX // dp, LANES),
        small_split,
        own_tile,
    )
    loss_sum, loss_count = (totals[1, 0, 0], totals[1, 1, 0])
    grad_norm = jnp.sqrt(jnp.sum(totals[0])) / loss_count
    outputs = adam_update(
        plan, table_split.shape[1], ffn_split.shape[2], shared_sum, split_sum, totals, states
    )
    return tuple(outputs) + (loss_sum, loss_count, grad_norm)


def solution(mesh):
    in_specs = (
        P("dp", None),
        P(("dp", "mp"), None, None),
        P(("dp", "mp"), None),
        P(("dp", "mp"), None),
        P(("dp", "mp"), None),
        P(("dp", "mp")),
        P("dp"),
        P("dp"),
        P(None, "dp", None),
        P(None, "dp", None),
        P(None, "dp", None),
        P(None, "dp", None),
        P(None, "dp", None),
        P(None, "dp", None),
        P("dp", None),
        P("dp", None),
        P("dp", None),
        P("dp", None),
        P("dp", None),
        P("dp", None),
        P(None, "dp"),
        P(None, "dp"),
        P(None, "dp"),
        P(("mp", "dp"), None),
        P(("mp", "dp"), None),
        P(("mp", "dp"), None),
        P(None, "dp", "mp"),
        P(None, "dp", "mp"),
        P(None, "dp", "mp"),
    )
    out_specs = (
        P(None, "dp", None),
        P(None, "dp", None),
        P(None, "dp", None),
        P(None, "dp", None),
        P(None, "dp", None),
        P(None, "dp", None),
        P("dp", None),
        P("dp", None),
        P("dp", None),
        P("dp", None),
        P("dp", None),
        P("dp", None),
        P(None, "dp"),
        P(None, "dp"),
        P(None, "dp"),
        P(("mp", "dp"), None),
        P(("mp", "dp"), None),
        P(("mp", "dp"), None),
        P(None, "dp", "mp"),
        P(None, "dp", "mp"),
        P(None, "dp", "mp"),
        P(),
        P(),
        P(),
    )
    return jax.shard_map(
        on_device, mesh=mesh, in_specs=in_specs, out_specs=out_specs, check_vma=False
    )
```

time: 687 us -> 590 us (0.86); the launches traced: 679 us -> 589 us
  Pallas kernels: 126 us -> 271 us
  matrix products: 109 us -> 0 us
  waiting for transfers between devices: 106 us -> 177 us
  local copies, waits for them, and re-layouts: 108 us -> 39.7 us
  other arithmetic: 121 us -> 53.2 us
  blocking collectives: 89.1 us -> 30.7 us
    pallas_call x0 -> x3, Pallas kernels: none -> 138 us  [the longest x1 91.3 us: head_step(): pl.pallas_call(body, out_shape=(jax.ShapeDtypeStruct((slots, D), WIDE), j...]
    dot_general x39 -> x0, matrix products: 109 us -> none  [the longest x22 60 us: dot(): lax.dot_general(left, right, (dims, ((), ())), preferred_element_type=f32)]
    all_gather x5, waiting for transfers between devices: 49.9 us -> 114 us  [the longest x4 63.5 us: gathered(): return lax.all_gather(part.astype(LOW), 'dp', axis=axis, tiled=True)]
    all_gather x7 -> x3, blocking collectives: 89.1 us -> 30.7 us  [gathered(): return lax.all_gather(part.astype(LOW), 'dp', axis=axis, tiled=True)]
    scatter-add x14 -> x1, other arithmetic: 59.1 us -> 23.1 us  [on_device(): jnp.zeros((vocab_shard, D), WIDE).at[safe_index]]
    gather x20 -> x0, local copies, waits for them, and re-layouts: 29.3 us -> none  [the longest x2 5.04 us: spatial(): tables[2][bottom_edge - top_edge]]
    unnamed x348 -> x59, local copies, waits for them, and re-layouts: 30.5 us -> 9.48 us
    reduce_sum x17 -> x1, other arithmetic: 15.2 us -> 0.13 us  [edge_rows_back(): low = jnp.sum(grad[..., :half + 1], -1, keepdims=True)]
  transfers between devices with their start and end apart: 9 -> 6, of which waited for: 5 -> 5; matrix products, arithmetic and copies ran while one was open for 33% -> 7% of each run, Pallas kernels for 0% -> 3%
where the time goes in v3:
time: 590 us; the launch traced here: 589 us
  Pallas kernels  271 us (46%)
  waiting for transfers between devices  177 us (30%)
  other arithmetic  53.2 us (9%)
  local copies, waits for them, and re-layouts  39.7 us (7%)
  blocking collectives  30.7 us (5%)
  between operations  17.2 us (3%)
    pallas_call x1, Pallas kernels, reduce_gradients(): pl.pallas_call(body, out_shape=(jax.ShapeDtypeStruct((plan.shared, D), WI...  122 us
    pallas_call x1, Pallas kernels, head_step(): pl.pallas_call(body, out_shape=(jax.ShapeDtypeStruct((slots, D), WIDE), j...  91.3 us
    all_gather x4, waiting for transfers between devices, gathered(): return lax.all_gather(part.astype(LOW), 'dp', axis=axis, tiled=True)  63.5 us
    reduce_scatter x1, waiting for transfers between devices, on_device(): lax.psum_scatter(partial_word, 'mp', scatter_dimension=0, tiled=True)[0]  62.4 us
    all_gather x1, waiting for transfers between devices, on_device(): group_word = lax.all_gather(grad_word[None], 'mp', axis=0, tiled=True)  50.8 us
    all_gather x3, blocking collectives, gathered(): return lax.all_gather(part.astype(LOW), 'dp', axis=axis, tiled=True)  30.7 us
    pallas_call x1, Pallas kernels, back_step(): pl.pallas_call(back_kernel, out_shape=(shape((TEXT, D), LOW), shape((TEXT...  26.4 us
    scatter-add x1, other arithmetic, on_device(): jnp.zeros((vocab_shard, D), WIDE).at[safe_index]  23.1 us
  transfers between devices with their start and end apart: 6, of which 5 were waited for; matrix products, arithmetic and copies ran while one was open for 7% of the time, Pallas kernels for 3%

profile of v3, /device:TPU:0, one launch (start us, length us, event | category | flops | bytes accessed | tf_op | source)
XLA Modules:
  0.0 589.3 jit_solution(4866519187972414507)
XLA Ops:
  7.3 2.4 convert_element_type.52
  9.8 0.9 convert_element_type.61
  10.7 0.7 convert_element_type.54
  11.6 45.6 %all-gather.8.cloned.1.call-done.refs_6_ = bf16[3840,768]{1,0:T(8,128)(2,1)} async-done(((bf16[480,768]{1,0:T(8,128)(2,1)}), bf16[3840,768]{1,0:T(8,128)(2,1)}) %all-gather.8.cloned.1.call-update) | async-done | bytes 5898256 | tf_op jit(solution)/shard_map/all_gather | solution.py:1131
  57.1 13.6 %gather_fusion = bf16[2048,768]{1,0:T(8,128)(2,1)} fusion(bf16[3840,768]{1,0:T(8,128)(2,1)} %all-gather.8.cloned.1.call-done.refs_6_, s32[2048]{0:T(1024)S(1)} %broadcast_clamp_fusion), kind=kCustom, calls=%fused_computation | custom fusion | bytes 6299648 | tf_op jit(solution)/shard_map/jit(_take)/gather | solution.py:1148
  70.7 3.5 select_select_fusion
  74.4 0.9 copy-done.1
  75.3 0.7 convert_element_type.62
  76.1 0.6 broadcast_in_dim.68.refs_7_
  76.7 0.6 broadcast_in_dim.69.refs_8_
  77.3 9.1 %all-gather.1 = bf16[8,96,17]{1,2,0:T(8,128)(2,1)S(1)} all-gather(bf16[1,96,17]{1,2,0:T(8,128)(2,1)S(1)} %convert_bitcast_fusion), channel_id=1, replica_groups=mesh['dp'=8,'mp'=4] {'dp'}, dimensions={0}, use_global_device_ids=true | all-gather | bytes 29376 | tf_op jit(solution)/shard_map/all_gather | solution.py:1131
  87.4 0.6 fusion.4
  88.1 0.9 copy.73.columns_ref
  88.9 0.6 pad.18.features_ref
  89.5 0.6 pad.19.edges_ref
  90.2 10.3 %all_gather.27.visual_ref = bf16[256,768]{1,0:T(8,128)(2,1)} all-gather(bf16[32,768]{1,0:T(8,128)(2,1)S(1)} %convert_element_type.55), channel_id=1, replica_groups=mesh['dp'=8,'mp'=4] {'dp'}, dimensions={0}, use_global_device_ids=true | all-gather | bytes 442368 | tf_op jit(solution)/shard_map/all_gather | solution.py:1131
  100.4 0.6 constant_dynamic-slice_fusion.refs_4_
  101.0 11.4 %all_gather.25.places_ref = bf16[512,768]{1,0:T(8,128)(2,1)} all-gather(bf16[64,768]{1,0:T(8,128)(2,1)S(1)} %convert_element_type.53), channel_id=1, replica_groups=mesh['dp'=8,'mp'=4] {'dp'}, dimensions={0}, use_global_device_ids=true | all-gather | bytes 884736 | tf_op jit(solution)/shard_map/all_gather | solution.py:1131
  112.4 4.1 slice.101.weights_ref
  116.4 2.4 slice_bitcast_fusion.refs_2_
  118.8 6.4 %all-gather.10.cloned.1.call-done.boxes_ref = bf16[4,1024,128]{2,1,0:T(8,128)(2,1)} async-done(((bf16[4,128,128]{2,1,0:T(8,128)(2,1)}), bf16[4,1024,128]{2,1,0:T(8,128)(2,1)}) %all-gather.10.cloned.1.call-update) | async-done | bytes 1048592 | tf_op jit(solution)/shard_map/all_gather | solution.py:1131
  125.2 62.4 %reduce-scatter.2.cloned.1.call-done = bf16[1,512,768]{2,1,0:T(8,128)(2,1)} async-done(((bf16[4,512,768]{2,1,0:T(8,128)(2,1)}), bf16[1,512,768]{2,1,0:T(8,128)(2,1)}) %reduce-scatter.2.cloned.1.call-update) | async-done | bytes 786448 | tf_op jit(solution)/shard_map/reduce_scatter | solution.py:1150
  187.7 19.9 %front_step.1 = (bf16[80,768]{1,0:T(8,128)(2,1)}, f32[80,768]{1,0:T(8,128)}, bf16[80,768]{1,0:T(8,128)(2,1)}, bf16[576,768]{1,0:T(8,128)(2,1)}, f32[576,768]{1,0...) custom-call(s32[80]{0:T(128)} %pos_ref.3, ...), custom_call_target="tpu_custom_call" | custom-call | tf_op jit(solution)/shard_map/front_step/pallas_call | solution.py:962
  207.6 11.5 %all-gather.14.cloned.1.call-done.refs_5_ = bf16[2,768,768]{2,1,0:T(8,128)(2,1)} async-done(((bf16[2,96,768]{2,1,0:T(8,128)(2,1)}), bf16[2,768,768]{2,1,0:T(8,128)(2,1)}) %all-gather.14.cloned.1.call-update) | async-done | bytes 2359312 | tf_op jit(solution)/shard_map/all_gather | solution.py:1131
  219.1 91.3 %head_step.1 = (f32[80,768]{1,0:T(8,128)}, bf16[80,768]{1,0:T(8,128)(2,1)}, bf16[768,768]{1,0:T(8,128)(2,1)}, bf16[2,768,768]{2,1,0:T(8,128)(2,1)}, bf16[3840,76...) custom-call(bf16[80,768]{1,0:T(8,128)(2,1)} %get-tuple-element.73.refs_0_, ...), custom_call_target="tpu_custom_call" | custom-call | tf_op jit(solution)/shard_map/head_step/pallas_call | solution.py:758
  310.4 26.4 %back_step.1 = (bf16[512,768]{1,0:T(8,128)(2,1)}, bf16[512,768]{1,0:T(8,128)(2,1)}, bf16[4,1024,128]{2,1,0:T(8,128)(2,1)}, bf16[256,768]{1,0:T(8,128)(2,1)}, bf1...) custom-call(s32[80]{0:T(128)} %pos_ref.3, f32[80,768]{1,0:T(8,128)} %get-tuple-element.76.grad_zero_ref, ...), custom_call_target="tpu_custom_call" | custom-call | tf_op jit(solution)/shard_map/back_step/pallas_call | solution.py:1094
  337.2 0.7 slice.132
  338.0 0.8 slice.131
  338.9 0.7 reshape.316
  340.5 0.6 pad.21.refs_7_
  341.2 8.2 %convert_element_type.63 = f32[3840,768]{1,0:T(8,128)} convert(bf16[3840,768]{1,0:T(8,128)(2,1)} %get-tuple-element.75) | non-fusion elementwise | flops 2949120 | bytes 17694720 | tf_op jit(solution)/shard_map/convert_element_type | solution.py:1184
  349.3 50.8 %all-gather.16.cloned.1.call-done = bf16[2048,768]{1,0:T(8,128)(2,1)} async-done(((bf16[512,768]{1,0:T(8,128)(2,1)}), bf16[2048,768]{1,0:T(8,128)(2,1)}) %all-gather.16.cloned.1.call-update) | async-done | bytes 3145744 | tf_op jit(solution)/shard_map/all_gather | solution.py:1183
  400.1 4.4 convert_select_fusion
  404.6 23.1 %scatter_fusion = f32[3840,768]{1,0:T(8,128)} fusion(f32[3840,768]{1,0:T(8,128)} %convert_element_type.63, s32[2048]{0:T(1024)S(1)} %bitcast.83, f32[2048,768]{1,0:T(8,128)} %bitcast.68), kind=kCustom, calls=%fused_computation.1 | custom fusion | flops 1572864 | bytes 18882560 | tf_op jit(solution)/shard_map/scatter-add | solution.py:1184
  427.7 7.4 %convert_element_type.65 = bf16[3840,768]{1,0:T(8,128)(2,1)} convert(f32[3840,768]{1,0:T(8,128)} %scatter_fusion) | non-fusion elementwise | flops 2949120 | bytes 17694720 | tf_op jit(solution)/shard_map/convert_element_type | solution.py:1190
  435.1 122.0 %reduce_gradients.1 = (f32[640,768]{1,0:T(8,128)}, f32[672,768]{1,0:T(8,128)}, f32[2,8,128]{2,1,0:T(8,128)}) custom-call(bf16[8,480,768]{2,1,0:T(8,128)(2,1)} %bitcast.69, bf16[3,8,96,768]{3,2,1,0:T(8,128)(2,1)} %bitcast.71, bf16[8,96,768]{2,1,0:T(8,128)(2,1)} %bitcast.74, bf16[2,8,96,768]{3,2,1,0:T(8,128)(2,1)} %bitcast.73, bf16[8,64,768]{2,1,0:T(8,128)(2,1)} %bitcast.76, ...), custom_call_target="tpu_custom_call" | custom-call | tf_op jit(solution)/shard_map/reduce_gradients/pallas_call | solution.py:355
  557.2 1.3 slice_reduce_fusion.2
  558.5 1.3 fusion.5
  561.2 1.1 copy-done.5
  562.2 1.1 copy-done.6
  563.3 0.9 copy-done.8
  564.2 0.9 copy-done.9
  565.2 0.9 copy-done.10
  566.1 0.9 copy-done.11
  567.0 0.9 copy-done.12
  567.9 0.9 copy-done.13
  568.8 0.7 copy-done.15
  569.5 11.8 %adam_update.1 = (f32[4,96,768]{2,1,0:T(8,128)}, f32[4,96,768]{2,1,0:T(8,128)}, f32[4,96,768]{2,1,0:T(8,128)}, f32[4,128,128]{2,1,0:T(8,128)}, f32[4,128,128]{2,...) custom-call(f32[640,768]{1,0:T(8,128)} %get-tuple-element.98.refs_0_, ...), custom_call_target="tpu_custom_call" | custom-call | tf_op jit(solution)/shard_map/adam_update/pallas_call | solution.py:444
  (113 shorter events, 2.7 us)
Async XLA Ops:
  7.2 2.6 copy-start
  7.2 3.5 copy-start.3
  7.2 4.3 copy-start.19
  7.2 49.9 %all-gather.8.cloned.1.call-start = ((), (), s32[]{:S(2)}) async-start(), calls=%async_computation.1 | async-start | bytes 6635520 | tf_op jit(solution)/shard_map/all_gather | solution.py:1131
  9.7 102.7 %all-gather.12.cloned.1.call-start = ((), (), s32[]{:S(2)}) async-start(), calls=%async_computation.4 | async-start | bytes 5308416 | tf_op jit(solution)/shard_map/all_gather | solution.py:1131
  10.7 114.6 %all-gather.10.cloned.1.call-start = ((), (), s32[]{:S(2)}) async-start(), calls=%async_computation.3 | async-start | bytes 1179648 | tf_op jit(solution)/shard_map/all_gather | solution.py:1131
  11.4 176.2 %reduce-scatter.2.cloned.1.call-start = ((), (), s32[]{:S(2)}) async-start(), calls=%async_computation.2 | async-start | bytes 3932160 | tf_op jit(solution)/shard_map/reduce_scatter | solution.py:1150
  74.2 1.1 copy-start.1
  74.2 1.9 copy-start.23
  74.2 2.5 copy-start.24
  74.2 3.0 copy-start.25
  74.2 3.1 copy-start.26
  74.2 3.1 copy-start.14
  74.2 12.3 %copy-start.7 = (f32[32,768]{1,0:T(8,128)S(1)}, f32[32,768]{1,0:T(8,128)}, u32[]{:S(2)}) copy-start(f32[32,768]{1,0:T(8,128)} %refs_12_.1) | copy-start | bytes 294916
  74.3 12.9 %copy-start.4 = (f32[64,768]{1,0:T(8,128)S(1)}, f32[64,768]{1,0:T(8,128)}, u32[]{:S(2)}) copy-start(f32[64,768]{1,0:T(8,128)} %refs_9_.1) | copy-start | bytes 589828
  74.3 13.0 %copy-start.21 = (s32[1,512,4]{1,2,0:T(4,128)S(1)}, s32[1,512,4]{1,2,0:T(4,128)}, u32[]{:S(2)}) copy-start(s32[1,512,4]{1,2,0:T(4,128)} %param.30) | copy-start | bytes 24580
  74.3 14.6 %copy-start.20 = (bf16[49,256]{1,0:T(8,128)(2,1)S(1)}, bf16[49,256]{1,0:T(8,128)(2,1)}, u32[]{:S(2)}) copy-start(bf16[49,256]{1,0:T(8,128)(2,1)} %param.33) | copy-start | bytes 75268
  74.3 144.8 %all-gather.14.cloned.1.call-start = ((), (), s32[]{:S(2)}) async-start(), calls=%async_computation.5 | async-start | bytes 2654208 | tf_op jit(solution)/shard_map/all_gather | solution.py:1131
  76.0 324.1 %all-gather.16.cloned.1.call-start = ((), (), s32[]{:S(2)}) async-start(), calls=%async_computation.6 | async-start | bytes 3932160 | tf_op jit(solution)/shard_map/all_gather | solution.py:1183
  86.6 29.8 %copy-start.18 = (f32[17,768]{1,0:T(8,128)}, f32[17,768]{1,0:T(8,128)S(1)}, u32[]{:S(2)}) copy-start(f32[17,768]{1,0:T(8,128)S(1)} %bitcast_convert_fusion.small_ref.refs_3_) | copy-start | bytes 156676
  310.4 26.4 %copy-start.22 = (f32[1,768]{1,0:T(1,128)S(1)}, f32[1,768]{1,0:T(1,128)}, u32[]{:S(2)}) copy-start(f32[1,768]{1,0:T(1,128)} %get-tuple-element.95) | copy-start | bytes 9220
  435.1 126.0 %copy-start.2 = (f32[4,96,768]{2,1,0:T(8,128)S(1)}, f32[4,96,768]{2,1,0:T(8,128)}, u32[]{:S(2)}) copy-start(f32[4,96,768]{2,1,0:T(8,128)} %refs_4_.1) | copy-start | bytes 3538948
  435.1 126.0 %copy-start.16 = (f32[17,96]{1,0:T(8,128)S(1)}, f32[17,96]{1,0:T(8,128)}, u32[]{:S(2)}) copy-start(f32[17,96]{1,0:T(8,128)} %refs_16_.1) | copy-start | bytes 19588
  435.1 126.0 %copy-start.17 = (f32[17,96]{1,0:T(8,128)S(1)}, f32[17,96]{1,0:T(8,128)}, u32[]{:S(2)}) copy-start(f32[17,96]{1,0:T(8,128)} %refs_17_.1) | copy-start | bytes 19588
  561.1 1.1 copy-start.5
  562.2 1.1 copy-start.6
  563.3 0.9 copy-start.8
  564.2 0.9 copy-start.9
  565.2 0.9 copy-start.10
  566.1 0.9 copy-start.11
  567.0 0.9 copy-start.12
  567.9 0.9 copy-start.13
  568.8 0.7 copy-start.15
Sparse Core Ops, SparseCore 0:
  10.5 46.5 all-gather.7
  59.6 39.4 all-gather.11
  101.6 23.5 all-gather.9
  127.4 60.2 reduce-scatter.1
  190.0 29.0 all-gather.13
  336.9 63.1 all-gather.15

commit v4 on v3

--- a/solution.py
+++ b/solution.py
@@ -66,9 +66,7 @@
     return count.bit_length() - 1
 
 
-def flip(index, bit, ring):
-    if ring and bit == 1:
-        return 3 - index
+def flip(index, bit):
     return index + (1 - 2 * ((index // 2**bit) % 2)) * 2**bit
 
 
@@ -106,22 +104,25 @@
     return next(t for t in (48, 32, 16) if rows % t == 0)
 
 
-def reduce_kernel(plan, table_rows, ffn_rows, refs):
+def reduce_kernel(plan, table_rows, ffn_rows, vocab_rows, refs):
     (
         table_in, proj_in, out_in, ffn_in, places_in, visual_in, boxes_in, small_in, tile_in,
+        word_in, tokens_ref,
         shared_out, split_out, tile_out,
-        shared_acc, split_acc, shared_got, split_got, ring_got, ring_own, tile_mp, tile_dp,
-        load_sem, send_sem, recv_sem, ring_send, ring_recv, tile_send, tile_recv,
+        shared_acc, split_acc, shared_got, split_got, ring_got, ring_own, words, tile_mp, tile_dp,
+        load_sem, send_sem, recv_sem, ring_send, ring_recv, word_send, word_recv, tile_send,
+        tile_recv,
     ) = refs
     dp, mp = plan.dp, plan.mp
     me, here = lax.axis_index("dp"), lax.axis_index("mp")
     depth, ring_depth = bits_of(dp), bits_of(mp)
-    ring = mp == 4
     loads = []
 
     def load(source, target):
         loads.append(pltpu.make_async_copy(source, target, load_sem.at[len(loads)]))
-
+        loads[-1].start()
+
+    load(word_in, words.at[here])
     for part in range(4):
         source = proj_in.at[part] if part < 3 else out_in
         load(source, shared_acc.at[:, pl.ds(part * plan.proj, plan.proj)])
@@ -136,13 +137,12 @@
         )
     row, lane = plan.box_slot(plan.box_parts)
     load(small_in, shared_acc.at[:, pl.ds(row, 32), pl.ds(lane, LANES)])
-    load(table_in, split_acc.at[:, pl.ds(0, table_rows)])
+    first_loads = len(loads)
     for part in range(2):
         wide = ffn_in.shape[3]
         row, lane = ffn_slot(part, table_rows, ffn_rows, wide)
         load(ffn_in.at[part], split_acc.at[:, pl.ds(row, ffn_rows), pl.ds(lane, wide)])
-    for copy in loads:
-        copy.start()
+    load(table_in, split_acc.at[:, pl.ds(0, table_rows)])
 
     barrier = pltpu.get_barrier_semaphore()
     for other in range(1, dp):
@@ -154,21 +154,30 @@
             barrier, 1, device_id={"mp": lax.rem(here + other, mp)}, device_id_type=MESH
         )
     pl.semaphore_wait(barrier, dp + mp - 2)
-    for copy in loads:
-        copy.wait()
-
     for part in range(plan.box_parts + 1, 6 * (plan.shared - plan.box_at) // 32):
         row, lane = plan.box_slot(part)
         shared_acc[:, pl.ds(row, 32), pl.ds(lane, LANES)] = jnp.zeros((dp, 32, LANES), LOW)
 
+    ring = Ring(mp, (word_send, word_recv))
+    loads[0].wait()
+    for stream in range(2):
+        ring.gather_start(words, 0, stream, 0)
+
+    def word_step(step):
+        for stream in range(2):
+            ring.gather_wait(words, 0, stream, step)
+            if step < ring.depth - 1:
+                ring.gather_start(words, 0, stream, step + 1)
+
     orders = ([0] + list(range(depth - 1, 0, -1)), list(range(depth)))
-    pieces = []
-    for acc, got, rows in (
-        (shared_acc, shared_got, plan.shared),
-        (split_acc, split_got, split_acc.shape[1]),
-    ):
-        for part in range(2):
-            pieces.append((acc, got, part * (rows // 2), rows // 2))
+    half, rest = plan.shared // 2, split_acc.shape[1] - table_rows
+    pieces = (
+        (shared_acc, shared_got, 0, half),
+        (shared_acc, shared_got, half, half),
+        (split_acc, split_got, table_rows, rest),
+        (split_acc, split_got, 0, table_rows // 2),
+        (split_acc, split_got, table_rows // 2, table_rows // 2),
+    )
 
     def chunk(order, step, free, away):
         index = 0
@@ -185,35 +194,35 @@
     def slot_base(step):
         return sum(2 ** (depth - 1 - s) for s in range(step))
 
-    def region(piece, stream, step):
+    def send_one(piece, stream, step, free):
+        acc, got, first, rows = pieces[piece]
+        order = orders[stream]
+        pltpu.make_async_remote_copy(
+            src_ref=acc.at[chunk(order, step, free, True), pl.ds(first, rows), lanes_of(stream)],
+            dst_ref=got.at[slot_base(step) + free, pl.ds(first, rows), lanes_of(stream)],
+            send_sem=send_sem.at[piece, stream, step],
+            recv_sem=recv_sem.at[piece, stream, step],
+            device_id={"dp": flip(me, order[step])},
+            device_id_type=MESH,
+        ).start()
+
+    def send(piece, step):
+        for stream in range(2):
+            for free in range(2 ** (depth - 1 - step)):
+                send_one(piece, stream, step, free)
+
+    def wait_bytes(piece, stream, step, sem):
         acc, got, first, rows = pieces[piece]
         count = 2 ** (depth - 1 - step)
-        return got.at[pl.ds(slot_base(step), count), pl.ds(first, rows), lanes_of(stream)]
-
-    def send(piece, stream, step):
-        acc, got, first, rows = pieces[piece]
-        order = orders[stream]
-        for free in range(2 ** (depth - 1 - step)):
-            pltpu.make_async_remote_copy(
-                src_ref=acc.at[chunk(order, step, free, True), pl.ds(first, rows), lanes_of(stream)],
-                dst_ref=got.at[slot_base(step) + free, pl.ds(first, rows), lanes_of(stream)],
-                send_sem=send_sem.at[piece, stream, step],
-                recv_sem=recv_sem.at[piece, stream, step],
-                device_id={"dp": flip(me, order[step], False)},
-                device_id_type=MESH,
-            ).start()
-
-    def wait_bytes(piece, stream, step, sem):
-        where = region(piece, stream, step)
+        where = got.at[pl.ds(slot_base(step), count), pl.ds(first, rows), lanes_of(stream)]
         pltpu.make_async_copy(where, where, sem.at[piece, stream, step]).wait()
 
-    def finish(piece, stream, step):
+    def add(piece, stream, step):
         acc, got, first, rows = pieces[piece]
         order = orders[stream]
         wait_bytes(piece, stream, step, recv_sem)
         tile = row_tile(rows)
         last = step == depth - 1
-        out, low_out = (shared_out, True) if acc is shared_acc else (split_out, False)
         for free in range(2 ** (depth - 1 - step)):
             kept = chunk(order, step, free, False)
 
@@ -223,8 +232,8 @@
                 total = acc[kept, where, lanes_of(stream)].astype(WIDE) + got[
                     slot_base(step) + free, where, lanes_of(stream)
                 ].astype(WIDE)
-                if last and not low_out:
-                    out[where, lanes_of(stream)] = total
+                if last and acc is split_acc:
+                    split_out[where, lanes_of(stream)] = total
                 elif last:
                     ring_own[0, where, lanes_of(stream)] = total.astype(LOW)
                 else:
@@ -232,6 +241,13 @@
                 return carry
 
             lax.fori_loop(0, rows // tile, body, 0)
+
+    def advance(piece, step):
+        for stream in range(2):
+            add(piece, stream, step)
+            if step < depth - 1:
+                for free in range(2 ** (depth - 2 - step)):
+                    send_one(piece, stream, step + 1, free)
 
     ring_orders = (list(range(ring_depth)), list(range(ring_depth - 1, -1, -1)))
 
@@ -241,43 +257,80 @@
             dst_ref=ring_got.at[step, :, lanes_of(stream)],
             send_sem=ring_send.at[stream, step],
             recv_sem=ring_recv.at[stream, step],
-            device_id={"mp": flip(here, ring_orders[stream][step], ring)},
+            device_id={"mp": flip(here, ring_orders[stream][step])},
             device_id_type=MESH,
         )
 
-    def ring_finish(stream, step):
-        ring_copy(stream, step).wait_recv()
-        rows = plan.shared
-        tile = row_tile(rows)
-
-        def body(index, carry):
-            where = pl.ds(pl.multiple_of(index * tile, 16), tile)
-            total = ring_own[step, where, lanes_of(stream)].astype(WIDE) + ring_got[
-                step, where, lanes_of(stream)
-            ].astype(WIDE)
-            if step == ring_depth - 1:
-                shared_out[where, lanes_of(stream)] = total
-            else:
-                ring_own[step + 1, where, lanes_of(stream)] = total.astype(LOW)
-            return carry
-
-        lax.fori_loop(0, rows // tile, body, 0)
-
-    everything = [(piece, stream) for piece in range(len(pieces)) for stream in range(2)]
-    for piece, stream in everything:
-        send(piece, stream, 0)
-    for step in range(depth):
-        for piece, stream in everything:
-            finish(piece, stream, step)
-            if step < depth - 1:
-                send(piece, stream, step + 1)
-            elif piece == 1:
-                ring_copy(stream, 0).start()
-    for step in range(ring_depth):
+    def ring_step(step):
         for stream in range(2):
-            ring_finish(stream, step)
+            ring_copy(stream, step).wait_recv()
+            rows = plan.shared
+            tile = row_tile(rows)
+
+            def body(index, carry):
+                where = pl.ds(pl.multiple_of(index * tile, 16), tile)
+                total = ring_own[step, where, lanes_of(stream)].astype(WIDE) + ring_got[
+                    step, where, lanes_of(stream)
+                ].astype(WIDE)
+                if step == ring_depth - 1:
+                    shared_out[where, lanes_of(stream)] = total
+                else:
+                    ring_own[step + 1, where, lanes_of(stream)] = total.astype(LOW)
+                return carry
+
+            lax.fori_loop(0, rows // tile, body, 0)
             if step < ring_depth - 1:
                 ring_copy(stream, step + 1).start()
+
+    ids = tokens_ref[...] - here * (vocab_rows * dp)
+
+    def scatter(index):
+        local = ids - index * vocab_rows
+        local = jnp.where(local < vocab_rows, local, -1)
+        place = lax.broadcasted_iota(jnp.int32, (table_rows, ids.shape[1]), 0)
+        hot = jnp.where(place == local, 1.0, 0.0).astype(LOW)
+        where = (index, pl.ds(0, table_rows))
+        total = split_acc[where].astype(WIDE) + mm(hot, words[...].reshape(mp * TEXT, D), NN)
+        split_acc[where] = total.astype(LOW)
+
+    for copy in loads[1:first_loads]:
+        copy.wait()
+    send(0, 0)
+    send(1, 0)
+    for copy in loads[first_loads:]:
+        copy.wait()
+    send(2, 0)
+    for step in range(depth):
+        for piece in range(3):
+            advance(piece, step)
+            if step == depth - 1 and piece == 1:
+                for stream in range(2):
+                    ring_copy(stream, 0).start()
+        if step < ring.depth - 1:
+            word_step(step)
+    for step in range(min(depth, ring.depth - 1), ring.depth):
+        word_step(step)
+    count = 2 ** (depth - 1)
+    other_core, own_core = 1 - me % 2, me % 2
+
+    def scatter_other(index, carry):
+        scatter(other_core + 2 * index)
+        return carry
+
+    def scatter_own(index, carry):
+        scatter(own_core + 2 * index)
+        return carry
+
+    lax.fori_loop(0, count, scatter_other, 0)
+    send(3, 0)
+    send(4, 0)
+    lax.fori_loop(0, count, scatter_own, 0)
+    for step in range(max(depth, ring_depth)):
+        for piece in (3, 4):
+            if step < depth:
+                advance(piece, step)
+        if step < ring_depth:
+            ring_step(step)
 
     def squares(ref, rows):
         tile = row_tile(rows)
@@ -293,7 +346,6 @@
         return folded
 
     folded = squares(shared_out, plan.shared) * (1.0 / mp) + squares(split_out, split_out.shape[0])
-    own = lax.broadcasted_iota(jnp.int32, (8, LANES), 0)
     tile_mp[here, 0] = folded
     tile_mp[here, 1] = tile_in[...]
 
@@ -331,26 +383,29 @@
     tile_out[...] = total
     for copy in pending:
         copy.wait_send()
-    for piece, stream in everything:
-        for step in range(depth):
-            wait_bytes(piece, stream, step, send_sem)
+    ring.finish()
+    for piece in range(len(pieces)):
+        for stream in range(2):
+            for step in range(depth):
+                wait_bytes(piece, stream, step, send_sem)
     for stream in range(2):
         for step in range(ring_depth):
             ring_copy(stream, step).wait_send()
 
 
-def reduce_gradients(plan, table, proj, out, ffn, places, visual, boxes, small, tile):
+def reduce_gradients(
+    plan, vocab_rows, table, proj, out, ffn, places, visual, boxes, small, tile, word, tokens
+):
     dp, mp = plan.dp, plan.mp
     table_rows, ffn_rows = table.shape[1], ffn.shape[2]
     split = table_rows + 2 * ffn_rows * ffn.shape[3] // D
     depth, ring_depth = bits_of(dp), bits_of(mp)
-    loads = 4 + 2 + plan.box_parts + 1 + 1 + 2
     anywhere = pl.BlockSpec(memory_space=pl.ANY)
     vmem = pl.BlockSpec(memory_space=pltpu.VMEM)
     dma = pltpu.SemaphoreType.DMA
 
     def body(*refs):
-        reduce_kernel(plan, table_rows, ffn_rows, refs)
+        reduce_kernel(plan, table_rows, ffn_rows, vocab_rows, refs)
 
     return pl.pallas_call(
         body,
@@ -359,7 +414,7 @@
             jax.ShapeDtypeStruct((split, D), WIDE),
             jax.ShapeDtypeStruct((2, 8, LANES), WIDE),
         ),
-        in_specs=[anywhere] * 8 + [vmem],
+        in_specs=[anywhere] * 8 + [vmem, anywhere, vmem],
         out_specs=(vmem, vmem, vmem),
         scratch_shapes=[
             pltpu.VMEM((dp, plan.shared, D), LOW),
@@ -368,21 +423,24 @@
             pltpu.VMEM((dp - 1, split, D), LOW),
             pltpu.VMEM((ring_depth, plan.shared, D), LOW),
             pltpu.VMEM((ring_depth, plan.shared, D), LOW),
+            pltpu.VMEM((mp, TEXT, D), LOW),
             pltpu.VMEM((mp, 2, 8, LANES), WIDE),
             pltpu.VMEM((dp, 2, 8, LANES), WIDE),
-            dma((loads,)),
-            dma((4, 2, depth)),
-            dma((4, 2, depth)),
+            dma((plan.box_parts + 12,)),
+            dma((5, 2, depth)),
+            dma((5, 2, depth)),
             dma((2, ring_depth)),
             dma((2, ring_depth)),
+            dma((1, 2, mp - 1)),
+            dma((1, 2, mp - 1)),
             dma((mp + dp,)),
             dma((mp + dp,)),
         ],
         compiler_params=pltpu.CompilerParams(
-            collective_id=5, has_side_effects=True, vmem_limit_bytes=56 * 2**20
+            collective_id=5, has_side_effects=True, vmem_limit_bytes=58 * 2**20
         ),
         name="reduce_gradients",
-    )(table, proj, out, ffn, places, visual, boxes, small, tile)
+    )(table, proj, out, ffn, places, visual, boxes, small, tile, word, tokens)
 
 
 def adam_kernel(plan, table_rows, ffn_rows, sizes, refs):
@@ -451,16 +509,16 @@
     )(shared, split, tile, *states)
 
 
-def combos(index, bits, ring):
+def combos(index, bits):
     found = [index]
     for bit in bits:
-        found = found + [flip(one, bit, ring) for one in found]
+        found = found + [flip(one, bit) for one in found]
     return found
 
 
 class Ring:
     def __init__(self, mp, sems):
-        self.mp, self.here, self.ring = mp, lax.axis_index("mp"), mp == 4
+        self.mp, self.here = mp, lax.axis_index("mp")
         self.send, self.recv = sems
         depth = bits_of(mp)
         self.depth = depth
@@ -487,8 +545,8 @@
 
     def gather_start(self, buffer, number, stream, step):
         order = self.orders[stream]
-        peer = flip(self.here, order[step], self.ring)
-        for place, slot in enumerate(combos(self.here, order[:step], self.ring)):
+        peer = flip(self.here, order[step])
+        for place, slot in enumerate(combos(self.here, order[:step])):
             part = buffer.at[slot, :, lanes_of(stream)]
             made = self.copy(part, part, number, stream, 2**step - 1 + place, peer)
             made.start()
@@ -496,8 +554,8 @@
 
     def gather_wait(self, buffer, number, stream, step):
         order = self.orders[stream]
-        peer = flip(self.here, order[step], self.ring)
-        for place, slot in enumerate(combos(peer, order[:step], self.ring)):
+        peer = flip(self.here, order[step])
+        for place, slot in enumerate(combos(peer, order[:step])):
             part = buffer.at[slot, :, lanes_of(stream)]
             self.copy(part, part, number, stream, 2**step - 1 + place, peer).wait_recv()
 
@@ -513,23 +571,27 @@
     def base(self, step):
         return sum(2 ** (self.depth - 1 - s) for s in range(step))
 
+    def reduce_one(self, buffer, got, number, stream, step, place):
+        order = self.orders[stream]
+        peer = flip(self.here, order[step])
+        slot = combos(peer, order[step + 1 :])[place]
+        index = self.base(step) + place
+        made = self.copy(
+            buffer.at[slot, :, lanes_of(stream)],
+            got.at[index, :, lanes_of(stream)],
+            number, stream, index, peer,
+        )
+        made.start()
+        self.started.append(made)
+
     def reduce_start(self, buffer, got, number, stream, step):
-        order = self.orders[stream]
-        peer = flip(self.here, order[step], self.ring)
-        for place, slot in enumerate(combos(peer, order[step + 1 :], self.ring)):
-            index = self.base(step) + place
-            made = self.copy(
-                buffer.at[slot, :, lanes_of(stream)],
-                got.at[index, :, lanes_of(stream)],
-                number, stream, index, peer,
-            )
-            made.start()
-            self.started.append(made)
+        for place in range(2 ** (self.depth - 1 - step)):
+            self.reduce_one(buffer, got, number, stream, step, place)
 
     def reduce_wait(self, buffer, got, number, stream, step):
         order = self.orders[stream]
-        peer = flip(self.here, order[step], self.ring)
-        for place, slot in enumerate(combos(self.here, order[step + 1 :], self.ring)):
+        peer = flip(self.here, order[step])
+        for place, slot in enumerate(combos(self.here, order[step + 1 :])):
             index = self.base(step) + place
             part = got.at[index, :, lanes_of(stream)]
             self.copy(part, part, number, stream, index, peer).wait_recv()
@@ -790,6 +852,246 @@
     )(mixed, zero, out_weight, small, bias, ffn, table, label, valid)
 
 
+def gather_kernel(plan, table_rows, refs):
+    (
+        word_in, proj_in, boxes_in, places_in, visual_in, small_in, ffn_in, tokens_ref,
+        table_out, proj_out, boxes_out, places_out, visual_out, small_out, ffn_out, word_out,
+        table_buf, shared_buf, ffn_buf, sums, got, acc,
+        out_sem, send_sem, recv_sem, ring_send, ring_recv,
+    ) = refs
+    dp, mp = plan.dp, plan.mp
+    me = lax.axis_index("dp")
+    ring = Ring(mp, (ring_send, ring_recv))
+    here = ring.here
+    depth = bits_of(dp)
+    rows = word_in.shape[0]
+    table_buf[me, 0:rows, :] = word_in[...].astype(LOW)
+    barrier = pltpu.get_barrier_semaphore()
+    for other in range(1, dp):
+        pl.semaphore_signal(
+            barrier, 1, device_id={"dp": lax.rem(me + other, dp)}, device_id_type=MESH
+        )
+    for other in range(1, mp):
+        pl.semaphore_signal(
+            barrier, 1, device_id={"mp": lax.rem(here + other, mp)}, device_id_type=MESH
+        )
+    pl.semaphore_wait(barrier, dp + mp - 2)
+
+    half = table_rows // 2
+    pieces = (
+        (table_buf, 0, half),
+        (table_buf, half, half),
+        (shared_buf, plan.places_at, plan.shared - plan.places_at),
+        (shared_buf, 0, plan.places_at),
+        (ffn_buf, 0, ffn_buf.shape[1]),
+    )
+    orders = (list(range(1, depth)) + [0], list(range(depth - 1, -1, -1)))
+    started = []
+
+    def part_of(piece, stream, slot):
+        buffer, first, count = pieces[piece]
+        return buffer.at[slot, pl.ds(first, count), lanes_of(stream)]
+
+    def copy(piece, stream, step, place, slot):
+        part = part_of(piece, stream, slot)
+        index = 2**step - 1 + place
+        return pltpu.make_async_remote_copy(
+            src_ref=part, dst_ref=part,
+            send_sem=send_sem.at[piece, stream, index],
+            recv_sem=recv_sem.at[piece, stream, index],
+            device_id={"dp": flip(me, orders[stream][step])},
+            device_id_type=MESH,
+        )
+
+    def start(piece, step):
+        for stream in range(2):
+            for place, slot in enumerate(combos(me, orders[stream][:step])):
+                made = copy(piece, stream, step, place, slot)
+                made.start()
+                started.append(made)
+
+    def wait(piece, step):
+        for stream in range(2):
+            peer = flip(me, orders[stream][step])
+            for place, slot in enumerate(combos(peer, orders[stream][:step])):
+                copy(piece, stream, step, place, slot).wait_recv()
+
+    outs = []
+
+    def put(source, target):
+        made = pltpu.make_async_copy(source, target, out_sem.at[len(outs)])
+        made.start()
+        outs.append(made)
+
+    start(0, 0)
+    start(1, 0)
+
+    def cast(target, first, source):
+        count = source.shape[0]
+        target[me, first : first + count, : source.shape[1]] = source.astype(LOW)
+
+    for part in range(4):
+        cast(shared_buf, part * plan.proj, proj_in[part])
+    cast(shared_buf, plan.places_at, places_in[...])
+    cast(shared_buf, plan.visual_at, visual_in[...])
+    pieces_box = plan.box // 32
+    for part in range(plan.box_parts):
+        row, lane = plan.box_slot(part)
+        first = 32 * (part % pieces_box)
+        shared_buf[me, row : row + 32, lane : lane + LANES] = boxes_in[
+            part // pieces_box, first : first + 32, :
+        ].astype(LOW)
+    row, lane = plan.box_slot(plan.box_parts)
+    shared_buf[me, row : row + 32, lane : lane + LANES] = small_in[...].astype(LOW)
+    for part in range(plan.box_parts + 1, 6 * (plan.shared - plan.box_at) // 32):
+        spare_row, spare_lane = plan.box_slot(part)
+        shared_buf[me, spare_row : spare_row + 32, spare_lane : spare_lane + LANES] = jnp.zeros(
+            (32, LANES), LOW
+        )
+    ffn_rows = ffn_out.shape[2]
+    wide = ffn_in.shape[2]
+    for part in range(2):
+        at, shift = ffn_slot(part, 0, ffn_rows, wide)
+        ffn_buf[me, at : at + ffn_in.shape[1], shift : shift + wide] = ffn_in[part].astype(LOW)
+
+    for step in range(depth):
+        for piece in range(2):
+            wait(piece, step)
+            if step < depth - 1:
+                start(piece, step + 1)
+        if step == depth - 2:
+            start(2, 0)
+    put(table_buf, table_out)
+
+    vocab = rows * dp
+
+    def lookup(slot):
+        ids = tokens_ref[slot] - here * vocab
+
+        def body(index, carry):
+            local = ids - index * rows
+            local = jnp.where(local < rows, local, -1)
+            place = lax.broadcasted_iota(jnp.int32, (TEXT, table_rows), 1)
+            hot = jnp.where(place == local, 1.0, 0.0).astype(LOW)
+            found = mm(hot, table_buf[index], NN)
+
+            @pl.when(index == 0)
+            def _():
+                acc[...] = found
+
+            @pl.when(index > 0)
+            def _():
+                acc[...] = acc[...] + found
+
+            return carry
+
+        lax.fori_loop(0, dp, body, 0)
+        sums[slot] = acc[...].astype(LOW)
+
+    events = []
+    for piece, ahead in ((2, 3), (3, 4), (4, None)):
+        for step in range(depth):
+            events.append((piece, step, ahead if step == depth - 2 else None))
+
+    def advance():
+        if not events:
+            return
+        piece, step, ahead = events.pop(0)
+        wait(piece, step)
+        if step < depth - 1:
+            start(piece, step + 1)
+        if ahead is not None:
+            start(ahead, 0)
+
+    masks = sorted(range(mp), key=lambda mask: -bin(mask).count("1"))
+    for mask in masks:
+        slot = here
+        for bit in range(ring.depth):
+            if mask >> bit & 1:
+                slot = flip(slot, bit)
+        lookup(slot)
+        for stream in range(2):
+            order = ring.orders[stream]
+            if mask >> order[0] & 1:
+                place = sum((mask >> bit & 1) << t for t, bit in enumerate(order[1:]))
+                ring.reduce_one(sums, got, 0, stream, 0, place)
+        if mask != masks[-1]:
+            advance()
+    while len(events) > 2:
+        advance()
+    for step in range(ring.depth):
+        for stream in range(2):
+            ring.reduce_wait(sums, got, 0, stream, step)
+            if step < ring.depth - 1:
+                ring.reduce_start(sums, got, 0, stream, step + 1)
+        advance()
+    word_out[...] = sums[here]
+    while events:
+        advance()
+    for part in range(4):
+        put(shared_buf.at[:, pl.ds(part * plan.proj, plan.proj)], proj_out.at[part])
+    put(shared_buf.at[:, pl.ds(plan.places_at, plan.places)], places_out)
+    put(shared_buf.at[:, pl.ds(plan.visual_at, plan.visual)], visual_out)
+    for part in range(plan.box_parts):
+        at, shift = plan.box_slot(part)
+        put(
+            shared_buf.at[:, pl.ds(at, 32), pl.ds(shift, LANES)],
+            boxes_out.at[part // pieces_box, :, pl.ds(32 * (part % pieces_box), 32)],
+        )
+    put(shared_buf.at[:, pl.ds(row, 32), pl.ds(lane, LANES)], small_out)
+    for part in range(2):
+        at, shift = ffn_slot(part, 0, ffn_rows, wide)
+        put(ffn_buf.at[:, pl.ds(at, ffn_rows), pl.ds(shift, wide)], ffn_out.at[part])
+    for made in started:
+        made.wait_send()
+    ring.finish()
+    for made in outs:
+        made.wait()
+
+
+def gather_weights(plan, word, proj, boxes, places, visual, small, ffn, tokens):
+    dp, mp = plan.dp, plan.mp
+    table_rows, ffn_rows, wide = pad_up(word.shape[0], 32), pad_up(ffn.shape[1], 16), ffn.shape[2]
+    ffn_all = 2 * ffn_rows * wide // D
+    depth = bits_of(dp)
+    anywhere = pl.BlockSpec(memory_space=pl.ANY)
+    vmem = pl.BlockSpec(memory_space=pltpu.VMEM)
+    dma = pltpu.SemaphoreType.DMA
+    shape = jax.ShapeDtypeStruct
+
+    def body(*refs):
+        gather_kernel(plan, table_rows, refs)
+
+    return pl.pallas_call(
+        body,
+        out_shape=(
+            shape((dp, table_rows, D), LOW), shape((4, dp, plan.proj, D), LOW),
+            shape((4, dp, plan.box, LANES), LOW), shape((dp, plan.places, D), LOW),
+            shape((dp, plan.visual, D), LOW), shape((dp, 32, LANES), LOW),
+            shape((2, dp, ffn_rows, wide), LOW), shape((TEXT, D), LOW),
+        ),
+        in_specs=[vmem] * 8,
+        out_specs=(anywhere,) * 7 + (vmem,),
+        scratch_shapes=[
+            pltpu.VMEM((dp, table_rows, D), LOW),
+            pltpu.VMEM((dp, plan.shared, D), LOW),
+            pltpu.VMEM((dp, ffn_all, D), LOW),
+            pltpu.VMEM((mp, TEXT, D), LOW),
+            pltpu.VMEM((mp - 1, TEXT, D), LOW),
+            pltpu.VMEM((TEXT, D), WIDE),
+            dma((plan.box_parts + 10,)),
+            dma((5, 2, dp - 1)),
+            dma((5, 2, dp - 1)),
+            dma((1, 2, mp - 1)),
+            dma((1, 2, mp - 1)),
+        ],
+        compiler_params=pltpu.CompilerParams(
+            collective_id=1, has_side_effects=True, vmem_limit_bytes=56 * 2**20
+        ),
+        name="gather_weights",
+    )(word, proj, boxes, places, visual, small, ffn, tokens)
+
+
 ROWS = 576
 KINDS = ((6, 3), (0, 4), (3, 4))
 
@@ -1127,28 +1429,28 @@
     dp, mp = lax.axis_size("dp"), lax.axis_size("mp")
     plan = Plan(dp, mp)
 
-    def gathered(part, axis):
-        return lax.all_gather(part.astype(LOW), "dp", axis=axis, tiled=True)
-
-    work_table = gathered(word_table, 0)
-    work_small = gathered(small_params, 1)
-    work_boxes = gathered(box_tables, 1)
-    work_places = gathered(position_table, 0)
-    work_visual = gathered(visual_proj, 0)
-    work_proj = gathered(projections, 1)
-    work_ffn = gathered(feedforward, 1)
+    cut = small_params.shape[1]
+    (
+        table_parts, proj_parts, box_parts, place_parts, visual_parts, small_parts, ffn_parts, word,
+    ) = gather_weights(
+        plan, word_table, projections, box_tables, position_table, visual_proj,
+        jnp.pad(small_params, ((0, 32 - VROWS), (0, LANES - cut))), feedforward, tokens[..., None],
+    )
+
+    def joined(parts, rows):
+        parts = parts[..., :rows, :]
+        return parts.reshape(parts.shape[:-3] + (dp * rows, parts.shape[-1]))
+
+    work_table = joined(table_parts, word_table.shape[0])
+    work_proj = joined(proj_parts, D // dp)
+    work_boxes = joined(box_parts, NBOX // dp)
+    work_places = joined(place_parts, TEXT // dp)
+    work_visual = joined(visual_parts, VCH // dp)
+    work_ffn = joined(ffn_parts, D // dp)
+    work_small = jnp.transpose(small_parts[:, :VROWS, :cut], (1, 0, 2)).reshape(VROWS, D)
     model_index = lax.axis_index("mp")
     vocab_shard, hidden_shard = work_table.shape[0], work_ffn.shape[2]
     small_float = work_small.astype(WIDE)
-
-    local_ids = tokens - model_index * vocab_shard
-    inside = (local_ids >= 0) & (local_ids < vocab_shard)
-    safe_index = jnp.clip(local_ids, 0, vocab_shard - 1)
-    partial_word = jnp.where(
-        inside[..., None], jnp.take(work_table, safe_index, axis=0), jnp.zeros((), LOW)
-    )
-    word = lax.psum_scatter(partial_word, "mp", scatter_dimension=0, tiled=True)[0]
-
     info = token_info(text_box[0], segments[0], alive_text[0])
     columns = info.T
     visual_rows = jnp.pad(features, ((0, ROWS - TEXT - features.shape[0]), (0, 0)))
@@ -1180,23 +1482,18 @@
     grad_small = jnp.concatenate(
         [front_rows[:4], head_rows[4:10], bias_full, edge_rows_back(grad_edges).reshape(3, D)], 0
     )
-    group_word = lax.all_gather(grad_word[None], "mp", axis=0, tiled=True)
-    grad_table = grad_table.astype(WIDE) + jnp.zeros((vocab_shard, D), WIDE).at[safe_index].add(
-        jnp.where(inside[..., None], group_word.astype(WIDE), 0.0)
-    )
-
     def split_rows(part):
         rows = part.shape[-2] // dp
         part = part.astype(LOW).reshape(part.shape[:-2] + (dp, rows, part.shape[-1]))
         extra = [(0, 0)] * (part.ndim - 2) + [(0, pad_up(rows, 16) - rows), (0, 0)]
         return jnp.pad(part, extra) if extra[-2][1] else part
 
-    cut = small_params.shape[1]
     small_split = jnp.transpose(grad_small.reshape(VROWS, dp, cut), (1, 0, 2)).astype(LOW)
     small_split = jnp.pad(small_split, ((0, 0), (0, 32 - VROWS), (0, LANES - cut)))
     table_split, ffn_split = split_rows(grad_table), split_rows(grad_ffn)
     shared_sum, split_sum, totals = reduce_gradients(
         plan,
+        word_table.shape[0],
         table_split,
         split_rows(grad_in_weight),
         split_rows(grad_out_weight),
@@ -1206,6 +1503,8 @@
         grad_boxes.reshape(4, dp, NBOX // dp, LANES),
         small_split,
         own_tile,
+        grad_word,
+        tokens.reshape(1, -1),
     )
     loss_sum, loss_count = (totals[1, 0, 0], totals[1, 1, 0])
     grad_norm = jnp.sqrt(jnp.sum(totals[0])) / loss_count

time: 590 us -> 412 us (0.70)
  waiting for transfers between devices: 177 us -> 0 us
  Pallas kernels: 271 us -> 375 us
  other arithmetic: 53.2 us -> 2.58 us
  blocking collectives: 30.7 us -> 0 us
  between operations: 17.2 us -> 3.65 us
  local copies, waits for them, and re-layouts: 39.7 us -> 29.8 us
    all_gather x5 -> x0, waiting for transfers between devices: 114 us -> none  [the longest x4 63.5 us: gathered(): return lax.all_gather(part.astype(LOW), 'dp', axis=axis, tiled=True)]
    pallas_call x0 -> x1, Pallas kernels: none -> 110 us  [gather_weights(): pl.pallas_call(body, out_shape=(shape((dp, table_rows, D), LOW), shape((4...]
    reduce_scatter x1 -> x0, waiting for transfers between devices: 62.4 us -> none  [on_device(): lax.psum_scatter(partial_word, 'mp', scatter_dimension=0, tiled=True)[0]]
    all_gather x3 -> x0, blocking collectives: 30.7 us -> none  [gathered(): return lax.all_gather(part.astype(LOW), 'dp', axis=axis, tiled=True)]
    scatter-add x1 -> x0, other arithmetic: 23.1 us -> none  [on_device(): jnp.zeros((vocab_shard, D), WIDE).at[safe_index]]
    convert_element_type x9 -> x0, other arithmetic: 20.3 us -> none  [the longest x1 8.15 us: on_device(): grad_table.astype(WIDE)]
    gather x1 -> x0, local copies, waits for them, and re-layouts: 13.6 us -> none  [on_device(): jnp.take(work_table, safe_index, axis=0)]
    select_n x2 -> x0, other arithmetic: 7.92 us -> none  [the longest x1 4.4 us: on_device(): jnp.where(inside[..., None], group_word.astype(WIDE), 0.0)]
  transfers between devices with their start and end apart: 6 -> 0, of which waited for: 5 -> 0; matrix products, arithmetic and copies ran while one was open for 7% -> 0% of each run, Pallas kernels for 3% -> 0%
where the time goes in v4:
time: 412 us; the launch traced here: 411 us
  Pallas kernels  375 us (91%)
  local copies, waits for them, and re-layouts  29.8 us (7%)
    pallas_call x1, Pallas kernels, reduce_gradients(): pl.pallas_call(body, out_shape=(jax.ShapeDtypeStruct((plan.shared, D), WI...  119 us
    pallas_call x1, Pallas kernels, gather_weights(): pl.pallas_call(body, out_shape=(shape((dp, table_rows, D), LOW), shape((4...  110 us
    pallas_call x1, Pallas kernels, head_step(): pl.pallas_call(body, out_shape=(jax.ShapeDtypeStruct((slots, D), WIDE), j...  89.1 us
    pallas_call x1, Pallas kernels, back_step(): pl.pallas_call(back_kernel, out_shape=(shape((TEXT, D), LOW), shape((TEXT...  26.3 us
    pallas_call x1, Pallas kernels, front_step(): pl.pallas_call(front_kernel, out_shape=(shape((slots, D), LOW), shape((sl...  20 us
    pallas_call x1, Pallas kernels, adam_update(): pl.pallas_call(body, out_shape=tuple((jax.ShapeDtypeStruct(part.shape, WI...  11.8 us
    unnamed x54, local copies, waits for them, and re-layouts  9.05 us

profile of v4, /device:TPU:0, one launch (start us, length us, event | category | flops | bytes accessed | tf_op | source)
XLA Modules:
  0.0 411.5 jit_solution(3899908158841318153)
XLA Ops:
  0.7 2.0 copy.88.refs_7_
  2.7 1.3 pad.22.refs_5_
  4.0 109.7 %gather_weights.1 = (bf16[8,480,768]{2,1,0:T(8,128)(2,1)}, bf16[4,8,96,768]{3,2,1,0:T(8,128)(2,1)}, bf16[4,8,128,128]{3,2,1,0:T(8,128)(2,1)}, bf16[8,64,768]{2,1...) custom-call(f32[480,768]{1,0:T(8,128)} %refs_18_.1, ...), custom_call_target="tpu_custom_call" | custom-call | tf_op jit(solution)/shard_map/gather_weights/pallas_call | solution.py:1065
  113.7 0.8 slice_bitcast_fusion
  114.8 0.1 copy.91
  114.9 0.1 pad_maximum_fusion
  115.0 0.6 pad.24.edges_ref
  116.0 0.6 fusion.4
  116.6 0.9 copy.92.columns_ref
  117.5 0.7 convert_element_type.27.small_ref.refs_3_
  118.2 4.0 slice.90
  122.2 0.6 pad.23.features_ref
  122.9 20.0 %front_step.1 = (bf16[80,768]{1,0:T(8,128)(2,1)}, f32[80,768]{1,0:T(8,128)}, bf16[80,768]{1,0:T(8,128)(2,1)}, bf16[576,768]{1,0:T(8,128)(2,1)}, f32[576,768]{1,0...) custom-call(s32[80]{0:T(128)} %pos_ref.3, ...), custom_call_target="tpu_custom_call" | custom-call | tf_op jit(solution)/shard_map/front_step/pallas_call | solution.py:1264
  142.9 0.1 reshape.333
  143.0 0.6 constant_dynamic-slice_fusion.refs_4_
  143.6 2.4 slice.92
  146.0 0.6 broadcast_in_dim.26.refs_7_
  146.5 0.6 broadcast_in_dim.27.refs_8_
  147.1 89.1 %head_step.1 = (f32[80,768]{1,0:T(8,128)}, bf16[80,768]{1,0:T(8,128)(2,1)}, bf16[768,768]{1,0:T(8,128)(2,1)}, bf16[2,768,768]{2,1,0:T(8,128)(2,1)}, bf16[3840,76...) custom-call(bf16[80,768]{1,0:T(8,128)(2,1)} %get-tuple-element.87.refs_0_, ...), custom_call_target="tpu_custom_call" | custom-call | tf_op jit(solution)/shard_map/head_step/pallas_call | solution.py:820
  236.3 26.3 %back_step.1 = (bf16[512,768]{1,0:T(8,128)(2,1)}, bf16[512,768]{1,0:T(8,128)(2,1)}, bf16[4,1024,128]{2,1,0:T(8,128)(2,1)}, bf16[256,768]{1,0:T(8,128)(2,1)}, bf1...) custom-call(s32[80]{0:T(128)} %pos_ref.3, f32[80,768]{1,0:T(8,128)} %get-tuple-element.92.grad_zero_ref, ...), custom_call_target="tpu_custom_call" | custom-call | tf_op jit(solution)/shard_map/back_step/pallas_call | solution.py:1396
  262.5 0.7 reshape.343
  263.3 0.1 slice_reduce_fusion.1
  263.4 0.1 copy.95
  263.5 0.1 copy.96
  263.8 0.1 maximum_bitcast_fusion.1
  263.8 0.1 copy.97
  264.0 0.1 concatenate.42
  264.1 0.7 slice.140
  264.8 0.1 concatenate.38
  264.9 0.8 slice.139
  265.7 0.1 concatenate.39
  265.9 0.2 dynamic_update_slice.3
  266.1 0.1 concatenate.40
  266.3 0.6 pad.26.refs_7_
  266.9 0.6 copy.104
  267.6 118.6 %reduce_gradients.1 = (f32[640,768]{1,0:T(8,128)}, f32[672,768]{1,0:T(8,128)}, f32[2,8,128]{2,1,0:T(8,128)}) custom-call(bf16[8,480,768]{2,1,0:T(8,128)(2,1)} %bitcast.64, bf16[3,8,96,768]{3,2,1,0:T(8,128)(2,1)} %bitcast.66, bf16[8,96,768]{2,1,0:T(8,128)(2,1)} %bitcast.69, bf16[2,8,96,768]{3,2,1,0:T(8,128)(2,1)} %bitcast.68, bf16[8,64,768]{2,1,0:T(8,128)(2,1)} %bitcast.72, ...), custom_call_target="tpu_custom_call" | custom-call | tf_op jit(solution)/shard_map/reduce_gradients/pallas_call | solution.py:410
  386.2 1.3 fusion.5
  387.5 1.3 slice_reduce_fusion.2
  390.2 1.1 copy-done.5
  391.3 1.1 copy-done.6
  392.3 0.9 copy-done.8
  393.3 0.9 copy-done.9
  394.2 0.9 copy-done.10
  395.2 0.9 copy-done.11
  396.1 0.9 copy-done.12
  397.0 0.9 copy-done.13
  397.9 0.7 copy-done.15
  398.6 11.8 %adam_update.1 = (f32[4,96,768]{2,1,0:T(8,128)}, f32[4,96,768]{2,1,0:T(8,128)}, f32[4,96,768]{2,1,0:T(8,128)}, f32[4,128,128]{2,1,0:T(8,128)}, f32[4,128,128]{2,...) custom-call(f32[640,768]{1,0:T(8,128)} %get-tuple-element.114.refs_0, ...), custom_call_target="tpu_custom_call" | custom-call | tf_op jit(solution)/shard_map/adam_update/pallas_call | solution.py:502
  (79 shorter events, 0.8 us)
Async XLA Ops:
  4.0 111.7 %copy-start.20 = (s32[1,512,4]{1,2,0:T(4,128)S(1)}, s32[1,512,4]{1,2,0:T(4,128)}, u32[]{:S(2)}) copy-start(s32[1,512,4]{1,2,0:T(4,128)} %param.30) | copy-start | bytes 24580
  4.0 111.8 %copy-start.24 = (s32[1,512]{1,0:T(1,128)S(1)}, s32[1,512]{1,0:T(1,128)}, u32[]{:S(2)}) copy-start(s32[1,512]{1,0:T(1,128)} %param.31) | copy-start | bytes 6148
  4.0 111.8 %copy-start.25 = (s32[1,512]{1,0:T(1,128)S(1)}, s32[1,512]{1,0:T(1,128)}, u32[]{:S(2)}) copy-start(s32[1,512]{1,0:T(1,128)} %param.32) | copy-start | bytes 6148
  118.2 4.0 copy-start.19
  142.9 3.1 copy-start.22
  142.9 3.6 copy-start.23
  236.2 29.6 %copy-start.21 = (f32[1,768]{1,0:T(1,128)S(1)}, f32[1,768]{1,0:T(1,128)}, u32[]{:S(2)}) copy-start(f32[1,768]{1,0:T(1,128)} %get-tuple-element.110) | copy-start | bytes 9220
  236.2 30.7 %copy-start.18 = (s32[4,512]{1,0:T(4,128)S(1)}, s32[4,512]{1,0:T(4,128)}, u32[]{:S(2)}) copy-start(s32[4,512]{1,0:T(4,128)} %param.29) | copy-start | bytes 24580
  267.5 122.6 %copy-start = (f32[4,96,768]{2,1,0:T(8,128)S(1)}, f32[4,96,768]{2,1,0:T(8,128)}, u32[]{:S(2)}) copy-start(f32[4,96,768]{2,1,0:T(8,128)} %refs_3_.3) | copy-start | bytes 3538948
  267.5 122.6 %copy-start.1 = (f32[2,96,768]{2,1,0:T(8,128)S(1)}, f32[2,96,768]{2,1,0:T(8,128)}, u32[]{:S(2)}) copy-start(f32[2,96,768]{2,1,0:T(8,128)} %refs_21_.1) | copy-start | bytes 1769476
  267.5 122.6 %copy-start.2 = (f32[4,96,768]{2,1,0:T(8,128)S(1)}, f32[4,96,768]{2,1,0:T(8,128)}, u32[]{:S(2)}) copy-start(f32[4,96,768]{2,1,0:T(8,128)} %refs_4_.3) | copy-start | bytes 3538948
  267.5 122.6 %copy-start.3 = (f32[4,128,128]{2,1,0:T(8,128)S(1)}, f32[4,128,128]{2,1,0:T(8,128)}, u32[]{:S(2)}) copy-start(f32[4,128,128]{2,1,0:T(8,128)} %refs_6_.3) | copy-start | bytes 786436
  267.5 122.6 %copy-start.4 = (f32[64,768]{1,0:T(8,128)S(1)}, f32[64,768]{1,0:T(8,128)}, u32[]{:S(2)}) copy-start(f32[64,768]{1,0:T(8,128)} %refs_9_.1) | copy-start | bytes 589828
  267.6 122.6 %copy-start.7 = (f32[32,768]{1,0:T(8,128)S(1)}, f32[32,768]{1,0:T(8,128)}, u32[]{:S(2)}) copy-start(f32[32,768]{1,0:T(8,128)} %refs_12_.1) | copy-start | bytes 294916
  267.6 122.6 %copy-start.14 = (f32[17,96]{1,0:T(8,128)S(1)}, f32[17,96]{1,0:T(8,128)}, u32[]{:S(2)}) copy-start(f32[17,96]{1,0:T(8,128)} %refs_15_.1) | copy-start | bytes 19588
  267.6 122.6 %copy-start.16 = (f32[17,96]{1,0:T(8,128)S(1)}, f32[17,96]{1,0:T(8,128)}, u32[]{:S(2)}) copy-start(f32[17,96]{1,0:T(8,128)} %refs_16_.1) | copy-start | bytes 19588
  267.6 122.6 %copy-start.17 = (f32[17,96]{1,0:T(8,128)S(1)}, f32[17,96]{1,0:T(8,128)}, u32[]{:S(2)}) copy-start(f32[17,96]{1,0:T(8,128)} %refs_17_.1) | copy-start | bytes 19588
  390.2 1.1 copy-start.5
  391.3 1.1 copy-start.6
  392.3 0.9 copy-start.8
  393.3 0.9 copy-start.9
  394.2 0.9 copy-start.10
  395.2 0.9 copy-start.11
  396.1 0.9 copy-start.12
  397.0 0.9 copy-start.13
  397.9 0.7 copy-start.15
